TPU v7x, 32 devices: a whole 2x2x4 slice. The times are simulated.
32 devices in a mesh: dp: 1, seq: 32 (over z, y, x, core).
Axes of the slice: x: 2, y: 2, z: 4, core: 2. Of those that a mesh axis runs over, the one named last changes fastest.
Arguments:
- queries: bfloat16 [1, 8192, 1024], P('dp', 'seq'), may hold values from -8 to 8
- keys: bfloat16 [1, 8192, 1024], P('dp', 'seq'), may hold values from -8 to 8
- values: bfloat16 [1, 8192, 1024], P('dp', 'seq'), may hold values from -12 to 12
- out_weight: bfloat16 [1024, 2048], P('seq', 'dp'), may hold values from -0.1875 to 0.1875
- out_grad: bfloat16 [1, 8192, 2048], P('dp', 'seq'), may hold values from -6 to 6
Outputs:
- attended: bfloat16 [1, 8192, 2048], P('dp', 'seq')
- grad_queries: bfloat16 [1, 8192, 1024], P('dp', 'seq')
- grad_keys: bfloat16 [1, 8192, 1024], P('dp', 'seq')
- grad_values: bfloat16 [1, 8192, 1024], P('dp', 'seq')
- grad_out_weight: float32 [1024, 2048], P('seq', 'dp')
All inputs are finite; a program needn't handle non-finite values.
Results may differ from a plain program's by a relative error of at most 0.029.
Values may be sent and summed in bfloat16 or wider, within the bound.
No kernel may reach another device: no remote copies, remote signals or barrier semaphores. Data moves between devices by JAX's collectives and lax.ppermute only.
A program may use at most 128 MiB of HBM per device.

v0:
```python
import math

import jax
import jax.numpy as jnp
from jax import lax
from jax.sharding import PartitionSpec as P

HEADS = 8
HS = 128
NR = 128


HALF_ROOT = 0.7071067811865476


def partner_2(value, axis, distance):
    mask = 2**distance
    pairs = [(source, source ^ mask) for source in range(lax.axis_size(axis))]
    return lax.ppermute(value, axis, pairs)


def pool_pairs(row_data):
    shaped = row_data.astype(jnp.float32).reshape(row_data.shape[0] // 2, 2, row_data.shape[1])
    return ((shaped[:, 0] + shaped[:, 1]) * HALF_ROOT).astype(jnp.bfloat16)


def unpool_pairs(grad_data):
    spread = grad_data * HALF_ROOT
    return jnp.broadcast_to(spread[:, None, :], (spread.shape[0], 2, spread.shape[1])).reshape(
        2 * spread.shape[0], spread.shape[1]
    )


def sibling_groups(row_data, blocks_here, height):
    chans = row_data.shape[1]
    groups = row_data.reshape(blocks_here >> height + 1, 2, NR, chans)[:, ::-1].reshape(
        blocks_here >> height, NR, chans
    )
    widened = groups[:, None]
    return widened.reshape(blocks_here, NR, chans)


def unsibling(grad_data, blocks_here, height):
    chans = grad_data.shape[2]
    summed = grad_data.reshape(blocks_here >> height, 2**height, NR, chans).sum(axis=1)
    swapped = summed.reshape(blocks_here >> height + 1, 2, NR, chans)[:, ::-1]
    return swapped.reshape((blocks_here >> height) * NR, chans)


def order_pair(own_panel, partner, upper_bit):
    first_half = jnp.where(upper_bit == 0, own_panel, partner)
    second_half = jnp.where(upper_bit == 0, partner, own_panel)
    return jnp.concatenate([first_half, second_half], axis=0)


def body(queries, keys, values, out_weight, out_grad):
    inner_width = queries.shape[2]
    length = queries.shape[1]
    chans = 2 * inner_width
    blocks_here = length // NR
    local_levels = blocks_here.bit_length() - 1
    seq_count = lax.axis_size("seq")
    seq_levels = seq_count.bit_length() - 1
    seq_rank = lax.axis_index("seq")
    score_scale = 1.0 / math.sqrt(HS)
    query_rows = queries[0]
    grad_rows = out_grad[0]
    pair_rows = jnp.concatenate([keys[0], values[0]], axis=1)
    wide_weight = lax.all_gather(out_weight, "dp", axis=1, tiled=True)
    full_weight = lax.all_gather(wide_weight, "seq", axis=0, tiled=True)
    d_attn = lax.dot_general(
        grad_rows, full_weight, (((1,), (1,)), ((), ())), preferred_element_type=jnp.float32
    ).astype(jnp.bfloat16)
    coarse = [pair_rows]
    coarse.append(pool_pairs(coarse[-1]))
    near_panels = [pair_rows.reshape(blocks_here, NR, chans)]
    height = 0
    near_panels.append(sibling_groups(coarse[height], blocks_here, height))
    near_rows = jnp.concatenate(near_panels, axis=1)
    own_panel = coarse[local_levels]
    far_panels = []
    upper_bits = []
    for height in range(seq_levels):
        partner = partner_2(own_panel, "seq", height)
        far_panels.append(partner)
        upper_bit = seq_rank // 2**height % 2
        upper_bits.append(upper_bit)
        if height + 1 < seq_levels:
            own_panel = pool_pairs(order_pair(own_panel, partner, upper_bit))
    far_rows = jnp.concatenate(far_panels, axis=0)
    near_count = near_rows.shape[1]
    far_count = far_rows.shape[0]
    near_keys = near_rows[:, :, :inner_width].reshape(blocks_here, near_count, HEADS, HS)
    near_values = near_rows[:, :, inner_width:].reshape(blocks_here, near_count, HEADS, HS)
    far_keys = far_rows[:, :inner_width].reshape(far_count, HEADS, HS)
    far_values = far_rows[:, inner_width:].reshape(far_count, HEADS, HS)
    query_heads = query_rows.reshape(blocks_here, NR, HEADS, HS)
    near_scores = (
        jnp.einsum("bqhd,bkhd->bhqk", query_heads, near_keys, preferred_element_type=jnp.float32)
        * score_scale
    )
    far_scores = (
        jnp.einsum("bqhd,khd->bhqk", query_heads, far_keys, preferred_element_type=jnp.float32)
        * score_scale
    )
    top_score = jnp.maximum(
        jnp.max(near_scores, axis=-1, keepdims=True), jnp.max(far_scores, axis=-1, keepdims=True)
    )
    near_exp = jnp.exp(near_scores - top_score)
    far_exp = jnp.exp(far_scores - top_score)
    total = jnp.sum(near_exp, axis=-1, keepdims=True) + jnp.sum(far_exp, axis=-1, keepdims=True)
    near_probs = near_exp / total
    far_probs = far_exp / total
    near_low = near_probs.astype(jnp.bfloat16)
    far_low = far_probs.astype(jnp.bfloat16)
    attn_heads = jnp.einsum(
        "bhqk,bkhd->bqhd", near_low, near_values, preferred_element_type=jnp.float32
    )
    attn_heads = attn_heads + jnp.einsum(
        "bhqk,khd->bqhd", far_low, far_values, preferred_element_type=jnp.float32
    )
    attn_rows = attn_heads.reshape(length, inner_width).astype(jnp.bfloat16)
    attended = jnp.dot(attn_rows, full_weight, preferred_element_type=jnp.float32).astype(
        jnp.bfloat16
    )
    grad_heads = d_attn.reshape(blocks_here, NR, HEADS, HS)
    near_dprob = jnp.einsum(
        "bqhd,bkhd->bhqk", grad_heads, near_values, preferred_element_type=jnp.float32
    )
    far_dprob = jnp.einsum(
        "bqhd,khd->bhqk", grad_heads, far_values, preferred_element_type=jnp.float32
    )
    center = jnp.sum(near_probs * near_dprob, axis=-1, keepdims=True) + jnp.sum(
        far_probs * far_dprob, axis=-1, keepdims=True
    )
    near_dscore = (near_probs * (near_dprob - center) * score_scale).astype(jnp.bfloat16)
    far_dscore = (far_probs * (far_dprob - center) * score_scale).astype(jnp.bfloat16)
    grad_query = jnp.einsum(
        "bhqk,bkhd->bqhd", near_dscore, near_keys, preferred_element_type=jnp.float32
    )
    grad_query = grad_query + jnp.einsum(
        "bhqk,khd->bqhd", far_dscore, far_keys, preferred_element_type=jnp.float32
    )
    near_key_grad = jnp.einsum(
        "bhqk,bqhd->bkhd", near_dscore, query_heads, preferred_element_type=jnp.float32
    )
    near_value_grad = jnp.einsum(
        "bhqk,bqhd->bkhd", near_low, grad_heads, preferred_element_type=jnp.float32
    )
    near_grad = jnp.concatenate(
        [
            near_key_grad.reshape(blocks_here, near_count, inner_width),
            near_value_grad.reshape(blocks_here, near_count, inner_width),
        ],
        axis=-1,
    )
    far_key_grad = jnp.einsum(
        "bhqk,bqhd->khd", far_dscore, query_heads, preferred_element_type=jnp.float32
    )
    far_value_grad = jnp.einsum(
        "bhqk,bqhd->khd", far_low, grad_heads, preferred_element_type=jnp.float32
    )
    far_grad = jnp.concatenate(
        [
            far_key_grad.reshape(far_count, inner_width),
            far_value_grad.reshape(far_count, inner_width),
        ],
        axis=-1,
    )
    coarse_grads = [unsibling(near_grad[:, NR : 2 * NR], blocks_here, 0)]
    coarse_grads[0] = coarse_grads[0] + near_grad[:, :NR].reshape(length, chans)
    far_parts = [far_grad[index * NR : (index + 1) * NR] for index in range(len(far_panels))]
    upper_grad = None
    for height in reversed(range(seq_levels)):
        partner_grad = far_parts[height]
        own_grad = jnp.zeros((NR, chans), jnp.float32)
        if upper_grad is not None:
            spread = unpool_pairs(upper_grad)
            lead_half = spread[:NR]
            tail_half = spread[NR:]
            own_grad = jnp.where(upper_bits[height] == 0, lead_half, tail_half)
            partner_grad = partner_grad + jnp.where(upper_bits[height] == 0, tail_half, lead_half)
        upper_grad = own_grad + partner_2(partner_grad, "seq", height)
    coarse_grads.append(upper_grad)
    for height in reversed(range(local_levels)):
        coarse_grads[height] = coarse_grads[height] + unpool_pairs(coarse_grads[height + 1])
    pair_grad = coarse_grads[0]
    token_total = length * seq_count * queries.shape[0] * lax.axis_size("dp")
    row_sums = lax.psum_scatter(
        lax.dot_general(
            attn_rows, grad_rows, (((0,), (0,)), ((), ())), preferred_element_type=jnp.float32
        ).astype(jnp.bfloat16),
        "seq",
        scatter_dimension=0,
        tiled=True,
    )
    weight_grad = lax.psum_scatter(row_sums, "dp", scatter_dimension=1, tiled=True).astype(
        jnp.float32
    )
    weight_grad = weight_grad * (1.0 / math.sqrt(token_total))
    grad_queries = grad_query.reshape(length, inner_width).astype(jnp.bfloat16)
    grad_keys = pair_grad[:, :inner_width].astype(jnp.bfloat16)
    grad_values = pair_grad[:, inner_width:].astype(jnp.bfloat16)
    return (attended[None], grad_queries[None], grad_keys[None], grad_values[None], weight_grad)


def solution(mesh):
    placed = (
        P("dp", "seq", None),
        P("dp", "seq", None),
        P("dp", "seq", None),
        P("seq", "dp"),
        P("dp", "seq", None),
    )
    return jax.shard_map(
        body,
        mesh=mesh,
        in_specs=placed,
        out_specs=(
            P("dp", "seq", None),
            P("dp", "seq", None),
            P("dp", "seq", None),
            P("dp", "seq", None),
            P("seq", "dp"),
        ),
        check_vma=False,
    )
```

profile of v0, /device:TPU:0, one launch (start us, length us, event | category | flops | bytes accessed | tf_op | source)
XLA Modules:
  0.0 389.5 jit_solution(10199949808572120726)
XLA Ops:
  18.7 4.4 %fusion.53 = bf16[128,1,2048]{2,1,0:T(2,128)(2,1)S(1)} fusion(f32[128,2,2048]{2,1,0:T(2,128)} %reshape.181), kind=kLoop, calls=%fused_computation.84 | loop fusion | flops 786432 | bytes 2621440 | tf_op jit(solution)/shard_map/convert_element_type | solution.py:24
  26.7 12.8 %collective-permute-done.1 = bf16[128,2048]{1,0:T(8,128)(2,1)S(1)} collective-permute-done((bf16[128,2048]{1,0:T(8,128)(2,1)S(1)}, bf16[128,2048]{1,0:T(8,128)(2,1)S(1)}, u32[]{:S(2)}, u32[]{:S(2)}) %collective-permute-start.1) | collective-permute-done | bytes 524320 | tf_op jit(solution)/shard_map/ppermute | solution.py:19
  43.3 4.4 %fusion.54 = bf16[128,1,2048]{2,1,0:T(2,128)(2,1)S(1)} fusion(f32[128,2,2048]{2,1,0:T(2,128)} %reshape.182), kind=kLoop, calls=%fused_computation.85 | loop fusion | flops 786432 | bytes 2621440 | tf_op jit(solution)/shard_map/convert_element_type | solution.py:24
  56.0 7.5 %collective-permute-done.2 = bf16[128,2048]{1,0:T(8,128)(2,1)} collective-permute-done((bf16[128,2048]{1,0:T(8,128)(2,1)}, bf16[128,2048]{1,0:T(8,128)(2,1)}, u32[]{:S(2)}, u32[]{:S(2)}) %collective-permute-start.2) | collective-permute-done | bytes 524320 | tf_op jit(solution)/shard_map/ppermute | solution.py:19
  68.3 4.4 %fusion.55 = bf16[128,1,2048]{2,1,0:T(2,128)(2,1)S(1)} fusion(f32[128,2,2048]{2,1,0:T(2,128)} %reshape.183), kind=kLoop, calls=%fused_computation.86 | loop fusion | flops 786432 | bytes 2621440 | tf_op jit(solution)/shard_map/convert_element_type | solution.py:24
  74.9 20.5 %collective-permute-done.3 = bf16[128,2048]{1,0:T(8,128)(2,1)S(1)} collective-permute-done((bf16[128,2048]{1,0:T(8,128)(2,1)S(1)}, bf16[128,2048]{1,0:T(8,128)(2,1)S(1)}, u32[]{:S(2)}, u32[]{:S(2)}) %collective-permute-start.3) | collective-permute-done | bytes 524320 | tf_op jit(solution)/shard_map/ppermute | solution.py:19
  98.2 3.5 reshape.184
  101.7 4.3 %fusion.56 = bf16[128,1,2048]{2,1,0:T(2,128)(2,1)S(1)} fusion(f32[128,2,2048]{2,1,0:T(2,128)} %reshape.184), kind=kLoop, calls=%fused_computation.87 | loop fusion | flops 786432 | bytes 2621440 | tf_op jit(solution)/shard_map/convert_element_type | solution.py:24
  116.8 15.7 %collective-permute-done.4 = bf16[128,2048]{1,0:T(8,128)(2,1)} collective-permute-done((bf16[128,2048]{1,0:T(8,128)(2,1)}, bf16[128,2048]{1,0:T(8,128)(2,1)}, u32[]{:S(2)}, u32[]{:S(2)}) %collective-permute-start.4) | collective-permute-done | bytes 524320 | tf_op jit(solution)/shard_map/ppermute | solution.py:19
  145.5 3.5 fusion.36
  150.6 4.2 %multiply_reduce_fusion = (f32[2,8,128]{2,1,0:T(8,128)S(1)}, f32[2,8,128,256]{2,3,1,0:T(8,128)}) fusion(f32[2,8,128]{2,1,0:T(8,128)S(1)} %copy_add_fusion.1, f32[2,8,128]{2,1,0:T(8,128)S(1)} %copy_maximum_fusion, f32[2,8,256,128]{3,2,1,0:T(8,128)} %copy-done.2, bf16[2,128,8,128]{1,3,2,0:T(8,128)(2,1)} %copy.338, bf16[2,256,8,128]{1,3,2,0:T(8,128)(2,1)} %bitcast.200), kind=kOutput, calls=%fused_computation.38 | convolution fusion | flops 136837120 | bytes 5791744 | tf_op jit(solution)/shard_map/bqhd,bkhd->bhqk/dot_general | solution.py:127
  156.6 3.0 fusion.3
  162.0 3.3 copy.345
  165.4 4.2 %fusion.71 = f32[8,128,640,1]{2,1,3,0:T(8,128)} fusion(bf16[2,128,8,128]{1,3,0,2:T(8,128)(2,1)S(1)} %copy.343, bf16[2,8,128,640]{2,3,0,1:T(8,128)(2,1)} %get-tuple-element.6), kind=kOutput, calls=%fused_computation.133 | convolution fusion | flops 335544320 | bytes 5767168 | tf_op jit(solution)/shard_map/bhqk,bqhd->khd/dot_general | solution.py:160
  169.6 3.4 copy.346
  174.3 47.9 %collective-permute-done.5 = f32[128,2048]{1,0:T(8,128)S(1)} collective-permute-done((f32[128,2048]{1,0:T(8,128)S(1)}, f32[128,2048]{1,0:T(8,128)S(1)}, u32[]{:S(2)}, u32[]{:S(2)}) %collective-permute-start.5) | collective-permute-done | bytes 1048608 | tf_op jit(solution)/shard_map/ppermute | solution.py:19
  234.0 4.3 %convolution_convert_fusion = bf16[1024,2048]{1,0:T(8,128)(2,1)} fusion(bf16[1,256,2048]{2,1,0:T(8,128)(2,1)S(1)} %copy-done, bf16[32,8,8,128]{3,2,1,0:T(8,128)(2,1)} %bitcast.196), kind=kOutput, calls=%fused_computation.21 | convolution fusion | flops 1075838976 | bytes 5767168 | tf_op jit(solution)/shard_map/dot_general | solution.py:190
  243.9 11.7 %collective-permute-done.6 = f32[128,2048]{1,0:T(8,128)} collective-permute-done((f32[128,2048]{1,0:T(8,128)}, f32[128,2048]{1,0:T(8,128)}, u32[]{:S(2)}, u32[]{:S(2)}) %collective-permute-start.6) | collective-permute-done | bytes 1048608 | tf_op jit(solution)/shard_map/ppermute | solution.py:19
  259.7 2.9 select_n.176
  271.7 22.6 %collective-permute-done.7 = f32[128,2048]{1,0:T(8,128)} collective-permute-done((f32[128,2048]{1,0:T(8,128)}, f32[128,2048]{1,0:T(8,128)}, u32[]{:S(2)}, u32[]{:S(2)}) %collective-permute-start.7) | collective-permute-done | bytes 1048608 | tf_op jit(solution)/shard_map/ppermute | solution.py:19
  311.2 26.8 %collective-permute-done.8 = f32[128,2048]{1,0:T(8,128)} collective-permute-done((f32[128,2048]{1,0:T(8,128)}, f32[128,2048]{1,0:T(8,128)}, u32[]{:S(2)}, u32[]{:S(2)}) %collective-permute-start.8) | collective-permute-done | bytes 1048608 | tf_op jit(solution)/shard_map/ppermute | solution.py:19
  354.1 4.7 %fusion.11 = bf16[1,256,2048]{2,1,0:T(8,128)(2,1)} fusion(bf16[1024,2048]{1,0:T(8,128)(2,1)} %all-gather.2.cloned.1.call-done, bf16[32,8,8,128]{3,2,1,0:T(8,128)(2,1)} %bitcast.197), kind=kOutput, calls=%fused_computation.27 | convolution fusion | flops 1074266112 | bytes 5767168 | tf_op jit(solution)/shard_map/dot_general | solution.py:123
  367.6 3.7 reshape.180
  374.2 6.6 %reduce-scatter.2.cloned.1.call-done = bf16[32,2048]{1,0:T(8,128)(2,1)} async-done(((bf16[1024,2048]{1,0:T(8,128)(2,1)}), bf16[32,2048]{1,0:T(8,128)(2,1)}) %reduce-scatter.2.cloned.1.call-update) | async-done | bytes 131088 | tf_op jit(solution)/shard_map/reduce_scatter | solution.py:189
  (172 shorter events, 144.3 us)
Async XLA Ops:
  7.2 138.3 %copy-start = (bf16[1,256,2048]{2,1,0:T(8,128)(2,1)S(1)}, bf16[1,256,2048]{2,1,0:T(8,128)(2,1)}, u32[]{:S(2)}) copy-start(bf16[1,256,2048]{2,1,0:T(8,128)(2,1)} %param.9) | copy-start | bytes 3145732
  7.2 138.3 %all-gather.2.cloned.1.call-start = ((), (), s32[]{:S(2)}) async-start(), calls=%async_computation.1 | async-start | bytes 4325376 | tf_op jit(solution)/shard_map/all_gather | solution.py:70
  12.9 2.1 collective-permute-start
  23.4 16.1 %collective-permute-start.1 = (bf16[128,2048]{1,0:T(8,128)(2,1)S(1)}, bf16[128,2048]{1,0:T(8,128)(2,1)S(1)}, u32[]{:S(2)}, u32[]{:S(2)}) collective-permute-start(bf16[128,2048]{1,0:T(8,128)(2,1)S(1)} %bitcast.202), channel_id=1, source_target_pairs={{0,2},{1,3},{2,0},{3,1},{4,6},{5,7},{6,4},{7,5},{8,10},{9,11},{10,... | collective-permute-start | bytes 1572872 | tf_op jit(solution)/shard_map/ppermute | solution.py:19
  26.3 354.4 %reduce-scatter.2.cloned.1.call-start = ((), (), s32[]{:S(2)}) async-start(), calls=%async_computation.2 | async-start | bytes 4325376 | tf_op jit(solution)/shard_map/reduce_scatter | solution.py:189
  47.7 6.3 %copy-start.13 = (bf16[1,256,1024]{2,1,0:T(8,128)(2,1)S(1)}, bf16[1,256,1024]{2,1,0:T(8,128)(2,1)}, u32[]{:S(2)}) copy-start(bf16[1,256,1024]{2,1,0:T(8,128)(2,1)} %param.7) | copy-start | bytes 1572868
  48.8 14.7 %collective-permute-start.2 = (bf16[128,2048]{1,0:T(8,128)(2,1)}, bf16[128,2048]{1,0:T(8,128)(2,1)}, u32[]{:S(2)}, u32[]{:S(2)}) collective-permute-start(bf16[128,2048]{1,0:T(8,128)(2,1)} %bitcast.173), channel_id=1, source_target_pairs={{0,4},{1,5},{2,6},{3,7},{4,0},{5,1},{6,2},{7,3},{8,12},{9,13},{10,... | collective-permute-start | bytes 1572872 | tf_op jit(solution)/shard_map/ppermute | solution.py:19
  68.3 6.3 %copy-start.17 = (bf16[1,2,128,2048]{3,2,1,0:T(8,128)(2,1)S(1)}, bf16[1,2,128,2048]{3,2,1,0:T(8,128)(2,1)}, u32[]{:S(2)}) copy-start(bf16[1,2,128,2048]{3,2,1,0:T(8,128)(2,1)} %pad_maximum_fusion.3) | copy-start | bytes 3145732
  73.1 22.3 %collective-permute-start.3 = (bf16[128,2048]{1,0:T(8,128)(2,1)S(1)}, bf16[128,2048]{1,0:T(8,128)(2,1)S(1)}, u32[]{:S(2)}, u32[]{:S(2)}) collective-permute-start(bf16[128,2048]{1,0:T(8,128)(2,1)S(1)} %bitcast.204), channel_id=1, source_target_pairs={{0,8},{1,9},{2,10},{3,11},{4,12},{5,13},{6,14},{7,15},{8,0},{9,1},... | collective-permute-start | bytes 1572872 | tf_op jit(solution)/shard_map/ppermute | solution.py:19
  107.2 25.4 %collective-permute-start.4 = (bf16[128,2048]{1,0:T(8,128)(2,1)}, bf16[128,2048]{1,0:T(8,128)(2,1)}, u32[]{:S(2)}, u32[]{:S(2)}) collective-permute-start(bf16[128,2048]{1,0:T(8,128)(2,1)} %bitcast.171), channel_id=1, source_target_pairs={{0,16},{1,17},{2,18},{3,19},{4,20},{5,21},{6,22},{7,23},{8,24},{9,... | collective-permute-start | bytes 1572872 | tf_op jit(solution)/shard_map/ppermute | solution.py:19
  114.8 17.8 %copy-start.19 = (bf16[640,2048]{1,0:T(8,128)(2,1)S(1)}, bf16[640,2048]{1,0:T(8,128)(2,1)}, u32[]{:S(2)}) copy-start(bf16[640,2048]{1,0:T(8,128)(2,1)} %get-tuple-element.29) | copy-start | bytes 7864324
  116.8 26.4 %copy-start.2 = (f32[2,8,256,128]{3,2,1,0:T(8,128)}, f32[2,8,256,128]{3,2,1,0:T(8,128)S(1)}, u32[]{:S(2)}) copy-start(f32[2,8,256,128]{3,2,1,0:T(8,128)S(1)} %get-tuple-element.34) | copy-start | bytes 6291460
  149.4 5.4 %slice-start = ((s8[5242880]{0:T(1024)(128)(4,1)}), s8[1048576]{0:T(1024)(128)(4,1)S(1)}, s32[]{:S(2)}) async-start(s8[5242880]{0:T(1024)(128)(4,1)} %bitcast.176), calls=%async_computation.3 | async-start | bytes 2097152
  150.6 4.2 %slice-start.1 = ((s8[5242880]{0:T(1024)(128)(4,1)}), s8[4194304]{0:T(1024)(128)(4,1)S(1)}, s32[]{:S(2)}) async-start(s8[5242880]{0:T(1024)(128)(4,1)} %bitcast.176), calls=%async_computation.4 | async-start | bytes 8388608
  150.6 4.2 %copy-start.24 = (bf16[640,1024]{0,1:T(8,128)(2,1)S(1)}, bf16[640,1024]{0,1:T(8,128)(2,1)}, u32[]{:S(2)}) copy-start(bf16[640,1024]{0,1:T(8,128)(2,1)} %copy.321) | copy-start | bytes 3932164
  174.3 47.9 %collective-permute-start.5 = (f32[128,2048]{1,0:T(8,128)S(1)}, f32[128,2048]{1,0:T(8,128)S(1)}, u32[]{:S(2)}, u32[]{:S(2)}) collective-permute-start(f32[128,2048]{1,0:T(8,128)S(1)} %fusion.39), channel_id=1, source_target_pairs={{0,16},{1,17},{2,18},{3,19},{4,20},{5,21},{6,22},{7,23},{8,24},{9,... | collective-permute-start | bytes 3145736 | tf_op jit(solution)/shard_map/ppermute | solution.py:19
  228.3 27.3 %collective-permute-start.6 = (f32[128,2048]{1,0:T(8,128)}, f32[128,2048]{1,0:T(8,128)}, u32[]{:S(2)}, u32[]{:S(2)}) collective-permute-start(f32[128,2048]{1,0:T(8,128)} %fusion.41), channel_id=1, source_target_pairs={{0,8},{1,9},{2,10},{3,11},{4,12},{5,13},{6,14},{7,15},{8,0},{9,1},... | collective-permute-start | bytes 3145736 | tf_op jit(solution)/shard_map/ppermute | solution.py:19
  265.5 28.8 %collective-permute-start.7 = (f32[128,2048]{1,0:T(8,128)}, f32[128,2048]{1,0:T(8,128)}, u32[]{:S(2)}, u32[]{:S(2)}) collective-permute-start(f32[128,2048]{1,0:T(8,128)} %fusion.43), channel_id=1, source_target_pairs={{0,4},{1,5},{2,6},{3,7},{4,0},{5,1},{6,2},{7,3},{8,12},{9,13},{10,... | collective-permute-start | bytes 3145736 | tf_op jit(solution)/shard_map/ppermute | solution.py:19
  301.4 4.4 %copy-start.7 = (bf16[2,8,128,256]{2,3,1,0:T(8,128)(2,1)S(1)}, bf16[2,8,128,256]{2,3,1,0:T(8,128)(2,1)}, u32[]{:S(2)}) copy-start(bf16[2,8,128,256]{2,3,1,0:T(8,128)(2,1)} %multiply_convert_fusion) | copy-start | bytes 3145732
  301.4 4.4 %copy-start.9 = (bf16[2,256,1024]{1,2,0:T(8,128)(2,1)S(1)}, bf16[2,256,1024]{1,2,0:T(8,128)(2,1)}, u32[]{:S(2)}) copy-start(bf16[2,256,1024]{1,2,0:T(8,128)(2,1)} %copy.311) | copy-start | bytes 3145732
  301.4 4.8 %copy-start.11 = (bf16[640,1024]{0,1:T(8,128)(2,1)S(1)}, bf16[640,1024]{0,1:T(8,128)(2,1)}, u32[]{:S(2)}) copy-start(bf16[640,1024]{0,1:T(8,128)(2,1)} %copy.314) | copy-start | bytes 3932164
  304.2 33.8 %collective-permute-start.8 = (f32[128,2048]{1,0:T(8,128)}, f32[128,2048]{1,0:T(8,128)}, u32[]{:S(2)}, u32[]{:S(2)}) collective-permute-start(f32[128,2048]{1,0:T(8,128)} %fusion.38), channel_id=1, source_target_pairs={{0,2},{1,3},{2,0},{3,1},{4,6},{5,7},{6,4},{7,5},{8,10},{9,11},{10,... | collective-permute-start | bytes 3145736 | tf_op jit(solution)/shard_map/ppermute | solution.py:19
  344.0 19.3 %collective-permute-start.9 = (f32[128,2048]{1,0:T(8,128)}, f32[128,2048]{1,0:T(8,128)}, u32[]{:S(2)}, u32[]{:S(2)}) collective-permute-start(f32[128,2048]{1,0:T(8,128)} %fusion.44), channel_id=1, source_target_pairs={{0,1},{1,0},{2,3},{3,2},{4,5},{5,4},{6,7},{7,6},{8,9},{9,8},{10,11... | collective-permute-start | bytes 3145736 | tf_op jit(solution)/shard_map/ppermute | solution.py:19
  354.1 4.7 %copy-start.21 = (f32[64,2048]{1,0:T(8,128)S(1)}, f32[64,2048]{1,0:T(8,128)}, u32[]{:S(2)}) copy-start(f32[64,2048]{1,0:T(8,128)} %get-tuple-element.14) | copy-start | bytes 1572868
  (18 other events, 40.4 us)
Sparse Core Ops, SparseCore 0:
  26.5 66.5 all-gather.1
  238.5 142.2 reduce-scatter.1
where the time goes:
time: 395 us; the launch traced here: 389 us
  waiting for transfers between devices  174 us (44%)
  local copies, waits for them, and re-layouts  88 us (22%)
  other arithmetic  65.9 us (17%)
  matrix products  35.8 us (9%)
  between operations  14.9 us (4%)
  starting transfers between devices  11.3 us (3%)
    ppermute x10, waiting for transfers between devices, partner_2(): return lax.ppermute(value, axis, pairs)  167 us
    convert_element_type x5, other arithmetic, pool_pairs(): return ((shaped[:, 0] + shaped[:, 1]) * HALF_ROOT).astype(jnp.bfloat16)  19.1 us
    broadcast_in_dim x9, local copies, waits for them, and re-layouts, unpool_pairs(): jnp.broadcast_to(spread[:, None, :], (spread.shape[0], 2, spread.shape[1]))  13.4 us
    ppermute x10, starting transfers between devices, partner_2(): return lax.ppermute(value, axis, pairs)  10.9 us
    add x4, other arithmetic, body(): partner_grad + jnp.where(upper_bits[height] == 0, tail_half, lead_half)  10.8 us
    convert_element_type x4, local copies, waits for them, and re-layouts, pool_pairs(): row_data.astype(jnp.float32)  10.2 us
    select_n x4, local copies, waits for them, and re-layouts, body(): own_grad = jnp.where(upper_bits[height] == 0, lead_half, tail_half)  9.53 us
    select_n x4, local copies, waits for them, and re-layouts, body(): jnp.where(upper_bits[height] == 0, tail_half, lead_half)  8.31 us
  transfers between devices with their start and end apart: 12, of which 10 were waited for; matrix products, arithmetic and copies ran while one was open for 35% of the time, Pallas kernels for 0%

commit v1 on v0

v1 whole, which is shorter than its diff:
```python
import math

import jax
import jax.numpy as jnp
from jax import lax
from jax.experimental import pallas as pl
from jax.experimental.pallas import tpu as pltpu
from jax.sharding import PartitionSpec as P

HEADS = 8
HS = 128
NR = 128

HALF_ROOT = 0.7071067811865476
SCORE_SCALE = 1.0 / math.sqrt(HS)
EXP2_SCALE = SCORE_SCALE * math.log2(math.e)
F32 = jnp.float32
BF16 = jnp.bfloat16
VMEM_LIMIT = 40 * 1024 * 1024


def permute(value, masks):
    count = lax.axis_size("seq")
    return lax.ppermute(value, "seq", [(i, i ^ masks[i & 1]) for i in range(count)])


def swap(value, mask):
    return permute(value, (mask, mask))


def call(body, meta, operands, specs, shapes, out_specs, scratch=(), grid=(1,), flops=0):
    moved = sum(math.prod(o.shape) * o.dtype.itemsize for o in operands)
    moved += sum(math.prod(s.shape) * s.dtype.itemsize for s in jax.tree.leaves(shapes))
    return pl.pallas_call(
        body,
        grid_spec=pltpu.PrefetchScalarGridSpec(
            num_scalar_prefetch=1,
            grid=grid,
            in_specs=specs,
            out_specs=out_specs,
            scratch_shapes=list(scratch),
        ),
        out_shape=shapes,
        compiler_params=pltpu.CompilerParams(vmem_limit_bytes=VMEM_LIMIT),
        cost_estimate=pl.CostEstimate(flops=flops, bytes_accessed=moved, transcendentals=0),
    )(meta, *operands)


def whole(array):
    return pl.BlockSpec(array.shape, lambda i, m: (0,) * len(array.shape))


def own_half(array):
    return pl.BlockSpec((array.shape[0], array.shape[1] // 2), lambda i, m: (0, m[0]))


def struct(rows, cols, dtype):
    return jax.ShapeDtypeStruct((rows, cols), dtype)


def dot(a, b, dims):
    return lax.dot_general(a, b, (dims, ((), ())), preferred_element_type=F32)


NN = ((1,), (0,))
NT = ((1,), (1,))
TN = ((0,), (0,))


def group_matrix(rows, cols, row_div, col_div):
    row = lax.broadcasted_iota(jnp.int32, (rows, cols), 0) // row_div
    col = lax.broadcasted_iota(jnp.int32, (rows, cols), 1) // col_div
    return jnp.where(row == col, 1.0, 0.0).astype(BF16)


def pool(rows):
    half = rows.shape[0] // 2
    return (dot(group_matrix(half, 2 * half, 1, 2), rows, NN) * HALF_ROOT).astype(BF16)


def spread(grad, times, factor):
    high = grad.astype(BF16)
    low = (grad - high.astype(F32)).astype(BF16)
    matrix = group_matrix(times * grad.shape[0], grad.shape[0], times, 1)
    return (dot(matrix, high, NN) + dot(matrix, low, NN)) * factor


def pool_body(meta, keys, values, other, *outs):
    own = jnp.concatenate([keys[...], values[...]], axis=1)
    first_own = pool(own)
    first_other = pool(other[...])
    outs[0][...] = first_own
    outs[1][...] = first_other
    rows = jnp.concatenate([pool(first_own), pool(first_other)], axis=0)
    outs[2][...] = rows
    for out in outs[3:]:
        rows = pool(rows)
        out[...] = rows


def forward_body(heads, n_far, meta, q_own, q_other, k_own, v_own, k_other, v_other, *refs):
    near_k = (k_own, k_other)
    near_v = (v_own, v_other)
    next_k = refs[0:2]
    next_v = refs[2:4]
    far_k_refs = refs[4 : 4 + n_far]
    far_v_refs = refs[4 + n_far : 4 + 2 * n_far]
    attn_ref, probs_ref = refs[4 + 2 * n_far :]
    for head in range(heads):
        at = slice(head * HS, (head + 1) * HS)
        far_k = [ref[:, at] for ref in far_k_refs]
        far_v = [ref[:, at] for ref in far_v_refs]
        for group, q_ref in enumerate((q_own, q_other)):
            length = q_ref.shape[0]
            key = jnp.concatenate([near_k[group][:, at], next_k[group][:, at]] + far_k, axis=0)
            value = jnp.concatenate([near_v[group][:, at], next_v[group][:, at]] + far_v, axis=0)
            scores = dot(key, q_ref[:, at], NT)
            top = jnp.max(scores, axis=0, keepdims=True)
            weights = jnp.exp2((scores - top) * EXP2_SCALE)
            total = jnp.sum(weights, axis=0, keepdims=True)
            probs = (weights * (1.0 / total)).astype(BF16)
            probs_ref[2 * head + group] = probs
            attn = dot(value, probs, TN)
            attn_ref[at, group * length : (group + 1) * length] = attn.astype(BF16)


def backward_body(
    heads, n_far, meta, q_own, q_other, k_own, v_own, k_other, v_other, d_keep, d_recv, probs_ref, *refs
):
    near_k = (k_own, k_other)
    near_v = (v_own, v_other)
    next_k = refs[0:2]
    next_v = refs[2:4]
    far_k_refs = refs[4 : 4 + n_far]
    far_v_refs = refs[4 + n_far : 4 + 2 * n_far]
    refs = refs[4 + 2 * n_far :]
    dq_refs = refs[0:2]
    near_dk = refs[2:4]
    near_dv = refs[4:6]
    far_dk = refs[6 : 6 + n_far]
    far_dv = refs[6 + n_far : 6 + 2 * n_far]
    near = near_k[0].shape[0]
    after = near + next_k[0].shape[0]
    for head in range(heads):
        at = slice(head * HS, (head + 1) * HS)
        far_k = [ref[:, at] for ref in far_k_refs]
        far_v = [ref[:, at] for ref in far_v_refs]
        dks = []
        dvs = []
        for group, q_ref in enumerate((q_own, q_other)):
            length = q_ref.shape[0]
            rows = slice(group * length, (group + 1) * length)
            query = q_ref[:, at]
            key = jnp.concatenate([near_k[group][:, at], next_k[group][:, at]] + far_k, axis=0)
            value = jnp.concatenate([near_v[group][:, at], next_v[group][:, at]] + far_v, axis=0)
            d_attn = (d_keep[rows, at] + d_recv[rows, at].astype(F32)).astype(BF16)
            probs_low = probs_ref[2 * head + group]
            probs = probs_low.astype(F32)
            d_prob = dot(value, d_attn, NT)
            center = jnp.sum(probs * d_prob, axis=0, keepdims=True)
            d_score = (probs * (d_prob - center)).astype(BF16)
            dq = dot(key, d_score, TN) * SCORE_SCALE
            dq_refs[group][:, at] = dq.T.astype(BF16)
            dks.append(dot(d_score, query, NN) * SCORE_SCALE)
            dvs.append(dot(probs_low, d_attn, NN))
        for grads, near_out, far_out in ((dks, near_dk, far_dk), (dvs, near_dv, far_dv)):
            for group in range(2):
                total = grads[group][:near] + spread(grads[1 - group][near:after], 2, HALF_ROOT)
                near_out[group][:, at] = total.astype(near_out[group].dtype)
            far = grads[0][after:] + grads[1][after:]
            start = 0
            for out in far_out:
                out[:, at] = far[start : start + out.shape[0]].astype(BF16)
                start += out.shape[0]


def ordered_weight(meta, first, second, scratch, piece):
    half = first.shape[0] // piece
    for index in range(2 * half):
        source = first if index < half else second
        start = (index % half) * piece
        place = pl.multiple_of(meta[1 + index] * piece, piece)
        scratch[pl.ds(place, piece), :] = source[start : start + piece, :]


def d_attn_body(piece, meta, grad_own, grad_other, first, second, keep, send, scratch):
    ordered_weight(meta, first, second, scratch, piece)
    length = grad_own.shape[0]
    width = keep.shape[1]
    mine = scratch[pl.ds(pl.multiple_of(meta[0] * width, width), width), :]
    theirs = scratch[pl.ds(pl.multiple_of((1 - meta[0]) * width, width), width), :]
    send[:length] = dot(grad_other[...], theirs, NT).astype(BF16)
    send[length:] = dot(grad_own[...], theirs, NT).astype(BF16)
    keep[:length] = dot(grad_own[...], mine, NT)
    keep[length:] = dot(grad_other[...], mine, NT)


def attended_body(piece, meta, attn_mine, attn_theirs, first, second, keep, send, scratch):
    ordered_weight(meta, first, second, scratch, piece)
    length = keep.shape[0]
    width = attn_mine.shape[0]
    mine = scratch[pl.ds(pl.multiple_of(meta[0] * width, width), width), :]
    theirs = scratch[pl.ds(pl.multiple_of((1 - meta[0]) * width, width), width), :]
    send[...] = (
        dot(attn_mine[:, length:], mine, TN) + dot(attn_theirs[:, :length], theirs, TN)
    ).astype(BF16)
    keep[...] = (
        dot(attn_mine[:, :length], mine, TN) + dot(attn_theirs[:, length:], theirs, TN)
    ).astype(BF16)


def weight_grad_body(piece, meta, attn_mine, attn_theirs, grad_own, grad_other, keep, send, scratch):
    length = grad_own.shape[0]
    width = attn_mine.shape[0]
    mine = dot(attn_mine[:, :length], grad_own[...], NN) + dot(
        attn_mine[:, length:], grad_other[...], NN
    )
    scratch[pl.ds(pl.multiple_of(meta[0] * width, width), width), :] = mine.astype(BF16)
    theirs = dot(attn_theirs[:, length:], grad_own[...], NN) + dot(
        attn_theirs[:, :length], grad_other[...], NN
    )
    scratch[pl.ds(pl.multiple_of((1 - meta[0]) * width, width), width), :] = theirs.astype(BF16)
    half = keep.shape[0] // piece
    for index in range(2 * half):
        target = keep if index < half else send
        start = (index % half) * piece
        place = pl.multiple_of(meta[1 + index] * piece, piece)
        target[start : start + piece, :] = scratch[pl.ds(place, piece), :]


def cascade_body(counts, meta, *refs):
    total = None
    start = 0
    for count in counts:
        level = refs[start][...].astype(F32)
        for ref in refs[start + 1 : start + count]:
            level = level + ref[...].astype(F32)
        start += count
        total = level if total is None else level + spread(total, 2, HALF_ROOT)
    keep, send = refs[start:]
    half = keep.shape[0]
    keep[...] = total[:half]
    send[...] = total[half:].astype(BF16)


def finish_body(meta, dk_keep, dv_keep, dk_recv, dv_recv, up_keep, up_recv, dk, dv):
    width = dk_keep.shape[1]
    times = dk_keep.shape[0] // up_keep.shape[0]
    factor = HALF_ROOT * HALF_ROOT
    kept = spread(up_keep[...], times, factor)
    matrix = group_matrix(dk.shape[0], up_recv.shape[0], times, 1)
    received = dot(matrix, up_recv[...], NN) * factor
    mine = pl.ds(pl.multiple_of(meta[0] * width, width), width)
    theirs = pl.ds(pl.multiple_of((1 - meta[0]) * width, width), width)
    dk[:, mine] = (dk_keep[...] + kept[:, :width]).astype(BF16)
    dv[:, mine] = (dv_keep[...] + kept[:, width:]).astype(BF16)
    dk[:, theirs] = (dk_recv[...].astype(F32) + received[:, :width]).astype(BF16)
    dv[:, theirs] = (dv_recv[...].astype(F32) + received[:, width:]).astype(BF16)


def place_body(meta, keep, received, out):
    @pl.when(pl.program_id(0) == 0)
    def _():
        out[...] = keep[...]

    @pl.when(pl.program_id(0) == 1)
    def _():
        out[...] = received[...]


def place_halves(meta, keep, received):
    rows, cols = keep.shape
    return call(
        place_body,
        meta,
        (keep, received),
        [whole(keep), whole(received)],
        struct(rows, 2 * cols, keep.dtype),
        pl.BlockSpec((rows, cols), lambda i, m: (0, (m[0] + i) % 2)),
        grid=(2,),
    )


def other_half(array, bit):
    width = array.shape[1] // 2
    return lax.dynamic_slice_in_dim(array, (1 - bit) * width, width, 1)


def body(queries, keys, values, out_weight, out_grad):
    inner = queries.shape[2]
    half = inner // 2
    length = queries.shape[1]
    heads = HEADS // 2
    seq_count = lax.axis_size("seq")
    seq_levels = seq_count.bit_length() - 1
    dp_count = lax.axis_size("dp")
    rank = lax.axis_index("seq")
    bit = rank % 2
    pair = rank // 2
    token_total = length * seq_count * queries.shape[0] * dp_count

    up = [1 << level for level in reversed(range(1, seq_levels))]
    orders = (up, up[:-2] + up[:-3:-1])
    stages = list(zip(*orders, strict=True))
    pieces = seq_count // 2
    masks = [
        [sum(m for s, m in enumerate(order) if index >> s & 1) // 2 for index in range(pieces)]
        for order in orders
    ]
    table = pair ^ jnp.where(bit == 0, jnp.array(masks[0]), jnp.array(masks[1]))
    meta = jnp.concatenate([jnp.reshape(bit, (1,)), table]).astype(jnp.int32)

    query = queries[0]
    key = keys[0]
    value = values[0]
    grad = out_grad[0]
    if dp_count > 1:
        out_weight = lax.all_gather(out_weight, "dp", axis=1, tiled=True)
    cols = out_weight.shape[1] // 2
    piece = 2 * out_weight.shape[0]

    kv_other = swap(jnp.concatenate([other_half(key, bit), other_half(value, bit)], axis=1), 1)
    w_mine = lax.dynamic_slice_in_dim(out_weight, bit * cols, cols, 1)
    w_theirs = swap(other_half(out_weight, bit), 1)
    q_other = swap(other_half(query, bit), 1)
    g_other = swap(other_half(grad, bit), 1)

    sizes = [length // 2, length // 2] + [2 * length >> level for level in range(2, seq_levels + 1)]
    shapes = [struct(rows, inner, BF16) for rows in sizes]
    pooled = call(
        pool_body,
        meta,
        (key, value, kv_other),
        [own_half(key), own_half(value), whole(kv_other)],
        shapes,
        [whole(s) for s in shapes],
    )
    next_own, next_other = pooled[:2]
    coarse = dict(zip(range(1, seq_levels), pooled[2:], strict=True))

    w_rows = jnp.where(
        bit == 0,
        jnp.concatenate([w_mine, w_theirs], axis=0),
        jnp.concatenate([w_theirs, w_mine], axis=0),
    )

    far_masks = [(h, (1 << h) + (low << 3)) for h in range(3, seq_levels) for low in range(1 << (h - 3))]
    high_parts = [swap(coarse[h], mask) for h, mask in far_masks]
    panels = [swap(coarse[1], 2), swap(coarse[2], 4), swap(coarse[2], 6)]
    high = jnp.concatenate(high_parts, axis=0)
    panels += [high, swap(high, 2), swap(high, 4), swap(high, 6)]
    n_far = len(panels)

    for step, stage in enumerate(stages):
        received = permute(w_rows, stage)
        if step + 1 < len(stages):
            w_rows = jnp.concatenate([w_rows, received], axis=0)
    w_first, w_second = w_rows, received

    per_step = 2
    steps = heads // per_step
    width = per_step * HS

    def of_own(array):
        return pl.BlockSpec((array.shape[0], width), lambda i, m: (0, m[0] * steps + i))

    def left(array):
        return pl.BlockSpec((array.shape[0], width), lambda i, m: (0, i))

    def right(array):
        return pl.BlockSpec((array.shape[0], width), lambda i, m: (0, steps + i))

    key_count = length + length // 2 + sum(p.shape[0] for p in panels)
    token_ops = (query, q_other, key, value, kv_other, kv_other)
    token_specs = [of_own(query), left(q_other), of_own(key), of_own(value), left(kv_other), right(kv_other)]
    panel_ops = (next_other, next_own, next_other, next_own, *panels, *panels)
    panel_specs = [left(next_other), left(next_own), right(next_other), right(next_own)]
    panel_specs += [left(p) for p in panels] + [right(p) for p in panels]
    probs_shape = jax.ShapeDtypeStruct((2 * heads, key_count, length), BF16)
    probs_spec = pl.BlockSpec((2 * per_step, key_count, length), lambda i, m: (i, 0, 0))
    one_matmul = 2 * 2 * length * key_count * half
    attn_mine, probs = call(
        lambda *refs: forward_body(per_step, n_far, *refs),
        meta,
        token_ops + panel_ops,
        token_specs + panel_specs,
        [struct(half, 2 * length, BF16), probs_shape],
        [pl.BlockSpec((width, 2 * length), lambda i, m: (i, 0)), probs_spec],
        grid=(steps,),
        flops=2 * one_matmul,
    )
    attn_theirs = swap(attn_mine, 1)

    half_rows = pieces * piece // 2
    scratch = [pltpu.VMEM((2 * half_rows, cols), BF16)]
    g_spec = [own_half(grad), whole(g_other)]
    half_shape = struct(half_rows, cols, BF16)
    proj_flops = 2 * 2 * length * inner * cols
    wg_keep, wg_send = call(
        lambda *refs: weight_grad_body(piece, *refs),
        meta,
        (attn_mine, attn_theirs, grad, g_other),
        [whole(attn_mine), whole(attn_theirs)] + g_spec,
        [half_shape, half_shape],
        [whole(half_shape), whole(half_shape)],
        scratch,
        flops=proj_flops,
    )
    for step, stage in enumerate(reversed(stages)):
        received = permute(wg_send, stage)
        total = wg_keep.astype(F32) + received.astype(F32)
        if step + 1 < len(stages):
            total = total.astype(BF16)
            rows = total.shape[0] // 2
            wg_keep, wg_send = total[:rows], total[rows:]
    rows = piece // 2
    wg_mine = lax.dynamic_slice_in_dim(total, bit * rows, rows, 0)
    wg_theirs = swap(lax.dynamic_slice_in_dim(total, (1 - bit) * rows, rows, 0).astype(BF16), 1)
    wg_theirs = wg_theirs.astype(F32)
    weight_grad = jnp.where(
        bit == 0,
        jnp.concatenate([wg_mine, wg_theirs], axis=1),
        jnp.concatenate([wg_theirs, wg_mine], axis=1),
    )
    if dp_count > 1:
        weight_grad = lax.psum_scatter(
            weight_grad.astype(BF16), "dp", scatter_dimension=1, tiled=True
        ).astype(F32)
    weight_grad = weight_grad * (1.0 / math.sqrt(token_total))

    w_spec = [whole(w_first), whole(w_second)]
    d_shapes = [struct(2 * length, half, F32), struct(2 * length, half, BF16)]
    d_keep, d_send = call(
        lambda *refs: d_attn_body(piece, *refs),
        meta,
        (grad, g_other, w_first, w_second),
        g_spec + w_spec,
        d_shapes,
        [whole(s) for s in d_shapes],
        scratch,
        flops=proj_flops,
    )
    d_recv = swap(d_send, 1)

    out_shapes = [struct(length, half, BF16)] * 2
    out_shapes += [struct(length, half, F32), struct(length, half, BF16)] * 2
    out_shapes += [struct(p.shape[0], half, BF16) for p in panels] * 2
    grads = call(
        lambda *refs: backward_body(per_step, n_far, *refs),
        meta,
        token_ops + (d_keep, d_recv, probs) + panel_ops,
        token_specs + [left(d_keep), left(d_recv), probs_spec] + panel_specs,
        out_shapes,
        [left(s) for s in out_shapes],
        grid=(steps,),
        flops=4 * one_matmul,
    )
    dq_keep, dq_send, dk_keep, dk_send, dv_keep, dv_send = grads[:6]
    panel_grads = [
        jnp.concatenate([dk, dv], axis=1)
        for dk, dv in zip(grads[6 : 6 + n_far], grads[6 + n_far :], strict=True)
    ]

    high_sum = panel_grads[3].astype(F32)
    for part, mask in zip(panel_grads[4:], (2, 4, 6), strict=True):
        high_sum = high_sum + swap(part, mask).astype(F32)
    high_sum = high_sum.astype(BF16)
    by_level = {1: [swap(panel_grads[0], 2)], 2: [swap(panel_grads[1], 4), swap(panel_grads[2], 6)]}
    start = 0
    for h, mask in far_masks:
        rows = coarse[h].shape[0]
        by_level.setdefault(h, []).append(swap(high_sum[start : start + rows], mask))
        start += rows
    levels = list(reversed(range(1, seq_levels)))
    received = [part for h in levels for part in by_level[h]]
    counts = [len(by_level[h]) for h in levels]
    up_rows = coarse[1].shape[0] // 2
    up_shapes = [struct(up_rows, inner, F32), struct(up_rows, inner, BF16)]
    up_keep, up_send = call(
        lambda *refs: cascade_body(counts, *refs),
        meta,
        received,
        [whole(r) for r in received],
        up_shapes,
        [whole(s) for s in up_shapes],
    )
    up_recv = swap(up_send, 1)
    dk_recv = swap(dk_send, 1)
    dv_recv = swap(dv_send, 1)
    dq_recv = swap(dq_send, 1)
    fin_ops = (dk_keep, dv_keep, dk_recv, dv_recv, up_keep, up_recv)
    fin_shape = struct(length, inner, BF16)
    grad_keys, grad_values = call(
        finish_body,
        meta,
        fin_ops,
        [whole(o) for o in fin_ops],
        [fin_shape, fin_shape],
        [whole(fin_shape), whole(fin_shape)],
    )
    grad_queries = place_halves(meta, dq_keep, dq_recv)

    at_shape = struct(length, cols, BF16)
    at_keep, at_send = call(
        lambda *refs: attended_body(piece, *refs),
        meta,
        (attn_mine, attn_theirs, w_first, w_second),
        [whole(attn_mine), whole(attn_theirs)] + w_spec,
        [at_shape, at_shape],
        [whole(at_shape), whole(at_shape)],
        scratch,
        flops=proj_flops,
    )
    attended = place_halves(meta, at_keep, swap(at_send, 1))
    return (attended[None], grad_queries[None], grad_keys[None], grad_values[None], weight_grad)


def solution(mesh):
    placed = (
        P("dp", "seq", None),
        P("dp", "seq", None),
        P("dp", "seq", None),
        P("seq", "dp"),
        P("dp", "seq", None),
    )
    return jax.shard_map(
        body,
        mesh=mesh,
        in_specs=placed,
        out_specs=(
            P("dp", "seq", None),
            P("dp", "seq", None),
            P("dp", "seq", None),
            P("dp", "seq", None),
            P("seq", "dp"),
        ),
        check_vma=False,
    )
```

time: 395 us -> 137 us (0.35); the launches traced: 389 us -> 137 us
  waiting for transfers between devices: 174 us -> 47.8 us
  local copies, waits for them, and re-layouts: 88 us -> 3.74 us
  other arithmetic: 65.9 us -> 6.35 us
  matrix products: 35.8 us -> 0 us
  starting transfers between devices: 11.3 us -> 46.1 us
  Pallas kernels: 0 us -> 32 us
  between operations: 14.9 us -> 1.04 us
    ppermute x10 -> x38, waiting for transfers between devices: 167 us -> 47.8 us  [permute(): lax.ppermute(value, 'seq', [(i, i ^ masks[i & 1]) for i in range(count)])]
    dot_general x15 -> x0, matrix products: 35.8 us -> none  [the longest x1 4.67 us: body(): jnp.dot(attn_rows, full_weight, preferred_element_type=jnp.float32)]
    ppermute x10 -> x38, starting transfers between devices: 10.9 us -> 46.1 us  [permute(): lax.ppermute(value, 'seq', [(i, i ^ masks[i & 1]) for i in range(count)])]
    pallas_call x0 -> x10, Pallas kernels: none -> 32 us  [call(): pl.pallas_call(body, grid_spec=pltpu.PrefetchScalarGridSpec(num_scalar_pr...]
    convert_element_type x12 -> x5, other arithmetic: 27.3 us -> 0.75 us  [the longest x3 0.67 us: body(): total = total.astype(BF16)]
    select_n x8 -> x0, local copies, waits for them, and re-layouts: 17.8 us -> none  [the longest x4 9.53 us: body(): own_grad = jnp.where(upper_bits[height] == 0, lead_half, tail_half)]
    convert_element_type x7 -> x1, local copies, waits for them, and re-layouts: 16.4 us -> 0.02 us  [body(): lax.dynamic_slice_in_dim(total, (1 - bit) * rows, rows, 0).astype(BF16)]
    broadcast_in_dim x10 -> x0, local copies, waits for them, and re-layouts: 14.5 us -> none  [the longest x9 13.4 us: unpool_pairs(): jnp.broadcast_to(spread[:, None, :], (spread.shape[0], 2, spread.shape[1]))]
  transfers between devices with their start and end apart: 12 -> 38, of which waited for: 10 -> 16; matrix products, arithmetic and copies ran while one was open for 35% -> 5% of each run, Pallas kernels for 0% -> 23%
where the time goes in v1:
time: 137 us
  waiting for transfers between devices  47.8 us (35%)
  starting transfers between devices  46.1 us (34%)
  Pallas kernels  32 us (23%)
  other arithmetic  6.35 us (5%)
  local copies, waits for them, and re-layouts  3.74 us (3%)
    ppermute x38, waiting for transfers between devices, permute(): lax.ppermute(value, 'seq', [(i, i ^ masks[i & 1]) for i in range(count)])  47.8 us
    ppermute x38, starting transfers between devices, permute(): lax.ppermute(value, 'seq', [(i, i ^ masks[i & 1]) for i in range(count)])  46.1 us
    pallas_call x10, Pallas kernels, call(): pl.pallas_call(body, grid_spec=pltpu.PrefetchScalarGridSpec(num_scalar_pr...  32 us
    concatenate x3, other arithmetic, body(): w_rows = jnp.concatenate([w_rows, received], axis=0)  2.9 us
  transfers between devices with their start and end apart: 38, of which 16 were waited for; matrix products, arithmetic and copies ran while one was open for 5% of the time, Pallas kernels for 23%

profile of v1, /device:TPU:0, one launch (start us, length us, event | category | flops | bytes accessed | tf_op | source)
XLA Modules:
  0.0 137.2 jit_solution(9683283737482323183)
XLA Ops:
  3.4 3.8 %collective-permute-start.13 = (bf16[64,1024]{1,0:T(8,128)(2,1)S(1)}, bf16[64,1024]{1,0:T(8,128)(2,1)}, u32[]{:S(2)}, u32[]{:S(2)}) collective-permute-start(bf16[64,1024]{1,0:T(8,128)(2,1)S(1)} %maximum_select_fusion.1), channel_id=1, source_target_pairs={{0,16},{1,17},{2,18},{3,19},{4,20},{5,21},{6,22},{7,23},{8,24},{9,... | collective-permute-start | bytes 393224 | tf_op jit(solution)/shard_map/ppermute | solution.py:24
  9.3 4.8 %collective-permute-done.13 = bf16[64,1024]{1,0:T(8,128)(2,1)} collective-permute-done((bf16[64,1024]{1,0:T(8,128)(2,1)S(1)}, bf16[64,1024]{1,0:T(8,128)(2,1)}, u32[]{:S(2)}, u32[]{:S(2)}) %collective-permute-start.13) | collective-permute-done | bytes 131104 | tf_op jit(solution)/shard_map/ppermute | solution.py:24
  18.6 5.2 %collective-permute-done.14 = bf16[128,1024]{1,0:T(8,128)(2,1)S(1)} collective-permute-done((bf16[128,1024]{1,0:T(8,128)(2,1)S(1)}, bf16[128,1024]{1,0:T(8,128)(2,1)S(1)}, u32[]{:S(2)}, u32[]{:S(2)}) %collective-permute-start.14) | collective-permute-done | bytes 262176 | tf_op jit(solution)/shard_map/ppermute | solution.py:24
  26.2 2.7 %collective-permute-start.6 = (bf16[16,1024]{1,0:T(8,128)(2,1)S(1)}, bf16[16,1024]{1,0:T(8,128)(2,1)S(1)}, u32[]{:S(2)}, u32[]{:S(2)}) collective-permute-start(bf16[16,1024]{1,0:T(8,128)(2,1)S(1)} %get-tuple-element.48), channel_id=1, source_target_pairs={{0,16},{1,17},{2,18},{3,19},{4,20},{5,21},{6,22},{7,23},{8,24},{9,... | collective-permute-start | bytes 98312 | tf_op jit(solution)/shard_map/ppermute | solution.py:24
  31.3 1.9 %collective-permute-start.4 = (bf16[64,1024]{1,0:T(8,128)(2,1)S(1)}, bf16[64,1024]{1,0:T(8,128)(2,1)S(1)}, u32[]{:S(2)}, u32[]{:S(2)}) collective-permute-start(bf16[64,1024]{1,0:T(8,128)(2,1)S(1)} %get-tuple-element.46), channel_id=1, source_target_pairs={{0,6},{1,7},{2,4},{3,5},{4,2},{5,3},{6,0},{7,1},{8,14},{9,15},{10,... | collective-permute-start | bytes 393224 | tf_op jit(solution)/shard_map/ppermute | solution.py:24
  36.7 4.4 %collective-permute-done.3.refs_12_.refs_19_.refs_15_.refs_22_ = bf16[64,1024]{1,0:T(8,128)(2,1)S(1)} collective-permute-done((bf16[64,1024]{1,0:T(8,128)(2,1)S(1)}, bf16[64,1024]{1,0:T(8,128)(2,1)S(1)}, u32[]{:S(2)}, u32[]{:S(2)}) %collective-permute-start.3) | collective-permute-done | bytes 131104 | tf_op jit(solution)/shard_map/ppermute | solution.py:24
  48.3 7.5 %shard_map.111 = (bf16[512,512]{1,0:T(8,128)(2,1)S(1)}, bf16[8,896,256]{2,1,0:T(8,128)(2,1)S(1)}) custom-call(s32[17]{0:T(128)S(1)} %pad_add_fusion.meta.refs_0_, bf16[256,1024]{1,0:T(8,128)(2,1)S(1)} %bitcast.23, bf16[256,512]{1,0:T(8,128)(2,1)S(1)} %collective-permute-done.refs_2_, bf16[256,1024]{1,0:T(8,128)(2,1)S(1)} %bitcast.18, ...), custom_call_target="tpu_custom_call" | custom-call | flops 939524096 | bytes 10223616 | tf_op jit(solution)/shard_map/pallas_call | solution.py:34
  56.9 2.2 %collective-permute-start.16 = (bf16[512,1024]{1,0:T(8,128)(2,1)S(1)}, bf16[512,1024]{1,0:T(8,128)(2,1)S(1)}, u32[]{:S(2)}, u32[]{:S(2)}) collective-permute-start(bf16[512,1024]{1,0:T(8,128)(2,1)S(1)} %pad_maximum_fusion.refs_3_), channel_id=1, source_target_pairs={{0,2},{1,5},{2,0},{3,7},{4,6},{5,1},{6,4},{7,3},{8,10},{9,13},{10,... | collective-permute-start | bytes 3145736 | tf_op jit(solution)/shard_map/ppermute | solution.py:24
  59.1 1.9 %shard_map.119 = (bf16[512,1024]{1,0:T(8,128)(2,1)S(1)}, bf16[512,1024]{1,0:T(8,128)(2,1)S(1)}) custom-call(s32[17]{0:T(128)S(1)} %pad_add_fusion.meta.refs_0_, bf16[512,512]{1,0:T(8,128)(2,1)S(1)} %get-tuple-element.49.refs_1_, bf16[512,512]{1,0:T(8,128)(2,1)S(1)} %collective-permute-done.11.refs_2_, bf16[256,2048]{1,0:T(8,128)(2,1)S(1)} %bitcast.25, ...), custom_call_target="tpu_custom_call" | custom-call | flops 1073741824 | bytes 4718592 | tf_op jit(solution)/shard_map/pallas_call | solution.py:34
  61.9 9.9 %collective-permute-done.16.refs_4_ = bf16[512,1024]{1,0:T(8,128)(2,1)S(1)} collective-permute-done((bf16[512,1024]{1,0:T(8,128)(2,1)S(1)}, bf16[512,1024]{1,0:T(8,128)(2,1)S(1)}, u32[]{:S(2)}, u32[]{:S(2)}) %collective-permute-start.16) | collective-permute-done | bytes 1048608 | tf_op jit(solution)/shard_map/ppermute | solution.py:24
  71.9 2.0 %shard_map.114 = (f32[512,512]{1,0:T(8,128)S(1)}, bf16[512,512]{1,0:T(8,128)(2,1)S(1)}) custom-call(s32[17]{0:T(128)S(1)} %pad_add_fusion.meta.refs_0_, bf16[256,2048]{1,0:T(8,128)(2,1)S(1)} %bitcast.26, bf16[256,1024]{1,0:T(8,128)(2,1)S(1)} %collective-permute-done.18.refs_2_.refs_4_, bf16[512,1024]{1,0:T(8,128)(2,1)S(1)} %pad_maximum_fusion.refs_3_, ...), custom_call_target="tpu_custom_call" | custom-call | flops 1073741824 | bytes 5242880 | tf_op jit(solution)/shard_map/pallas_call | solution.py:34
  74.0 2.0 %shard_map.112 = (bf16[256,1024]{1,0:T(8,128)(2,1)S(1)}, bf16[256,1024]{1,0:T(8,128)(2,1)S(1)}) custom-call(s32[17]{0:T(128)S(1)} %pad_add_fusion.meta.refs_0_, bf16[512,512]{1,0:T(8,128)(2,1)S(1)} %get-tuple-element.49.refs_1_, bf16[512,512]{1,0:T(8,128)(2,1)S(1)} %collective-permute-done.11.refs_2_, bf16[512,1024]{1,0:T(8,128)(2,1)S(1)} %pad_maximum_fusion.refs_3_, ...), custom_call_target="tpu_custom_call" | custom-call | flops 1073741824 | bytes 4194304 | tf_op jit(solution)/shard_map/pallas_call | solution.py:34
  76.5 6.6 %collective-permute-done.33 = bf16[512,1024]{1,0:T(8,128)(2,1)S(1)} collective-permute-done((bf16[512,1024]{1,0:T(8,128)(2,1)S(1)}, bf16[512,1024]{1,0:T(8,128)(2,1)S(1)}, u32[]{:S(2)}, u32[]{:S(2)}) %collective-permute-start.33) | collective-permute-done | bytes 1048608 | tf_op jit(solution)/shard_map/ppermute | solution.py:24
  84.3 10.5 %shard_map.115 = (bf16[256,512]{1,0:T(8,128)(2,1)S(1)}, bf16[256,512]{1,0:T(8,128)(2,1)}, f32[256,512]{1,0:T(8,128)S(1)}, bf16[256,512]{1,0:T(8,128)(2,1)}, f32[...) custom-call(s32[17]{0:T(128)S(1)} %pad_add_fusion.meta.refs_0_, ...), custom_call_target="tpu_custom_call" | custom-call | flops 1879048192 | bytes 14417920 | tf_op jit(solution)/shard_map/pallas_call | solution.py:34
  94.8 2.9 %collective-permute-start.25 = (bf16[64,1024]{1,0:T(8,128)(2,1)S(1)}, bf16[64,1024]{1,0:T(8,128)(2,1)S(1)}, u32[]{:S(2)}, u32[]{:S(2)}) collective-permute-start(bf16[64,1024]{1,0:T(8,128)(2,1)S(1)} %pad_maximum_fusion.7), channel_id=1, source_target_pairs={{0,6},{1,7},{2,4},{3,5},{4,2},{5,3},{6,0},{7,1},{8,14},{9,15},{10,... | collective-permute-start | bytes 393224 | tf_op jit(solution)/shard_map/ppermute | solution.py:24
  98.5 3.6 %collective-permute-done.25 = bf16[64,1024]{1,0:T(8,128)(2,1)S(1)} collective-permute-done((bf16[64,1024]{1,0:T(8,128)(2,1)S(1)}, bf16[64,1024]{1,0:T(8,128)(2,1)S(1)}, u32[]{:S(2)}, u32[]{:S(2)}) %collective-permute-start.25) | collective-permute-done | bytes 131104 | tf_op jit(solution)/shard_map/ppermute | solution.py:24
  107.3 1.8 %collective-permute-start.35 = (bf16[128,1024]{1,0:T(8,128)(2,1)S(1)}, bf16[128,1024]{1,0:T(8,128)(2,1)S(1)}, u32[]{:S(2)}, u32[]{:S(2)}) collective-permute-start(bf16[128,1024]{1,0:T(8,128)(2,1)S(1)} %slice.42), channel_id=1, source_target_pairs={{0,8},{1,9},{2,10},{3,11},{4,12},{5,13},{6,14},{7,15},{8,0},{9,1},... | collective-permute-start | bytes 786440 | tf_op jit(solution)/shard_map/ppermute | solution.py:24
  109.1 3.5 %collective-permute-start.26 = (bf16[16,1024]{1,0:T(8,128)(2,1)S(1)}, bf16[16,1024]{1,0:T(8,128)(2,1)S(1)}, u32[]{:S(2)}, u32[]{:S(2)}) collective-permute-start(bf16[16,1024]{1,0:T(8,128)(2,1)S(1)} %get-tuple-element.82), channel_id=1, source_target_pairs={{0,16},{1,17},{2,18},{3,19},{4,20},{5,21},{6,22},{7,23},{8,24},{9,... | collective-permute-start | bytes 98312 | tf_op jit(solution)/shard_map/ppermute | solution.py:24
  115.2 3.5 %collective-permute-start.27 = (bf16[16,1024]{1,0:T(8,128)(2,1)S(1)}, bf16[16,1024]{1,0:T(8,128)(2,1)S(1)}, u32[]{:S(2)}, u32[]{:S(2)}) collective-permute-start(bf16[16,1024]{1,0:T(8,128)(2,1)S(1)} %get-tuple-element.81), channel_id=1, source_target_pairs={{0,24},{1,25},{2,26},{3,27},{4,28},{5,29},{6,30},{7,31},{8,16},{9,... | collective-permute-start | bytes 98312 | tf_op jit(solution)/shard_map/ppermute | solution.py:24
  118.8 2.2 %collective-permute-done.27.refs_2_ = bf16[16,1024]{1,0:T(8,128)(2,1)S(1)} collective-permute-done((bf16[16,1024]{1,0:T(8,128)(2,1)S(1)}, bf16[16,1024]{1,0:T(8,128)(2,1)S(1)}, u32[]{:S(2)}, u32[]{:S(2)}) %collective-permute-start.27) | collective-permute-done | bytes 32800 | tf_op jit(solution)/shard_map/ppermute | solution.py:24
  121.5 1.8 %shard_map.117 = (f32[64,1024]{1,0:T(8,128)S(1)}, bf16[64,1024]{1,0:T(8,128)(2,1)}) custom-call(s32[17]{0:T(128)S(1)} %pad_add_fusion.meta.refs_0_, bf16[16,1024]{1,0:T(8,128)(2,1)S(1)} %collective-permute-done.26.refs_1_, bf16[16,1024]{1,0:T(8,128)(2,1)S(1)} %collective-permute-done.27.refs_2_, bf16[32,1024]{1,0:T(8,128)(2,1)S(1)} %collective-permute-done.28.refs_3_, ...), custom_call_target="tpu_custom_call" | custom-call | bytes 1048576 | tf_op jit(solution)/shard_map/pallas_call | solution.py:34
  124.6 2.3 %collective-permute-start.36 = (bf16[64,1024]{1,0:T(8,128)(2,1)}, bf16[64,1024]{1,0:T(8,128)(2,1)}, u32[]{:S(2)}, u32[]{:S(2)}) collective-permute-start(bf16[64,1024]{1,0:T(8,128)(2,1)} %slice.44), channel_id=1, source_target_pairs={{0,16},{1,17},{2,18},{3,19},{4,20},{5,21},{6,22},{7,23},{8,24},{9,... | collective-permute-start | bytes 393224 | tf_op jit(solution)/shard_map/ppermute | solution.py:24
  130.0 2.0 %shard_map.118 = (bf16[256,1024]{1,0:T(8,128)(2,1)}, bf16[256,1024]{1,0:T(8,128)(2,1)}) custom-call(s32[17]{0:T(128)S(1)} %pad_add_fusion.meta.refs_0_, f32[256,512]{1,0:T(8,128)S(1)} %copy-done.4, f32[256,512]{1,0:T(8,128)S(1)} %copy-done.6, bf16[256,512]{1,0:T(8,128)(2,1)S(1)} %collective-permute-done.21.dk_recv, ...), custom_call_target="tpu_custom_call" | custom-call | bytes 3014656 | tf_op jit(solution)/shard_map/pallas_call | solution.py:34
  132.0 2.2 %collective-permute-done.36 = bf16[64,1024]{1,0:T(8,128)(2,1)} collective-permute-done((bf16[64,1024]{1,0:T(8,128)(2,1)}, bf16[64,1024]{1,0:T(8,128)(2,1)}, u32[]{:S(2)}, u32[]{:S(2)}) %collective-permute-start.36) | collective-permute-done | bytes 131104 | tf_op jit(solution)/shard_map/ppermute | solution.py:24
  (128 shorter events, 44.7 us)
Async XLA Ops:
  3.4 10.7 %collective-permute-start.13 = (bf16[64,1024]{1,0:T(8,128)(2,1)S(1)}, bf16[64,1024]{1,0:T(8,128)(2,1)}, u32[]{:S(2)}, u32[]{:S(2)}) collective-permute-start(bf16[64,1024]{1,0:T(8,128)(2,1)S(1)} %maximum_select_fusion.1), channel_id=1, source_target_pairs={{0,16},{1,17},{2,18},{3,19},{4,20},{5,21},{6,22},{7,23},{8,24},{9,... | collective-permute-start | bytes 393224 | tf_op jit(solution)/shard_map/ppermute | solution.py:24
  8.0 7.8 %collective-permute-start.1 = (bf16[256,1024]{1,0:T(8,128)(2,1)}, bf16[256,1024]{1,0:T(8,128)(2,1)S(1)}, u32[]{:S(2)}, u32[]{:S(2)}) collective-permute-start(bf16[256,1024]{1,0:T(8,128)(2,1)} %pad_maximum_fusion.1), channel_id=1, source_target_pairs={{0,1},{1,0},{2,3},{3,2},{4,5},{5,4},{6,7},{7,6},{8,9},{9,8},{10,11... | collective-permute-start | bytes 1572872 | tf_op jit(solution)/shard_map/ppermute | solution.py:24
  8.8 27.3 %collective-permute-start = (bf16[256,512]{1,0:T(8,128)(2,1)}, bf16[256,512]{1,0:T(8,128)(2,1)S(1)}, u32[]{:S(2)}, u32[]{:S(2)}) collective-permute-start(bf16[256,512]{1,0:T(8,128)(2,1)} %dynamic-slice_bitcast_fusion.3), channel_id=1, source_target_pairs={{0,1},{1,0},{2,3},{3,2},{4,5},{5,4},{6,7},{7,6},{8,9},{9,8},{10,11... | collective-permute-start | bytes 786440 | tf_op jit(solution)/shard_map/ppermute | solution.py:24
  15.0 8.8 %collective-permute-start.14 = (bf16[128,1024]{1,0:T(8,128)(2,1)S(1)}, bf16[128,1024]{1,0:T(8,128)(2,1)S(1)}, u32[]{:S(2)}, u32[]{:S(2)}) collective-permute-start(bf16[128,1024]{1,0:T(8,128)(2,1)S(1)} %pad_maximum_fusion.3), channel_id=1, source_target_pairs={{0,8},{1,9},{2,10},{3,11},{4,12},{5,13},{6,14},{7,15},{8,0},{9,1},... | collective-permute-start | bytes 786440 | tf_op jit(solution)/shard_map/ppermute | solution.py:24
  17.2 12.9 %collective-permute-start.5 = (bf16[32,1024]{1,0:T(8,128)(2,1)S(1)}, bf16[32,1024]{1,0:T(8,128)(2,1)S(1)}, u32[]{:S(2)}, u32[]{:S(2)}) collective-permute-start(bf16[32,1024]{1,0:T(8,128)(2,1)S(1)} %get-tuple-element.47), channel_id=1, source_target_pairs={{0,8},{1,9},{2,10},{3,11},{4,12},{5,13},{6,14},{7,15},{8,0},{9,1},... | collective-permute-start | bytes 196616 | tf_op jit(solution)/shard_map/ppermute | solution.py:24
  24.9 31.0 %collective-permute-start.15 = (bf16[256,1024]{1,0:T(8,128)(2,1)S(1)}, bf16[256,1024]{1,0:T(8,128)(2,1)S(1)}, u32[]{:S(2)}, u32[]{:S(2)}) collective-permute-start(bf16[256,1024]{1,0:T(8,128)(2,1)S(1)} %pad_maximum_fusion.2), channel_id=1, source_target_pairs={{0,4},{1,3},{2,6},{3,1},{4,0},{5,7},{6,2},{7,5},{8,12},{9,11},{10,... | collective-permute-start | bytes 1572872 | tf_op jit(solution)/shard_map/ppermute | solution.py:24
  30.2 10.9 %collective-permute-start.3 = (bf16[64,1024]{1,0:T(8,128)(2,1)S(1)}, bf16[64,1024]{1,0:T(8,128)(2,1)S(1)}, u32[]{:S(2)}, u32[]{:S(2)}) collective-permute-start(bf16[64,1024]{1,0:T(8,128)(2,1)S(1)} %get-tuple-element.46), channel_id=1, source_target_pairs={{0,4},{1,5},{2,6},{3,7},{4,0},{5,1},{6,2},{7,3},{8,12},{9,13},{10,... | collective-permute-start | bytes 393224 | tf_op jit(solution)/shard_map/ppermute | solution.py:24
  31.3 11.1 %collective-permute-start.4 = (bf16[64,1024]{1,0:T(8,128)(2,1)S(1)}, bf16[64,1024]{1,0:T(8,128)(2,1)S(1)}, u32[]{:S(2)}, u32[]{:S(2)}) collective-permute-start(bf16[64,1024]{1,0:T(8,128)(2,1)S(1)} %get-tuple-element.46), channel_id=1, source_target_pairs={{0,6},{1,7},{2,4},{3,5},{4,2},{5,3},{6,0},{7,1},{8,14},{9,15},{10,... | collective-permute-start | bytes 393224 | tf_op jit(solution)/shard_map/ppermute | solution.py:24
  34.6 13.7 %collective-permute-start.2 = (bf16[128,1024]{1,0:T(8,128)(2,1)S(1)}, bf16[128,1024]{1,0:T(8,128)(2,1)S(1)}, u32[]{:S(2)}, u32[]{:S(2)}) collective-permute-start(bf16[128,1024]{1,0:T(8,128)(2,1)S(1)} %get-tuple-element.45), channel_id=1, source_target_pairs={{0,2},{1,3},{2,0},{3,1},{4,6},{5,7},{6,4},{7,5},{8,10},{9,11},{10,... | collective-permute-start | bytes 786440 | tf_op jit(solution)/shard_map/ppermute | solution.py:24
  36.1 9.8 %collective-permute-start.8 = (bf16[64,1024]{1,0:T(8,128)(2,1)S(1)}, bf16[64,1024]{1,0:T(8,128)(2,1)S(1)}, u32[]{:S(2)}, u32[]{:S(2)}) collective-permute-start(bf16[64,1024]{1,0:T(8,128)(2,1)S(1)} %constant_dynamic-update-slice_fusion.refs_14_.refs_21_.refs_17_.refs_24_), channel_id=1, source_target_pairs={{0,2},{1,3},{2,0},{3,1},{4,6},{5,7},{6,4},{7,5},{8,10},{9,11},{10,... | collective-permute-start | bytes 393224 | tf_op jit(solution)/shard_map/ppermute | solution.py:24
  45.9 13.2 %collective-permute-start.18 = (bf16[256,1024]{1,0:T(8,128)(2,1)S(1)}, bf16[256,1024]{1,0:T(8,128)(2,1)S(1)}, u32[]{:S(2)}, u32[]{:S(2)}) collective-permute-start(bf16[256,1024]{1,0:T(8,128)(2,1)S(1)} %dynamic-slice_bitcast_fusion), channel_id=1, source_target_pairs={{0,1},{1,0},{2,3},{3,2},{4,5},{5,4},{6,7},{7,6},{8,9},{9,8},{10,11... | collective-permute-start | bytes 1572872 | tf_op jit(solution)/shard_map/ppermute | solution.py:24
  56.9 15.0 %collective-permute-start.16 = (bf16[512,1024]{1,0:T(8,128)(2,1)S(1)}, bf16[512,1024]{1,0:T(8,128)(2,1)S(1)}, u32[]{:S(2)}, u32[]{:S(2)}) collective-permute-start(bf16[512,1024]{1,0:T(8,128)(2,1)S(1)} %pad_maximum_fusion.refs_3_), channel_id=1, source_target_pairs={{0,2},{1,5},{2,0},{3,7},{4,6},{5,1},{6,4},{7,3},{8,10},{9,13},{10,... | collective-permute-start | bytes 3145736 | tf_op jit(solution)/shard_map/ppermute | solution.py:24
  61.1 22.1 %collective-permute-start.33 = (bf16[512,1024]{1,0:T(8,128)(2,1)S(1)}, bf16[512,1024]{1,0:T(8,128)(2,1)S(1)}, u32[]{:S(2)}, u32[]{:S(2)}) collective-permute-start(bf16[512,1024]{1,0:T(8,128)(2,1)S(1)} %get-tuple-element.80), channel_id=1, source_target_pairs={{0,2},{1,5},{2,0},{3,7},{4,6},{5,1},{6,4},{7,3},{8,10},{9,13},{10,... | collective-permute-start | bytes 3145736 | tf_op jit(solution)/shard_map/ppermute | solution.py:24
  73.9 10.4 %collective-permute-start.19 = (bf16[512,512]{1,0:T(8,128)(2,1)S(1)}, bf16[512,512]{1,0:T(8,128)(2,1)S(1)}, u32[]{:S(2)}, u32[]{:S(2)}) collective-permute-start(bf16[512,512]{1,0:T(8,128)(2,1)S(1)} %get-tuple-element.53), channel_id=1, source_target_pairs={{0,1},{1,0},{2,3},{3,2},{4,5},{5,4},{6,7},{7,6},{8,9},{9,8},{10,11... | collective-permute-start | bytes 1572872 | tf_op jit(solution)/shard_map/ppermute | solution.py:24
  75.9 48.7 %collective-permute-start.17 = (bf16[256,1024]{1,0:T(8,128)(2,1)S(1)}, bf16[256,1024]{1,0:T(8,128)(2,1)S(1)}, u32[]{:S(2)}, u32[]{:S(2)}) collective-permute-start(bf16[256,1024]{1,0:T(8,128)(2,1)S(1)} %get-tuple-element.51), channel_id=1, source_target_pairs={{0,1},{1,0},{2,3},{3,2},{4,5},{5,4},{6,7},{7,6},{8,9},{9,8},{10,11... | collective-permute-start | bytes 1572872 | tf_op jit(solution)/shard_map/ppermute | solution.py:24
  83.6 23.5 %collective-permute-start.34 = (bf16[256,1024]{1,0:T(8,128)(2,1)S(1)}, bf16[256,1024]{1,0:T(8,128)(2,1)S(1)}, u32[]{:S(2)}, u32[]{:S(2)}) collective-permute-start(bf16[256,1024]{1,0:T(8,128)(2,1)S(1)} %slice.40), channel_id=1, source_target_pairs={{0,4},{1,3},{2,6},{3,1},{4,0},{5,7},{6,2},{7,5},{8,12},{9,11},{10,... | collective-permute-start | bytes 1572872 | tf_op jit(solution)/shard_map/ppermute | solution.py:24
  103.9 8.8 %collective-permute-start.30 = (bf16[64,1024]{1,0:T(8,128)(2,1)S(1)}, bf16[64,1024]{1,0:T(8,128)(2,1)S(1)}, u32[]{:S(2)}, u32[]{:S(2)}) collective-permute-start(bf16[64,1024]{1,0:T(8,128)(2,1)S(1)} %pad_maximum_fusion.9), channel_id=1, source_target_pairs={{0,6},{1,7},{2,4},{3,5},{4,2},{5,3},{6,0},{7,1},{8,14},{9,15},{10,... | collective-permute-start | bytes 393224 | tf_op jit(solution)/shard_map/ppermute | solution.py:24
  105.6 15.9 %collective-permute-start.31 = (bf16[128,1024]{1,0:T(8,128)(2,1)S(1)}, bf16[128,1024]{1,0:T(8,128)(2,1)S(1)}, u32[]{:S(2)}, u32[]{:S(2)}) collective-permute-start(bf16[128,1024]{1,0:T(8,128)(2,1)S(1)} %pad_maximum_fusion.4), channel_id=1, source_target_pairs={{0,2},{1,3},{2,0},{3,1},{4,6},{5,7},{6,4},{7,5},{8,10},{9,11},{10,... | collective-permute-start | bytes 786440 | tf_op jit(solution)/shard_map/ppermute | solution.py:24
  107.3 16.1 %collective-permute-start.35 = (bf16[128,1024]{1,0:T(8,128)(2,1)S(1)}, bf16[128,1024]{1,0:T(8,128)(2,1)S(1)}, u32[]{:S(2)}, u32[]{:S(2)}) collective-permute-start(bf16[128,1024]{1,0:T(8,128)(2,1)S(1)} %slice.42), channel_id=1, source_target_pairs={{0,8},{1,9},{2,10},{3,11},{4,12},{5,13},{6,14},{7,15},{8,0},{9,1},... | collective-permute-start | bytes 786440 | tf_op jit(solution)/shard_map/ppermute | solution.py:24
  112.7 8.3 %collective-permute-start.28 = (bf16[32,1024]{1,0:T(8,128)(2,1)S(1)}, bf16[32,1024]{1,0:T(8,128)(2,1)S(1)}, u32[]{:S(2)}, u32[]{:S(2)}) collective-permute-start(bf16[32,1024]{1,0:T(8,128)(2,1)S(1)} %slice.38), channel_id=1, source_target_pairs={{0,8},{1,9},{2,10},{3,11},{4,12},{5,13},{6,14},{7,15},{8,0},{9,1},... | collective-permute-start | bytes 196616 | tf_op jit(solution)/shard_map/ppermute | solution.py:24
  121.0 7.6 %collective-permute-start.20 = (bf16[256,512]{1,0:T(8,128)(2,1)}, bf16[256,512]{1,0:T(8,128)(2,1)S(1)}, u32[]{:S(2)}, u32[]{:S(2)}) collective-permute-start(bf16[256,512]{1,0:T(8,128)(2,1)} %get-tuple-element.56), channel_id=1, source_target_pairs={{0,1},{1,0},{2,3},{3,2},{4,5},{5,4},{6,7},{7,6},{8,9},{9,8},{10,11... | collective-permute-start | bytes 786440 | tf_op jit(solution)/shard_map/ppermute | solution.py:24
  121.0 9.0 %collective-permute-start.21 = (bf16[256,512]{1,0:T(8,128)(2,1)}, bf16[256,512]{1,0:T(8,128)(2,1)S(1)}, u32[]{:S(2)}, u32[]{:S(2)}) collective-permute-start(bf16[256,512]{1,0:T(8,128)(2,1)} %get-tuple-element.59), channel_id=1, source_target_pairs={{0,1},{1,0},{2,3},{3,2},{4,5},{5,4},{6,7},{7,6},{8,9},{9,8},{10,11... | collective-permute-start | bytes 786440 | tf_op jit(solution)/shard_map/ppermute | solution.py:24
  121.5 8.5 %collective-permute-start.22 = (bf16[256,512]{1,0:T(8,128)(2,1)}, bf16[256,512]{1,0:T(8,128)(2,1)S(1)}, u32[]{:S(2)}, u32[]{:S(2)}) collective-permute-start(bf16[256,512]{1,0:T(8,128)(2,1)} %get-tuple-element.60), channel_id=1, source_target_pairs={{0,1},{1,0},{2,3},{3,2},{4,5},{5,4},{6,7},{7,6},{8,9},{9,8},{10,11... | collective-permute-start | bytes 786440 | tf_op jit(solution)/shard_map/ppermute | solution.py:24
  124.6 9.5 %collective-permute-start.36 = (bf16[64,1024]{1,0:T(8,128)(2,1)}, bf16[64,1024]{1,0:T(8,128)(2,1)}, u32[]{:S(2)}, u32[]{:S(2)}) collective-permute-start(bf16[64,1024]{1,0:T(8,128)(2,1)} %slice.44), channel_id=1, source_target_pairs={{0,16},{1,17},{2,18},{3,19},{4,20},{5,21},{6,22},{7,23},{8,24},{9,... | collective-permute-start | bytes 393224 | tf_op jit(solution)/shard_map/ppermute | solution.py:24
  (30 other events, 277.1 us)

commit v2 on v1

v2 whole, which is shorter than its diff:
```python
import math

import jax
import jax.numpy as jnp
from jax import lax
from jax.experimental import pallas as pl
from jax.experimental.pallas import tpu as pltpu
from jax.sharding import PartitionSpec as P

HEADS = 8
HS = 128
NR = 128

HALF_ROOT = 0.7071067811865476
SCORE_SCALE = 1.0 / math.sqrt(HS)
EXP2_SCALE = SCORE_SCALE * math.log2(math.e)
F32 = jnp.float32
BF16 = jnp.bfloat16
VMEM_LIMIT = 40 * 1024 * 1024


def permute(value, masks):
    count = lax.axis_size("seq")
    return lax.ppermute(value, "seq", [(i, i ^ masks[i & 1]) for i in range(count)])


def swap(value, mask):
    return permute(value, (mask, mask))


def after(value, *others):
    return lax.optimization_barrier((value, *others))[0]


def call(body, meta, operands, specs, shapes, out_specs, scratch=(), grid=(1,)):
    return pl.pallas_call(
        body,
        grid_spec=pltpu.PrefetchScalarGridSpec(
            num_scalar_prefetch=1,
            grid=grid,
            in_specs=specs,
            out_specs=out_specs,
            scratch_shapes=list(scratch),
        ),
        out_shape=shapes,
        compiler_params=pltpu.CompilerParams(vmem_limit_bytes=VMEM_LIMIT),
        cost_estimate=pl.CostEstimate(flops=0, bytes_accessed=0, transcendentals=0),
    )(meta, *operands)


def whole(array):
    return pl.BlockSpec(array.shape, lambda i, m: (0,) * len(array.shape))


def own_half(array):
    return pl.BlockSpec((array.shape[0], array.shape[1] // 2), lambda i, m: (0, m[0]))


def struct(rows, cols, dtype):
    return jax.ShapeDtypeStruct((rows, cols), dtype)


def planes(rows, cols, dtype):
    return jax.ShapeDtypeStruct((2, rows, cols), dtype)


def dot(a, b, dims):
    return lax.dot_general(a, b, (dims, ((), ())), preferred_element_type=F32)


NN = ((1,), (0,))
NT = ((1,), (1,))
TN = ((0,), (0,))


def group_matrix(rows, cols, row_div, col_div):
    row = lax.broadcasted_iota(jnp.int32, (rows, cols), 0) // row_div
    col = lax.broadcasted_iota(jnp.int32, (rows, cols), 1) // col_div
    return jnp.where(row == col, 1.0, 0.0).astype(BF16)


def pool(rows):
    half = rows.shape[0] // 2
    return (dot(group_matrix(half, 2 * half, 1, 2), rows, NN) * HALF_ROOT).astype(BF16)


def spread(grad, times, factor):
    high = grad.astype(BF16)
    low = (grad - high.astype(F32)).astype(BF16)
    matrix = group_matrix(times * grad.shape[0], grad.shape[0], times, 1)
    return (dot(matrix, high, NN) + dot(matrix, low, NN)) * factor


def lanes(ref):
    return jnp.concatenate([ref[0], ref[1]], axis=1)


def put_planes(ref, rows):
    width = ref.shape[2]
    ref[0] = rows[:, :width].astype(ref.dtype)
    ref[1] = rows[:, width:].astype(ref.dtype)


def pool_body(meta, keys, values, other, *outs):
    own = jnp.concatenate([keys[...], values[...]], axis=1)
    first_own = pool(own)
    first_other = pool(lanes(other))
    put_planes(outs[0], first_own)
    put_planes(outs[1], first_other)
    rows = jnp.concatenate([pool(first_own), pool(first_other)], axis=0)
    put_planes(outs[2], rows)
    for out in outs[3:]:
        rows = pool(rows)
        put_planes(out, rows)


def key_sets(k_own, v_own, kv_other, next_own, next_other, far, at):
    far_rows = [[ref[plane, start : start + rows, at] for ref, start, rows in far] for plane in range(2)]
    near = ((k_own[:, at], kv_other[0, :, at]), (v_own[:, at], kv_other[1, :, at]))
    coarse = (next_other, next_own)
    return [
        [
            jnp.concatenate([near[plane][group], coarse[group][plane, :, at]] + far_rows[plane], axis=0)
            for group in range(2)
        ]
        for plane in range(2)
    ]


def forward_body(heads, parts, meta, q_own, q_other, k_own, v_own, kv_other, next_own, next_other, *refs):
    n_far = len(refs) - 2
    attn_ref, probs_ref = refs[n_far:]
    far = [(refs[index], start, rows) for index, start, rows in parts]
    for head in range(heads):
        at = slice(head * HS, (head + 1) * HS)
        keys, values = key_sets(k_own, v_own, kv_other, next_own, next_other, far, at)
        for group, q_ref in enumerate((q_own, q_other)):
            length = q_ref.shape[0]
            scores = dot(keys[group], q_ref[:, at], NT)
            top = jnp.max(scores, axis=0, keepdims=True)
            weights = jnp.exp2((scores - top) * EXP2_SCALE)
            total = jnp.sum(weights, axis=0, keepdims=True)
            probs = (weights * (1.0 / total)).astype(BF16)
            probs_ref[2 * head + group] = probs
            attn = dot(values[group], probs, TN)
            attn_ref[at, group * length : (group + 1) * length] = attn.astype(BF16)


def backward_body(
    heads, parts, n_far, meta, q_own, q_other, k_own, v_own, kv_other, next_own, next_other, *refs
):
    far = [(refs[index], start, rows) for index, start, rows in parts]
    d_keep, d_recv, probs_ref, dq_own, dq_other, near_own, near_other = refs[n_far : n_far + 7]
    far_grads = refs[n_far + 7 :]
    near_rows = k_own.shape[0]
    after_next = near_rows + next_own.shape[1]
    for head in range(heads):
        at = slice(head * HS, (head + 1) * HS)
        keys, values = key_sets(k_own, v_own, kv_other, next_own, next_other, far, at)
        grads = ([], [])
        for group, (q_ref, dq_ref) in enumerate(((q_own, dq_own), (q_other, dq_other))):
            length = q_ref.shape[0]
            rows = slice(group * length, (group + 1) * length)
            d_attn = (d_keep[rows, at] + d_recv[rows, at].astype(F32)).astype(BF16)
            probs_low = probs_ref[2 * head + group]
            probs = probs_low.astype(F32)
            d_prob = dot(values[group], d_attn, NT)
            center = jnp.sum(probs * d_prob, axis=0, keepdims=True)
            d_score = (probs * (d_prob - center)).astype(BF16)
            dq = dot(keys[group], d_score, TN) * SCORE_SCALE
            dq_ref[:, at] = dq.T.astype(BF16)
            grads[0].append(dot(d_score, q_ref[:, at], NN) * SCORE_SCALE)
            grads[1].append(dot(probs_low, d_attn, NN))
        for plane in range(2):
            for group, near in enumerate((near_own, near_other)):
                total = grads[plane][group][:near_rows]
                total = total + spread(grads[plane][1 - group][near_rows:after_next], 2, HALF_ROOT)
                near[plane, :, at] = total.astype(near.dtype)
            total = grads[plane][0][after_next:] + grads[plane][1][after_next:]
            done = 0
            for index, start, rows in parts:
                out = far_grads[index]
                out[plane, start : start + rows, at] = total[done : done + rows].astype(BF16)
                done += rows


def pieces_of(quarters, piece):
    return [(quarter, start) for quarter in quarters for start in range(0, quarter.shape[0], piece)]


def rows_of_piece(meta, masks, index, piece):
    owner = meta[1] ^ jnp.where(meta[0] == 0, masks[0][index], masks[1][index])
    return pl.ds(pl.multiple_of(owner * piece, piece), piece)


def ordered_weight(meta, quarters, scratch, piece, masks):
    for index, (quarter, start) in enumerate(pieces_of(quarters, piece)):
        scratch[rows_of_piece(meta, masks, index, piece), :] = quarter[start : start + piece, :]


def half_rows_of(meta, scratch, mine):
    width = scratch.shape[0] // 2
    start = meta[0] * width if mine else (1 - meta[0]) * width
    return pl.ds(pl.multiple_of(start, width), width)


def d_attn_body(piece, masks, meta, grad_own, grad_other, *refs):
    keep, send, scratch = refs[-3:]
    ordered_weight(meta, refs[:-3], scratch, piece, masks)
    length = grad_own.shape[0]
    mine = scratch[half_rows_of(meta, scratch, True), :]
    theirs = scratch[half_rows_of(meta, scratch, False), :]
    send[:length] = dot(grad_other[...], theirs, NT).astype(BF16)
    send[length:] = dot(grad_own[...], theirs, NT).astype(BF16)
    keep[:length] = dot(grad_own[...], mine, NT)
    keep[length:] = dot(grad_other[...], mine, NT)


def attended_body(piece, masks, meta, attn_mine, attn_theirs, *refs):
    keep, send, scratch = refs[-3:]
    ordered_weight(meta, refs[:-3], scratch, piece, masks)
    length = keep.shape[0]
    mine = scratch[half_rows_of(meta, scratch, True), :]
    theirs = scratch[half_rows_of(meta, scratch, False), :]
    send[...] = (
        dot(attn_mine[:, length:], mine, TN) + dot(attn_theirs[:, :length], theirs, TN)
    ).astype(BF16)
    keep[...] = (
        dot(attn_mine[:, :length], mine, TN) + dot(attn_theirs[:, length:], theirs, TN)
    ).astype(BF16)


def weight_grad_body(piece, masks, meta, attn_mine, attn_theirs, grad_own, grad_other, *refs):
    scratch = refs[-1]
    length = grad_own.shape[0]
    mine = dot(attn_mine[:, :length], grad_own[...], NN) + dot(
        attn_mine[:, length:], grad_other[...], NN
    )
    scratch[half_rows_of(meta, scratch, True), :] = mine.astype(BF16)
    theirs = dot(attn_theirs[:, length:], grad_own[...], NN) + dot(
        attn_theirs[:, :length], grad_other[...], NN
    )
    scratch[half_rows_of(meta, scratch, False), :] = theirs.astype(BF16)
    for index, (quarter, start) in enumerate(pieces_of(refs[:-1], piece)):
        quarter[start : start + piece, :] = scratch[rows_of_piece(meta, masks, index, piece), :]


def high_body(cuts, skips, meta, own, *refs):
    received = refs[: len(skips)]
    for plane in range(2):
        total = own[plane].astype(F32)
        for ref, skip in zip(received, skips, strict=True):
            total = total + ref[plane, skip:].astype(F32)
        start = 0
        for out, rows in zip(refs[len(skips) :], cuts, strict=True):
            out[plane] = total[start : start + rows].astype(BF16)
            start += rows


def cascade_body(counts, meta, *refs):
    keep, send = refs[-2:]
    half = keep.shape[1]
    total = None
    start = 0
    rows = 2 * half >> (len(counts) - 1)
    for count in counts:
        level = lanes(refs[start])[:rows].astype(F32)
        for ref in refs[start + 1 : start + count]:
            level = level + lanes(ref)[:rows].astype(F32)
        start += count
        rows *= 2
        total = level if total is None else level + spread(total, 2, HALF_ROOT)
    put_planes(keep, total[:half])
    put_planes(send, total[half:])


def finish_body(meta, near_keep, near_recv, up_keep, up_recv, dk, dv):
    width = near_keep.shape[2]
    times = near_keep.shape[1] // up_keep.shape[1]
    factor = HALF_ROOT * HALF_ROOT
    matrix = group_matrix(dk.shape[0], up_recv.shape[1], times, 1)
    mine = pl.ds(pl.multiple_of(meta[0] * width, width), width)
    theirs = pl.ds(pl.multiple_of((1 - meta[0]) * width, width), width)
    for plane, out in enumerate((dk, dv)):
        out[:, mine] = (near_keep[plane] + spread(up_keep[plane], times, factor)).astype(BF16)
        received = dot(matrix, up_recv[plane], NN) * factor
        out[:, theirs] = (near_recv[plane].astype(F32) + received).astype(BF16)


def place_body(meta, keep, received, out):
    @pl.when(pl.program_id(0) == 0)
    def _():
        out[...] = keep[...]

    @pl.when(pl.program_id(0) == 1)
    def _():
        out[...] = received[...]


def place_halves(meta, keep, received):
    rows, cols = keep.shape
    return call(
        place_body,
        meta,
        (keep, received),
        [whole(keep), whole(received)],
        struct(rows, 2 * cols, keep.dtype),
        pl.BlockSpec((rows, cols), lambda i, m: (0, (m[0] + i) % 2)),
        grid=(2,),
    )


def other_half(array, bit):
    width = array.shape[1] // 2
    return lax.dynamic_slice_in_dim(array, (1 - bit) * width, width, 1)


def body(queries, keys, values, out_weight, out_grad):
    inner = queries.shape[2]
    half = inner // 2
    length = queries.shape[1]
    heads = HEADS // 2
    seq_count = lax.axis_size("seq")
    seq_levels = seq_count.bit_length() - 1
    dp_count = lax.axis_size("dp")
    rank = lax.axis_index("seq")
    bit = rank % 2
    pair = rank // 2
    token_total = length * seq_count * queries.shape[0] * dp_count

    up = [1 << level for level in reversed(range(1, seq_levels))]
    orders = (up[:-2] + [2, 4], [2] + up[:-3] + [4, 8])
    stages = list(zip(*orders, strict=True))
    pieces = seq_count // 2
    masks = [
        [sum(m for s, m in enumerate(order) if index >> s & 1) // 2 for index in range(pieces)]
        for order in orders
    ]
    meta = jnp.stack([bit, pair]).astype(jnp.int32)

    query = queries[0]
    key = keys[0]
    value = values[0]
    grad = out_grad[0]
    if dp_count > 1:
        out_weight = lax.all_gather(out_weight, "dp", axis=1, tiled=True)
    cols = out_weight.shape[1] // 2
    piece = 2 * out_weight.shape[0]

    kv_other = swap(jnp.stack([other_half(key, bit), other_half(value, bit)]), 1)
    w_mine = lax.dynamic_slice_in_dim(out_weight, bit * cols, cols, 1)
    w_theirs = swap(other_half(out_weight, bit), 1)

    sizes = [length // 2, length // 2] + [2 * length >> level for level in range(2, seq_levels + 1)]
    shapes = [planes(rows, half, BF16) for rows in sizes]
    pooled = call(
        pool_body,
        meta,
        (key, value, kv_other),
        [own_half(key), own_half(value), whole(kv_other)],
        shapes,
        [whole(s) for s in shapes],
    )
    next_own, next_other = pooled[:2]
    coarse = dict(zip(range(1, seq_levels), pooled[2:], strict=True))

    w_rows = jnp.where(
        bit == 0,
        jnp.concatenate([w_mine, w_theirs], axis=0),
        jnp.concatenate([w_theirs, w_mine], axis=0),
    )
    w_received = permute(w_rows, stages[0])
    far_masks = [(h, (1 << h) + (low << 3)) for h in range(3, seq_levels) for low in range(1 << (h - 3))]
    high_parts = [swap(coarse[h], mask) for h, mask in far_masks]
    first_panel = swap(coarse[1], 2)
    w_received, *high_parts = lax.optimization_barrier((w_received, *high_parts))

    high = jnp.concatenate(high_parts, axis=1)
    second = jnp.concatenate([coarse[2], high], axis=1)
    panels = [high, first_panel, swap(high, 2), swap(second, 4), swap(second, 6)]
    for stage in stages[1:-2]:
        w_rows = jnp.concatenate([w_rows, w_received], axis=0)
        w_received = permute(w_rows, stage)
    q_other = swap(after(other_half(query, bit), high), 1)
    g_other = swap(after(other_half(grad, bit), high), 1)
    n_high, n_second = high.shape[1], coarse[2].shape[1]
    parts = ((1, 0, coarse[1].shape[1]), (3, 0, n_second), (4, 0, n_second))
    parts += ((0, 0, n_high), (2, 0, n_high), (3, n_second, n_high), (4, n_second, n_high))

    w_rows = jnp.concatenate([w_rows, after(w_received, *panels)], axis=0)
    w_received = permute(w_rows, stages[-2])
    w_last = permute(w_rows, stages[-1])

    per_step = 2
    steps = heads // per_step
    width = per_step * HS

    def of_own(array):
        return pl.BlockSpec((array.shape[0], width), lambda i, m: (0, m[0] * steps + i))

    def left(array):
        return pl.BlockSpec((array.shape[0], width), lambda i, m: (0, i))

    def both(array):
        return pl.BlockSpec((2, array.shape[1], width), lambda i, m: (0, 0, i))

    key_count = length + length // 2 + sum(rows for _, _, rows in parts)
    plane_ops = (kv_other, next_own, next_other, *panels)
    att_ops = (query, q_other, key, value, *plane_ops)
    att_specs = [of_own(query), left(q_other), of_own(key), of_own(value)] + [both(a) for a in plane_ops]
    probs_shape = jax.ShapeDtypeStruct((2 * heads, key_count, length), BF16)
    probs_spec = pl.BlockSpec((2 * per_step, key_count, length), lambda i, m: (i, 0, 0))
    attn_mine, probs = call(
        lambda *refs: forward_body(per_step, parts, *refs),
        after(meta, w_rows),
        att_ops,
        att_specs,
        [struct(half, 2 * length, BF16), probs_shape],
        [pl.BlockSpec((width, 2 * length), lambda i, m: (i, 0)), probs_spec],
        grid=(steps,),
    )

    w_received = after(w_received, attn_mine)
    quarters = (w_rows, w_received, w_last, permute(w_received, stages[-1]))
    attn_theirs = swap(attn_mine, 1)

    scratch = [pltpu.VMEM((pieces * piece, cols), BF16)]
    g_spec = [own_half(grad), whole(g_other)]
    wg_shapes = [struct(pieces * piece // 4, cols, BF16)] * 4
    wg = call(
        lambda *refs: weight_grad_body(piece, masks, *refs),
        meta,
        (attn_mine, attn_theirs, grad, g_other),
        [whole(attn_mine), whole(attn_theirs)] + g_spec,
        wg_shapes,
        [whole(s) for s in wg_shapes],
        scratch,
    )
    wg_received = [permute(after(part, quarters[3]), stages[-1]) for part in (wg[3], wg[2])]

    w_spec = [whole(quarter) for quarter in quarters]
    d_shapes = [struct(2 * length, half, F32), struct(2 * length, half, BF16)]
    d_keep, d_send = call(
        lambda *refs: d_attn_body(piece, masks, *refs),
        after(meta, wg[0]),
        (grad, g_other, *quarters),
        g_spec + w_spec,
        d_shapes,
        [whole(s) for s in d_shapes],
        scratch,
    )
    d_recv = swap(d_send, 1)

    out_shapes = [struct(length, half, BF16)] * 2
    out_specs = [left(s) for s in out_shapes]
    plane_shapes = [planes(length, half, F32), planes(length, half, BF16)]
    plane_shapes += [planes(p.shape[1], half, BF16) for p in panels[:1]]
    plane_shapes += [planes(p.shape[1], half, BF16) for p in panels[1:]]
    grads = call(
        lambda *refs: backward_body(per_step, parts, len(panels), *refs),
        meta,
        att_ops + (d_keep, d_recv, probs),
        att_specs + [left(d_keep), left(d_recv), probs_spec],
        out_shapes + plane_shapes,
        out_specs + [both(s) for s in plane_shapes],
        grid=(steps,),
    )
    dq_keep, dq_send, near_keep, near_send, high_own, first_grad, *rest = grads

    def add(kept, received):
        return (kept.astype(F32) + received.astype(F32)).astype(BF16)

    wg_send = add(wg[1], after(wg_received[0], dq_keep))
    wg_keep = add(wg[0], after(wg_received[1], dq_keep))
    wg_received = permute(wg_send, stages[-2])

    first_back = swap(first_grad, 2)
    back = [swap(part, mask) for part, mask in zip(rest, (2, 4, 6), strict=True)]
    cuts = [coarse[h].shape[1] for h, _ in far_masks]
    high_shapes = [planes(rows, half, BF16) for rows in cuts]
    high_sums = call(
        lambda *refs: high_body(cuts, (0, n_second, n_second), *refs),
        meta,
        (high_own, *back),
        [whole(high_own)] + [whole(b) for b in back],
        high_shapes,
        [whole(s) for s in high_shapes],
    )
    by_level = {1: [first_back], 2: back[1:]}
    for (h, mask), part in zip(far_masks, high_sums, strict=True):
        by_level.setdefault(h, []).append(swap(part, mask))
    near_recv = swap(after(near_send, first_grad), 1)
    dq_recv = swap(after(dq_send, first_grad), 1)
    grad_queries = place_halves(meta, dq_keep, dq_recv)

    at_shape = struct(length, cols, BF16)
    at_keep, at_send = call(
        lambda *refs: attended_body(piece, masks, *refs),
        after(meta, first_grad),
        (attn_mine, attn_theirs, *quarters),
        [whole(attn_mine), whole(attn_theirs)] + w_spec,
        [at_shape, at_shape],
        [whole(at_shape), whole(at_shape)],
        scratch,
    )
    attended = place_halves(meta, at_keep, swap(at_send, 1))

    for stage in reversed(stages[:-2]):
        total = add(wg_keep, wg_received)
        rows = total.shape[0] // 2
        wg_keep, wg_send = total[:rows], total[rows:]
        wg_received = permute(wg_send, stage)
    total = wg_keep.astype(F32) + wg_received.astype(F32)
    rows = piece // 2
    wg_mine = lax.dynamic_slice_in_dim(total, bit * rows, rows, 0)
    wg_theirs = swap(lax.dynamic_slice_in_dim(total, (1 - bit) * rows, rows, 0).astype(BF16), 1)
    wg_theirs = wg_theirs.astype(F32)
    weight_grad = jnp.where(
        bit == 0,
        jnp.concatenate([wg_mine, wg_theirs], axis=1),
        jnp.concatenate([wg_theirs, wg_mine], axis=1),
    )
    if dp_count > 1:
        weight_grad = lax.psum_scatter(
            weight_grad.astype(BF16), "dp", scatter_dimension=1, tiled=True
        ).astype(F32)
    weight_grad = weight_grad * (1.0 / math.sqrt(token_total))

    levels = list(reversed(range(1, seq_levels)))
    received = [part for h in levels for part in by_level[h]]
    counts = [len(by_level[h]) for h in levels]
    up_rows = coarse[1].shape[1] // 2
    up_shapes = [planes(up_rows, half, F32), planes(up_rows, half, BF16)]
    up_keep, up_send = call(
        lambda *refs: cascade_body(counts, *refs),
        meta,
        received,
        [whole(r) for r in received],
        up_shapes,
        [whole(s) for s in up_shapes],
    )
    fin_ops = (near_keep, near_recv, up_keep, swap(up_send, 1))
    fin_shape = struct(length, inner, BF16)
    grad_keys, grad_values = call(
        finish_body,
        meta,
        fin_ops,
        [whole(o) for o in fin_ops],
        [fin_shape, fin_shape],
        [whole(fin_shape), whole(fin_shape)],
    )
    return (attended[None], grad_queries[None], grad_keys[None], grad_values[None], weight_grad)


def solution(mesh):
    placed = (
        P("dp", "seq", None),
        P("dp", "seq", None),
        P("dp", "seq", None),
        P("seq", "dp"),
        P("dp", "seq", None),
    )
    return jax.shard_map(
        body,
        mesh=mesh,
        in_specs=placed,
        out_specs=(
            P("dp", "seq", None),
            P("dp", "seq", None),
            P("dp", "seq", None),
            P("dp", "seq", None),
            P("seq", "dp"),
        ),
        check_vma=False,
    )
```

time: 137 us -> 120 us (0.88)
  starting transfers between devices: 46.1 us -> 33.8 us
  other arithmetic: 6.35 us -> 2.4 us
  waiting for transfers between devices: 47.8 us -> 44.9 us
  local copies, waits for them, and re-layouts: 3.74 us -> 5.69 us
    ppermute x38 -> x35, starting transfers between devices: 46.1 us -> 33.8 us  [permute(): lax.ppermute(value, 'seq', [(i, i ^ masks[i & 1]) for i in range(count)])]
    concatenate x11 -> x2, other arithmetic: 3.91 us -> 0.05 us  [the longest x1 0.03 us: body(): w_rows = jnp.concatenate([w_rows, after(w_received, *panels)], axis=0)]
    ppermute x38 -> x35, waiting for transfers between devices: 47.8 us -> 44.9 us  [permute(): lax.ppermute(value, 'seq', [(i, i ^ masks[i & 1]) for i in range(count)])]
    unnamed x34 -> x19, local copies, waits for them, and re-layouts: 0.1 us -> 2.83 us
    pallas_call x10 -> x11, Pallas kernels: 32 us -> 32.3 us  [call(): pl.pallas_call(body, grid_spec=pltpu.PrefetchScalarGridSpec(num_scalar_pr...]
  transfers between devices with their start and end apart: 38 -> 35, of which waited for: 16 -> 16; matrix products, arithmetic and copies ran while one was open for 5% -> 2% of each run, Pallas kernels for 23% -> 25%
where the time goes in v2:
time: 120 us
  waiting for transfers between devices  44.9 us (37%)
  starting transfers between devices  33.8 us (28%)
  Pallas kernels  32.3 us (27%)
  local copies, waits for them, and re-layouts  5.69 us (5%)
  other arithmetic  2.4 us (2%)
    ppermute x35, waiting for transfers between devices, permute(): lax.ppermute(value, 'seq', [(i, i ^ masks[i & 1]) for i in range(count)])  44.9 us
    ppermute x35, starting transfers between devices, permute(): lax.ppermute(value, 'seq', [(i, i ^ masks[i & 1]) for i in range(count)])  33.8 us
    pallas_call x11, Pallas kernels, call(): pl.pallas_call(body, grid_spec=pltpu.PrefetchScalarGridSpec(num_scalar_pr...  32.3 us
    unnamed x19, local copies, waits for them, and re-layouts  2.83 us
  transfers between devices with their start and end apart: 35, of which 16 were waited for; matrix products, arithmetic and copies ran while one was open for 2% of the time, Pallas kernels for 25%

profile of v2, /device:TPU:0, one launch (start us, length us, event | category | flops | bytes accessed | tf_op | source)
XLA Modules:
  0.0 120.0 jit_solution(13368681658064007849)
XLA Ops:
  4.7 3.8 %collective-permute-start.1 = (bf16[64,1024]{1,0:T(8,128)(2,1)S(1)}, bf16[64,1024]{1,0:T(8,128)(2,1)S(1)}, u32[]{:S(2)}, u32[]{:S(2)}) collective-permute-start(bf16[64,1024]{1,0:T(8,128)(2,1)S(1)} %maximum_select_fusion.1), channel_id=1, source_target_pairs={{0,16},{1,3},{2,18},{3,1},{4,20},{5,7},{6,22},{7,5},{8,24},{9,11},... | collective-permute-start | bytes 393224 | tf_op jit(solution)/shard_map/ppermute | solution.py:24
  13.4 1.7 %collective-permute-start.4 = (bf16[2,16,512]{2,1,0:T(8,128)(2,1)S(1)}, bf16[2,16,512]{2,1,0:T(8,128)(2,1)S(1)}, u32[]{:S(2)}, u32[]{:S(2)}) collective-permute-start(bf16[2,16,512]{2,1,0:T(8,128)(2,1)S(1)} %get-tuple-element.55), channel_id=1, source_target_pairs={{0,16},{1,17},{2,18},{3,19},{4,20},{5,21},{6,22},{7,23},{8,24},{9,... | collective-permute-start | bytes 98312 | tf_op jit(solution)/shard_map/ppermute | solution.py:24
  19.6 2.3 %collective-permute-start.10 = (bf16[2,128,512]{2,1,0:T(8,128)(2,1)S(1)}, bf16[2,128,512]{2,1,0:T(8,128)(2,1)S(1)}, u32[]{:S(2)}, u32[]{:S(2)}) collective-permute-start(bf16[2,128,512]{2,1,0:T(8,128)(2,1)S(1)} %get-tuple-element.107), channel_id=1, source_target_pairs={{0,6},{1,7},{2,4},{3,5},{4,2},{5,3},{6,0},{7,1},{8,14},{9,15},{10,... | collective-permute-start | bytes 786440 | tf_op jit(solution)/shard_map/ppermute | solution.py:24
  24.4 7.0 %collective-permute-done.8.refs_10_ = bf16[2,64,512]{2,1,0:T(8,128)(2,1)S(1)} collective-permute-done((bf16[2,64,512]{2,1,0:T(8,128)(2,1)S(1)}, bf16[2,64,512]{2,1,0:T(8,128)(2,1)S(1)}, u32[]{:S(2)}, u32[]{:S(2)}) %collective-permute-start.8) | collective-permute-done | bytes 131104 | tf_op jit(solution)/shard_map/ppermute | solution.py:24
  31.4 2.1 %collective-permute-done.9.refs_11_ = bf16[2,128,512]{2,1,0:T(8,128)(2,1)S(1)} collective-permute-done((bf16[2,128,512]{2,1,0:T(8,128)(2,1)S(1)}, bf16[2,128,512]{2,1,0:T(8,128)(2,1)S(1)}, u32[]{:S(2)}, u32[]{:S(2)}) %collective-permute-start.9) | collective-permute-done | bytes 262176 | tf_op jit(solution)/shard_map/ppermute | solution.py:24
  36.6 7.1 %shard_map.93 = (bf16[512,512]{1,0:T(8,128)(2,1)S(1)}, bf16[8,896,256]{2,1,0:T(8,128)(2,1)S(1)}) custom-call(s32[2]{0:T(128)S(1)} %pad_add_fusion.meta.refs_0_, bf16[256,1024]{1,0:T(8,128)(2,1)S(1)} %bitcast.22, bf16[256,512]{1,0:T(8,128)(2,1)S(1)} %collective-permute-done.6.refs_2_, bf16[256,1024]{1,0:T(8,128)(2,1)S(1)} %bitcast.17, ...), custom_call_target="tpu_custom_call" | custom-call | tf_op jit(solution)/shard_map/pallas_call | solution.py:36
  46.0 1.9 %shard_map.94 = (bf16[256,1024]{1,0:T(8,128)(2,1)S(1)}, bf16[256,1024]{1,0:T(8,128)(2,1)S(1)}, bf16[256,1024]{1,0:T(8,128)(2,1)S(1)}, bf16[256,1024]{1,0:T(8,128)(2,1)S(1)}) custom-call(s32[2]{0:T(128)S(1)} %pad_add_fusion.meta.refs_0_, bf16[512,512]{1,0:T(8,128)(2,1)S(1)} %get-tuple-element.67.refs_1_, ...), custom_call_target="tpu_custom_call" | custom-call | tf_op jit(solution)/shard_map/pallas_call | solution.py:36
  47.9 5.2 %collective-permute-done.15.refs_5_ = bf16[256,1024]{1,0:T(8,128)(2,1)S(1)} collective-permute-done((bf16[256,1024]{1,0:T(8,128)(2,1)S(1)}, bf16[256,1024]{1,0:T(8,128)(2,1)S(1)}, u32[]{:S(2)}, u32[]{:S(2)}) %collective-permute-start.15) | collective-permute-done | bytes 524320 | tf_op jit(solution)/shard_map/ppermute | solution.py:24
  53.1 5.6 %collective-permute-done.16.refs_6_ = bf16[256,1024]{1,0:T(8,128)(2,1)S(1)} collective-permute-done((bf16[256,1024]{1,0:T(8,128)(2,1)S(1)}, bf16[256,1024]{1,0:T(8,128)(2,1)S(1)}, u32[]{:S(2)}, u32[]{:S(2)}) %collective-permute-start.16) | collective-permute-done | bytes 524320 | tf_op jit(solution)/shard_map/ppermute | solution.py:24
  58.7 2.0 %shard_map.95 = (f32[512,512]{1,0:T(8,128)S(1)}, bf16[512,512]{1,0:T(8,128)(2,1)S(1)}) custom-call(s32[2]{0:T(128)S(1)} %pad_add_fusion.meta.refs_0_, bf16[256,2048]{1,0:T(8,128)(2,1)S(1)} %bitcast.15, bf16[256,1024]{1,0:T(8,128)(2,1)S(1)} %collective-permute-done.13.refs_4_.refs_2_, bf16[256,1024]{1,0:T(8,128)(2,1)S(1)} %pad_maximum_fusion.1.refs_3_, ...), custom_call_target="tpu_custom_call" | custom-call | tf_op jit(solution)/shard_map/pallas_call | solution.py:36
  62.9 10.2 %shard_map.96 = (bf16[256,512]{1,0:T(8,128)(2,1)S(1)}, bf16[256,512]{1,0:T(8,128)(2,1)}, f32[2,256,512]{2,1,0:T(8,128)S(1)}, bf16[2,256,512]{2,1,0:T(8,128)(2,1)...) custom-call(s32[2]{0:T(128)S(1)} %pad_add_fusion.meta.refs_0_, ...), custom_call_target="tpu_custom_call" | custom-call | tf_op jit(solution)/shard_map/pallas_call | solution.py:36
  74.1 1.6 %collective-permute-done.29 = bf16[256,1024]{1,0:T(8,128)(2,1)S(1)} collective-permute-done((bf16[256,1024]{1,0:T(8,128)(2,1)S(1)}, bf16[256,1024]{1,0:T(8,128)(2,1)S(1)}, u32[]{:S(2)}, u32[]{:S(2)}) %collective-permute-start.29) | collective-permute-done | bytes 524320 | tf_op jit(solution)/shard_map/ppermute | solution.py:24
  77.3 1.8 %collective-permute-start.23 = (bf16[2,128,512]{2,1,0:T(8,128)(2,1)S(1)}, bf16[2,128,512]{2,1,0:T(8,128)(2,1)S(1)}, u32[]{:S(2)}, u32[]{:S(2)}) collective-permute-start(bf16[2,128,512]{2,1,0:T(8,128)(2,1)S(1)} %get-tuple-element.88), channel_id=1, source_target_pairs={{0,6},{1,7},{2,4},{3,5},{4,2},{5,3},{6,0},{7,1},{8,14},{9,15},{10,... | collective-permute-start | bytes 786440 | tf_op jit(solution)/shard_map/ppermute | solution.py:24
  79.9 7.4 %collective-permute-done.31 = bf16[256,1024]{1,0:T(8,128)(2,1)S(1)} collective-permute-done((bf16[256,1024]{1,0:T(8,128)(2,1)S(1)}, bf16[256,1024]{1,0:T(8,128)(2,1)S(1)}, u32[]{:S(2)}, u32[]{:S(2)}) %collective-permute-start.31) | collective-permute-done | bytes 524320 | tf_op jit(solution)/shard_map/ppermute | solution.py:24
  87.7 2.2 %shard_map.97 = (bf16[256,1024]{1,0:T(8,128)(2,1)S(1)}, bf16[256,1024]{1,0:T(8,128)(2,1)}) custom-call(s32[2]{0:T(128)S(1)} %pad_add_fusion.meta.refs_0_, bf16[512,512]{1,0:T(8,128)(2,1)S(1)} %get-tuple-element.67.refs_1_, bf16[512,512]{1,0:T(8,128)(2,1)S(1)} %collective-permute-done.12.refs_2_, bf16[256,1024]{1,0:T(8,128)(2,1)S(1)} %pad_maximum_fusion.1.refs_3_, ...), custom_call_target="tpu_custom_call" | custom-call | tf_op jit(solution)/shard_map/pallas_call | solution.py:36
  90.6 3.5 %collective-permute-done.23.refs_4_.refs_5_ = bf16[2,128,512]{2,1,0:T(8,128)(2,1)S(1)} collective-permute-done((bf16[2,128,512]{2,1,0:T(8,128)(2,1)S(1)}, bf16[2,128,512]{2,1,0:T(8,128)(2,1)S(1)}, u32[]{:S(2)}, u32[]{:S(2)}) %collective-permute-start.23) | collective-permute-done | bytes 262176 | tf_op jit(solution)/shard_map/ppermute | solution.py:24
  94.7 1.9 %collective-permute-start.24 = (bf16[2,16,512]{2,1,0:T(8,128)(2,1)S(1)}, bf16[2,16,512]{2,1,0:T(8,128)(2,1)S(1)}, u32[]{:S(2)}, u32[]{:S(2)}) collective-permute-start(bf16[2,16,512]{2,1,0:T(8,128)(2,1)S(1)} %get-tuple-element.89), channel_id=1, source_target_pairs={{0,16},{1,17},{2,18},{3,19},{4,20},{5,21},{6,22},{7,23},{8,24},{9,... | collective-permute-start | bytes 98312 | tf_op jit(solution)/shard_map/ppermute | solution.py:24
  97.9 2.0 %collective-permute-done.24.refs_1_ = bf16[2,16,512]{2,1,0:T(8,128)(2,1)S(1)} collective-permute-done((bf16[2,16,512]{2,1,0:T(8,128)(2,1)S(1)}, bf16[2,16,512]{2,1,0:T(8,128)(2,1)S(1)}, u32[]{:S(2)}, u32[]{:S(2)}) %collective-permute-start.24) | collective-permute-done | bytes 32800 | tf_op jit(solution)/shard_map/ppermute | solution.py:24
  99.9 2.9 %collective-permute-start.25 = (bf16[2,16,512]{2,1,0:T(8,128)(2,1)S(1)}, bf16[2,16,512]{2,1,0:T(8,128)(2,1)S(1)}, u32[]{:S(2)}, u32[]{:S(2)}) collective-permute-start(bf16[2,16,512]{2,1,0:T(8,128)(2,1)S(1)} %get-tuple-element.90), channel_id=1, source_target_pairs={{0,24},{1,25},{2,26},{3,27},{4,28},{5,29},{6,30},{7,31},{8,16},{9,... | collective-permute-start | bytes 98312 | tf_op jit(solution)/shard_map/ppermute | solution.py:24
  102.8 2.8 %collective-permute-done.25.refs_2_ = bf16[2,16,512]{2,1,0:T(8,128)(2,1)S(1)} collective-permute-done((bf16[2,16,512]{2,1,0:T(8,128)(2,1)S(1)}, bf16[2,16,512]{2,1,0:T(8,128)(2,1)S(1)}, u32[]{:S(2)}, u32[]{:S(2)}) %collective-permute-start.25) | collective-permute-done | bytes 32800 | tf_op jit(solution)/shard_map/ppermute | solution.py:24
  105.6 1.8 %shard_map.101 = (f32[2,64,512]{2,1,0:T(8,128)S(1)}, bf16[2,64,512]{2,1,0:T(8,128)(2,1)}) custom-call(s32[2]{0:T(128)S(1)} %pad_add_fusion.meta.refs_0_, bf16[2,16,512]{2,1,0:T(8,128)(2,1)S(1)} %collective-permute-done.24.refs_1_, bf16[2,16,512]{2,1,0:T(8,128)(2,1)S(1)} %collective-permute-done.25.refs_2_, ...), custom_call_target="tpu_custom_call" | custom-call | tf_op jit(solution)/shard_map/pallas_call | solution.py:36
  110.8 1.6 %shard_map.98 = bf16[256,2048]{1,0:T(8,128)(2,1)} custom-call(s32[2]{0:T(128)S(1)} %pad_add_fusion.meta.refs_0_, bf16[256,1024]{1,0:T(8,128)(2,1)S(1)} %get-tuple-element.77.keep, bf16[256,1024]{1,0:T(8,128)(2,1)S(1)} %collective-permute-done.18.received), custom_call_target="tpu_custom_call" | custom-call | tf_op jit(solution)/shard_map/pallas_call | solution.py:36
  112.4 2.0 %shard_map.102 = (bf16[256,1024]{1,0:T(8,128)(2,1)}, bf16[256,1024]{1,0:T(8,128)(2,1)}) custom-call(s32[2]{0:T(128)S(1)} %pad_add_fusion.meta.refs_0_, f32[2,256,512]{2,1,0:T(8,128)S(1)} %get-tuple-element.82.near_keep, bf16[2,256,512]{2,1,0:T(8,128)(2,1)S(1)} %collective-permute-done.20.near_recv, f32[2,64,512]{2,1,0:T(8,128)S(1)} %get-tuple-element.92.up_keep, ...), custom_call_target="tpu_custom_call" | custom-call | tf_op jit(solution)/shard_map/pallas_call | solution.py:36
  114.4 2.5 %collective-permute-done.33 = bf16[64,1024]{1,0:T(8,128)(2,1)} collective-permute-done((bf16[64,1024]{1,0:T(8,128)(2,1)}, bf16[64,1024]{1,0:T(8,128)(2,1)}, u32[]{:S(2)}, u32[]{:S(2)}) %collective-permute-start.33) | collective-permute-done | bytes 131104 | tf_op jit(solution)/shard_map/ppermute | solution.py:24
  (96 shorter events, 35.9 us)
Async XLA Ops:
  1.9 6.6 %collective-permute-start.2 = (bf16[2,256,512]{2,1,0:T(8,128)(2,1)S(1)}, bf16[2,256,512]{2,1,0:T(8,128)(2,1)S(1)}, u32[]{:S(2)}, u32[]{:S(2)}) collective-permute-start(bf16[2,256,512]{2,1,0:T(8,128)(2,1)S(1)} %pad_maximum_fusion), channel_id=1, source_target_pairs={{0,1},{1,0},{2,3},{3,2},{4,5},{5,4},{6,7},{7,6},{8,9},{9,8},{10,11... | collective-permute-start | bytes 1572872 | tf_op jit(solution)/shard_map/ppermute | solution.py:24
  4.7 13.3 %collective-permute-start.1 = (bf16[64,1024]{1,0:T(8,128)(2,1)S(1)}, bf16[64,1024]{1,0:T(8,128)(2,1)S(1)}, u32[]{:S(2)}, u32[]{:S(2)}) collective-permute-start(bf16[64,1024]{1,0:T(8,128)(2,1)S(1)} %maximum_select_fusion.1), channel_id=1, source_target_pairs={{0,16},{1,3},{2,18},{3,1},{4,20},{5,7},{6,22},{7,5},{8,24},{9,11},... | collective-permute-start | bytes 393224 | tf_op jit(solution)/shard_map/ppermute | solution.py:24
  12.0 6.0 %collective-permute-start.5 = (bf16[2,16,512]{2,1,0:T(8,128)(2,1)S(1)}, bf16[2,16,512]{2,1,0:T(8,128)(2,1)S(1)}, u32[]{:S(2)}, u32[]{:S(2)}) collective-permute-start(bf16[2,16,512]{2,1,0:T(8,128)(2,1)S(1)} %get-tuple-element.55), channel_id=1, source_target_pairs={{0,24},{1,25},{2,26},{3,27},{4,28},{5,29},{6,30},{7,31},{8,16},{9,... | collective-permute-start | bytes 98312 | tf_op jit(solution)/shard_map/ppermute | solution.py:24
  16.4 15.0 %collective-permute-start.7 = (bf16[2,128,512]{2,1,0:T(8,128)(2,1)S(1)}, bf16[2,128,512]{2,1,0:T(8,128)(2,1)S(1)}, u32[]{:S(2)}, u32[]{:S(2)}) collective-permute-start(bf16[2,128,512]{2,1,0:T(8,128)(2,1)S(1)} %get-tuple-element.62), channel_id=1, source_target_pairs={{0,2},{1,3},{2,0},{3,1},{4,6},{5,7},{6,4},{7,5},{8,10},{9,11},{10,... | collective-permute-start | bytes 786440 | tf_op jit(solution)/shard_map/ppermute | solution.py:24
  19.6 11.9 %collective-permute-start.10 = (bf16[2,128,512]{2,1,0:T(8,128)(2,1)S(1)}, bf16[2,128,512]{2,1,0:T(8,128)(2,1)S(1)}, u32[]{:S(2)}, u32[]{:S(2)}) collective-permute-start(bf16[2,128,512]{2,1,0:T(8,128)(2,1)S(1)} %get-tuple-element.107), channel_id=1, source_target_pairs={{0,6},{1,7},{2,4},{3,5},{4,2},{5,3},{6,0},{7,1},{8,14},{9,15},{10,... | collective-permute-start | bytes 786440 | tf_op jit(solution)/shard_map/ppermute | solution.py:24
  21.9 11.6 %collective-permute-start.9 = (bf16[2,128,512]{2,1,0:T(8,128)(2,1)S(1)}, bf16[2,128,512]{2,1,0:T(8,128)(2,1)S(1)}, u32[]{:S(2)}, u32[]{:S(2)}) collective-permute-start(bf16[2,128,512]{2,1,0:T(8,128)(2,1)S(1)} %get-tuple-element.107), channel_id=1, source_target_pairs={{0,4},{1,5},{2,6},{3,7},{4,0},{5,1},{6,2},{7,3},{8,12},{9,13},{10,... | collective-permute-start | bytes 786440 | tf_op jit(solution)/shard_map/ppermute | solution.py:24
  22.4 11.1 %collective-permute-start.11 = (bf16[128,1024]{1,0:T(8,128)(2,1)S(1)}, bf16[128,1024]{1,0:T(8,128)(2,1)S(1)}, u32[]{:S(2)}, u32[]{:S(2)}) collective-permute-start(bf16[128,1024]{1,0:T(8,128)(2,1)S(1)} %pad_maximum_fusion.2), channel_id=1, source_target_pairs={{0,8},{1,17},{2,10},{3,19},{4,12},{5,21},{6,14},{7,23},{8,0},{9,25... | collective-permute-start | bytes 786440 | tf_op jit(solution)/shard_map/ppermute | solution.py:24
  23.9 7.6 %collective-permute-start.8 = (bf16[2,64,512]{2,1,0:T(8,128)(2,1)S(1)}, bf16[2,64,512]{2,1,0:T(8,128)(2,1)S(1)}, u32[]{:S(2)}, u32[]{:S(2)}) collective-permute-start(bf16[2,64,512]{2,1,0:T(8,128)(2,1)S(1)} %get-tuple-element.108.refs_8_), channel_id=1, source_target_pairs={{0,2},{1,3},{2,0},{3,1},{4,6},{5,7},{6,4},{7,5},{8,10},{9,11},{10,... | collective-permute-start | bytes 393224 | tf_op jit(solution)/shard_map/ppermute | solution.py:24
  33.6 11.2 %collective-permute-start.14 = (bf16[256,1024]{1,0:T(8,128)(2,1)S(1)}, bf16[256,1024]{1,0:T(8,128)(2,1)S(1)}, u32[]{:S(2)}, u32[]{:S(2)}) collective-permute-start(bf16[256,1024]{1,0:T(8,128)(2,1)S(1)} %pad_maximum_fusion.1.refs_3_), channel_id=1, source_target_pairs={{0,2},{1,5},{2,0},{3,7},{4,6},{5,1},{6,4},{7,3},{8,10},{9,13},{10,... | collective-permute-start | bytes 1572872 | tf_op jit(solution)/shard_map/ppermute | solution.py:24
  35.1 10.9 %collective-permute-start.13 = (bf16[256,1024]{1,0:T(8,128)(2,1)S(1)}, bf16[256,1024]{1,0:T(8,128)(2,1)S(1)}, u32[]{:S(2)}, u32[]{:S(2)}) collective-permute-start(bf16[256,1024]{1,0:T(8,128)(2,1)S(1)} %dynamic-slice_bitcast_fusion), channel_id=1, source_target_pairs={{0,1},{1,0},{2,3},{3,2},{4,5},{5,4},{6,7},{7,6},{8,9},{9,8},{10,11... | collective-permute-start | bytes 1572872 | tf_op jit(solution)/shard_map/ppermute | solution.py:24
  43.9 9.2 %collective-permute-start.15 = (bf16[256,1024]{1,0:T(8,128)(2,1)S(1)}, bf16[256,1024]{1,0:T(8,128)(2,1)S(1)}, u32[]{:S(2)}, u32[]{:S(2)}) collective-permute-start(bf16[256,1024]{1,0:T(8,128)(2,1)S(1)} %pad_maximum_fusion.1.refs_3_), channel_id=1, source_target_pairs={{0,4},{1,9},{2,6},{3,11},{4,0},{5,13},{6,2},{7,15},{8,12},{9,1},{1... | collective-permute-start | bytes 1572872 | tf_op jit(solution)/shard_map/ppermute | solution.py:24
  44.8 13.9 %collective-permute-start.16 = (bf16[256,1024]{1,0:T(8,128)(2,1)S(1)}, bf16[256,1024]{1,0:T(8,128)(2,1)S(1)}, u32[]{:S(2)}, u32[]{:S(2)}) collective-permute-start(bf16[256,1024]{1,0:T(8,128)(2,1)S(1)} %collective-permute-done.14.refs_4_), channel_id=1, source_target_pairs={{0,4},{1,9},{2,6},{3,11},{4,0},{5,13},{6,2},{7,15},{8,12},{9,1},{1... | collective-permute-start | bytes 1572872 | tf_op jit(solution)/shard_map/ppermute | solution.py:24
  60.8 12.3 %collective-permute-start.30 = (bf16[256,1024]{1,0:T(8,128)(2,1)S(1)}, bf16[256,1024]{1,0:T(8,128)(2,1)S(1)}, u32[]{:S(2)}, u32[]{:S(2)}) collective-permute-start(bf16[256,1024]{1,0:T(8,128)(2,1)S(1)} %get-tuple-element.101), channel_id=1, source_target_pairs={{0,4},{1,9},{2,6},{3,11},{4,0},{5,13},{6,2},{7,15},{8,12},{9,1},{1... | collective-permute-start | bytes 1572872 | tf_op jit(solution)/shard_map/ppermute | solution.py:24
  61.7 13.9 %collective-permute-start.29 = (bf16[256,1024]{1,0:T(8,128)(2,1)S(1)}, bf16[256,1024]{1,0:T(8,128)(2,1)S(1)}, u32[]{:S(2)}, u32[]{:S(2)}) collective-permute-start(bf16[256,1024]{1,0:T(8,128)(2,1)S(1)} %get-tuple-element.97), channel_id=1, source_target_pairs={{0,4},{1,9},{2,6},{3,11},{4,0},{5,13},{6,2},{7,15},{8,12},{9,1},{1... | collective-permute-start | bytes 1572872 | tf_op jit(solution)/shard_map/ppermute | solution.py:24
  73.3 14.0 %collective-permute-start.31 = (bf16[256,1024]{1,0:T(8,128)(2,1)S(1)}, bf16[256,1024]{1,0:T(8,128)(2,1)S(1)}, u32[]{:S(2)}, u32[]{:S(2)}) collective-permute-start(bf16[256,1024]{1,0:T(8,128)(2,1)S(1)} %add_convert_fusion.1), channel_id=1, source_target_pairs={{0,2},{1,5},{2,0},{3,7},{4,6},{5,1},{6,4},{7,3},{8,10},{9,13},{10,... | collective-permute-start | bytes 1572872 | tf_op jit(solution)/shard_map/ppermute | solution.py:24
  75.7 14.4 %collective-permute-start.21 = (bf16[2,64,512]{2,1,0:T(8,128)(2,1)S(1)}, bf16[2,64,512]{2,1,0:T(8,128)(2,1)S(1)}, u32[]{:S(2)}, u32[]{:S(2)}) collective-permute-start(bf16[2,64,512]{2,1,0:T(8,128)(2,1)S(1)} %get-tuple-element.86), channel_id=1, source_target_pairs={{0,2},{1,3},{2,0},{3,1},{4,6},{5,7},{6,4},{7,5},{8,10},{9,11},{10,... | collective-permute-start | bytes 393224 | tf_op jit(solution)/shard_map/ppermute | solution.py:24
  76.4 13.9 %collective-permute-start.22 = (bf16[2,128,512]{2,1,0:T(8,128)(2,1)S(1)}, bf16[2,128,512]{2,1,0:T(8,128)(2,1)S(1)}, u32[]{:S(2)}, u32[]{:S(2)}) collective-permute-start(bf16[2,128,512]{2,1,0:T(8,128)(2,1)S(1)} %get-tuple-element.87), channel_id=1, source_target_pairs={{0,4},{1,5},{2,6},{3,7},{4,0},{5,1},{6,2},{7,3},{8,12},{9,13},{10,... | collective-permute-start | bytes 786440 | tf_op jit(solution)/shard_map/ppermute | solution.py:24
  77.3 16.7 %collective-permute-start.23 = (bf16[2,128,512]{2,1,0:T(8,128)(2,1)S(1)}, bf16[2,128,512]{2,1,0:T(8,128)(2,1)S(1)}, u32[]{:S(2)}, u32[]{:S(2)}) collective-permute-start(bf16[2,128,512]{2,1,0:T(8,128)(2,1)S(1)} %get-tuple-element.88), channel_id=1, source_target_pairs={{0,6},{1,7},{2,4},{3,5},{4,2},{5,3},{6,0},{7,1},{8,14},{9,15},{10,... | collective-permute-start | bytes 786440 | tf_op jit(solution)/shard_map/ppermute | solution.py:24
  79.2 17.4 %collective-permute-start.27 = (bf16[2,128,512]{2,1,0:T(8,128)(2,1)S(1)}, bf16[2,128,512]{2,1,0:T(8,128)(2,1)S(1)}, u32[]{:S(2)}, u32[]{:S(2)}) collective-permute-start(bf16[2,128,512]{2,1,0:T(8,128)(2,1)S(1)} %get-tuple-element.75), channel_id=1, source_target_pairs={{0,2},{1,3},{2,0},{3,1},{4,6},{5,7},{6,4},{7,5},{8,10},{9,11},{10,... | collective-permute-start | bytes 786440 | tf_op jit(solution)/shard_map/ppermute | solution.py:24
  87.6 20.4 %collective-permute-start.32 = (bf16[128,1024]{1,0:T(8,128)(2,1)S(1)}, bf16[128,1024]{1,0:T(8,128)(2,1)S(1)}, u32[]{:S(2)}, u32[]{:S(2)}) collective-permute-start(bf16[128,1024]{1,0:T(8,128)(2,1)S(1)} %slice.17), channel_id=1, source_target_pairs={{0,8},{1,17},{2,10},{3,19},{4,12},{5,21},{6,14},{7,23},{8,0},{9,25... | collective-permute-start | bytes 786440 | tf_op jit(solution)/shard_map/ppermute | solution.py:24
  90.1 20.7 %collective-permute-start.18 = (bf16[256,1024]{1,0:T(8,128)(2,1)}, bf16[256,1024]{1,0:T(8,128)(2,1)S(1)}, u32[]{:S(2)}, u32[]{:S(2)}) collective-permute-start(bf16[256,1024]{1,0:T(8,128)(2,1)} %get-tuple-element.78), channel_id=1, source_target_pairs={{0,1},{1,0},{2,3},{3,2},{4,5},{5,4},{6,7},{7,6},{8,9},{9,8},{10,11... | collective-permute-start | bytes 1572872 | tf_op jit(solution)/shard_map/ppermute | solution.py:24
  90.4 22.1 %collective-permute-start.20 = (bf16[2,256,512]{2,1,0:T(8,128)(2,1)}, bf16[2,256,512]{2,1,0:T(8,128)(2,1)S(1)}, u32[]{:S(2)}, u32[]{:S(2)}) collective-permute-start(bf16[2,256,512]{2,1,0:T(8,128)(2,1)} %get-tuple-element.84), channel_id=1, source_target_pairs={{0,1},{1,0},{2,3},{3,2},{4,5},{5,4},{6,7},{7,6},{8,9},{9,8},{10,11... | collective-permute-start | bytes 1572872 | tf_op jit(solution)/shard_map/ppermute | solution.py:24
  96.6 9.0 %collective-permute-start.26 = (bf16[2,32,512]{2,1,0:T(8,128)(2,1)S(1)}, bf16[2,32,512]{2,1,0:T(8,128)(2,1)S(1)}, u32[]{:S(2)}, u32[]{:S(2)}) collective-permute-start(bf16[2,32,512]{2,1,0:T(8,128)(2,1)S(1)} %get-tuple-element.91), channel_id=1, source_target_pairs={{0,8},{1,9},{2,10},{3,11},{4,12},{5,13},{6,14},{7,15},{8,0},{9,1},... | collective-permute-start | bytes 196616 | tf_op jit(solution)/shard_map/ppermute | solution.py:24
  109.4 7.5 %collective-permute-start.33 = (bf16[64,1024]{1,0:T(8,128)(2,1)}, bf16[64,1024]{1,0:T(8,128)(2,1)}, u32[]{:S(2)}, u32[]{:S(2)}) collective-permute-start(bf16[64,1024]{1,0:T(8,128)(2,1)} %slice.19), channel_id=1, source_target_pairs={{0,16},{1,3},{2,18},{3,1},{4,20},{5,7},{6,22},{7,5},{8,24},{9,11},... | collective-permute-start | bytes 393224 | tf_op jit(solution)/shard_map/ppermute | solution.py:24
  (19 other events, 155.7 us)

commit v3 on v2

v3 whole, which is shorter than its diff:
```python
import math

import jax
import jax.numpy as jnp
from jax import lax
from jax.experimental import pallas as pl
from jax.experimental.pallas import tpu as pltpu
from jax.sharding import PartitionSpec as P

HEADS = 8
HS = 128
NR = 128

HALF_ROOT = 0.7071067811865476
SCORE_SCALE = 1.0 / math.sqrt(HS)
EXP2_SCALE = SCORE_SCALE * math.log2(math.e)
F32 = jnp.float32
BF16 = jnp.bfloat16
VMEM_LIMIT = 20 * 1024 * 1024


def permute(value, masks):
    count = lax.axis_size("seq")
    return lax.ppermute(value, "seq", [(i, i ^ masks[i & 1]) for i in range(count)])


def swap(value, mask):
    return permute(value, (mask, mask))


def after(value, *others):
    return lax.optimization_barrier((value, *others))[0]


def call(body, meta, operands, shapes, scratch=(), last=False, flops=0):
    specs = [pl.BlockSpec(memory_space=pltpu.VMEM) for _ in operands]
    if last:
        out_specs = [pl.BlockSpec(s.shape, lambda i: (0,) * len(s.shape)) for s in shapes]
    else:
        out_specs = [pl.BlockSpec(memory_space=pltpu.VMEM) for _ in shapes]
    return pl.pallas_call(
        body,
        grid=(1,) if last else (),
        in_specs=[pl.BlockSpec(memory_space=pltpu.SMEM)] + specs,
        out_specs=out_specs,
        out_shape=shapes,
        scratch_shapes=list(scratch),
        compiler_params=pltpu.CompilerParams(vmem_limit_bytes=VMEM_LIMIT),
        cost_estimate=pl.CostEstimate(flops=flops, bytes_accessed=0, transcendentals=0),
    )(meta, *operands)


def struct(rows, cols, dtype):
    return jax.ShapeDtypeStruct((rows, cols), dtype)


def planes(rows, cols, dtype):
    return jax.ShapeDtypeStruct((2, rows, cols), dtype)


def dot(a, b, dims):
    return lax.dot_general(a, b, (dims, ((), ())), preferred_element_type=F32)


NN = ((1,), (0,))
NT = ((1,), (1,))
TN = ((0,), (0,))


def group_matrix(rows, cols, row_div, col_div):
    row = lax.broadcasted_iota(jnp.int32, (rows, cols), 0) // row_div
    col = lax.broadcasted_iota(jnp.int32, (rows, cols), 1) // col_div
    return jnp.where(row == col, 1.0, 0.0).astype(BF16)


def pool(rows):
    half = rows.shape[0] // 2
    return (dot(group_matrix(half, 2 * half, 1, 2), rows, NN) * HALF_ROOT).astype(BF16)


def spread(grad, times, factor):
    high = grad.astype(BF16)
    low = (grad - high.astype(F32)).astype(BF16)
    matrix = group_matrix(times * grad.shape[0], grad.shape[0], times, 1)
    return (dot(matrix, high, NN) + dot(matrix, low, NN)) * factor


def lanes(ref):
    return jnp.concatenate([ref[0], ref[1]], axis=1)


def put_planes(ref, rows):
    width = ref.shape[2]
    ref[0] = rows[:, :width].astype(ref.dtype)
    ref[1] = rows[:, width:].astype(ref.dtype)


def half_of(meta, width, mine):
    start = meta[0] * width if mine else (1 - meta[0]) * width
    return pl.ds(pl.multiple_of(start, width), width)


def pool_body(meta, own, other, *outs):
    first_own = pool(lanes(own))
    first_other = pool(lanes(other))
    put_planes(outs[0], first_own)
    put_planes(outs[1], first_other)
    rows = jnp.concatenate([pool(first_own), pool(first_other)], axis=0)
    put_planes(outs[2], rows)
    for out in outs[3:]:
        rows = pool(rows)
        put_planes(out, rows)


def key_sets(kv_own, kv_other, next_own, next_other, far, at):
    near = (kv_own, kv_other)
    coarse = (next_other, next_own)
    sets = []
    for plane in range(2):
        far_rows = [ref[plane, start : start + rows, at] for ref, start, rows in far]
        sets.append(
            [
                jnp.concatenate([near[group][plane, :, at], coarse[group][plane, :, at]] + far_rows, axis=0)
                for group in range(2)
            ]
        )
    return sets


def forward_body(parts, meta, q_own, q_other, kv_own, kv_other, next_own, next_other, *refs):
    attn_ref, probs_ref = refs[-2:]
    far = [(refs[index], start, rows) for index, start, rows in parts]
    length, width = q_own.shape
    chunk = length // 2
    for head in range(width // HS):
        at = slice(head * HS, (head + 1) * HS)
        keys, values = key_sets(kv_own, kv_other, next_own, next_other, far, at)
        for group, q_ref in enumerate((q_own, q_other)):
            scores = dot(keys[group], q_ref[:, at], NT)
            for start in range(0, length, chunk):
                some = scores[:, start : start + chunk]
                top = jnp.max(some, axis=0, keepdims=True)
                weights = jnp.exp2((some - top) * EXP2_SCALE)
                total = jnp.sum(weights, axis=0, keepdims=True)
                probs = (weights * (1.0 / total)).astype(BF16)
                probs_ref[2 * head + group, :, start : start + chunk] = probs
                first = group * length + start
                attn_ref[first : first + chunk, at] = dot(probs, values[group], TN).astype(BF16)


def backward_body(
    parts, n_far, n_out, heads, meta, q_own, q_other, kv_own, kv_other, next_own, next_other, *refs
):
    far = [(refs[index], start, rows) for index, start, rows in parts]
    d_keep, d_recv, probs_ref = refs[n_far : n_far + 3]
    outs = refs[len(refs) - n_out :]
    for previous, out in zip(refs[n_far + 3 : len(refs) - n_out], outs, strict=False):
        out[..., : previous.shape[-1]] = previous[...]
    dq_own, dq_other, near_own, near_other, *far_grads = outs
    near_rows = kv_own.shape[1]
    after_next = near_rows + next_own.shape[1]
    for head in heads:
        at = slice(head * HS, (head + 1) * HS)
        keys, values = key_sets(kv_own, kv_other, next_own, next_other, far, at)
        grads = ([], [])
        for group, (q_ref, dq_ref) in enumerate(((q_own, dq_own), (q_other, dq_other))):
            length = q_ref.shape[0]
            rows = slice(group * length, (group + 1) * length)
            d_attn = (d_keep[rows, at] + d_recv[rows, at].astype(F32)).astype(BF16)
            probs_low = probs_ref[2 * head + group]
            probs = probs_low.astype(F32)
            d_prob = dot(values[group], d_attn, NT)
            center = jnp.sum(probs * d_prob, axis=0, keepdims=True)
            d_score = (probs * (d_prob - center)).astype(BF16)
            dq_ref[:, at] = (dot(d_score, keys[group], TN) * SCORE_SCALE).astype(BF16)
            grads[0].append(dot(d_score, q_ref[:, at], NN))
            grads[1].append(dot(probs_low, d_attn, NN))
        for plane, factor in enumerate((SCORE_SCALE, 1.0)):
            for group, near in enumerate((near_own, near_other)):
                mine, other = grads[plane][group], grads[plane][1 - group]
                near[plane, :near_rows, at] = (mine[:near_rows] * factor).astype(near.dtype)
                near[plane, near_rows:, at] = (other[near_rows:after_next] * factor).astype(near.dtype)
            total = (grads[plane][0][after_next:] + grads[plane][1][after_next:]) * factor
            done = 0
            for index, start, rows in parts:
                out = far_grads[index]
                out[plane, start : start + rows, at] = total[done : done + rows].astype(BF16)
                done += rows


def pieces_of(quarters, piece):
    return [(quarter, start) for quarter in quarters for start in range(0, quarter.shape[0], piece)]


def rows_of_piece(meta, masks, index, piece):
    owner = meta[1] ^ jnp.where(meta[0] == 0, masks[0][index], masks[1][index])
    return pl.ds(pl.multiple_of(owner * piece, piece), piece)


def ordered_weight(meta, quarters, scratch, piece, masks):
    for index, (quarter, start) in enumerate(pieces_of(quarters, piece)):
        scratch[rows_of_piece(meta, masks, index, piece), :] = quarter[start : start + piece, :]


def d_attn_body(piece, masks, meta, grad_own, grad_other, *refs):
    keep, send, scratch = refs[-3:]
    ordered_weight(meta, refs[:-3], scratch, piece, masks)
    length = grad_own.shape[0]
    mine = scratch[half_of(meta, keep.shape[1], True), :]
    theirs = scratch[half_of(meta, keep.shape[1], False), :]
    send[:length] = dot(grad_other[...], theirs, NT).astype(BF16)
    send[length:] = dot(grad_own[...], theirs, NT).astype(BF16)
    keep[:length] = dot(grad_own[...], mine, NT)
    keep[length:] = dot(grad_other[...], mine, NT)


def attended_body(piece, masks, meta, attn_mine, attn_theirs, *refs):
    keep, send, scratch = refs[-3:]
    ordered_weight(meta, refs[:-3], scratch, piece, masks)
    length = keep.shape[0]
    mine = scratch[half_of(meta, attn_mine.shape[1], True), :]
    theirs = scratch[half_of(meta, attn_mine.shape[1], False), :]
    send[...] = (
        dot(attn_mine[length:], mine, NN) + dot(attn_theirs[:length], theirs, NN)
    ).astype(BF16)
    keep[...] = (
        dot(attn_mine[:length], mine, NN) + dot(attn_theirs[length:], theirs, NN)
    ).astype(BF16)


def weight_grad_body(piece, masks, meta, attn_mine, attn_theirs, grad_own, grad_other, *refs):
    scratch = refs[-1]
    length = grad_own.shape[0]
    width = attn_mine.shape[1]
    mine = dot(attn_mine[:length], grad_own[...], TN) + dot(attn_mine[length:], grad_other[...], TN)
    scratch[half_of(meta, width, True), :] = mine.astype(BF16)
    theirs = dot(attn_theirs[length:], grad_own[...], TN) + dot(
        attn_theirs[:length], grad_other[...], TN
    )
    scratch[half_of(meta, width, False), :] = theirs.astype(BF16)
    for index, (quarter, start) in enumerate(pieces_of(refs[:-1], piece)):
        quarter[start : start + piece, :] = scratch[rows_of_piece(meta, masks, index, piece), :]


def high_body(cuts, skips, meta, own, *refs):
    received = refs[: len(skips)]
    for plane in range(2):
        total = own[plane].astype(F32)
        for ref, skip in zip(received, skips, strict=True):
            total = total + ref[plane, skip:].astype(F32)
        start = 0
        for out, rows in zip(refs[len(skips) :], cuts, strict=True):
            out[plane] = total[start : start + rows].astype(BF16)
            start += rows


def cascade_body(counts, meta, *refs):
    keep, send = refs[-2:]
    half = keep.shape[1]
    total = None
    start = 0
    rows = 2 * half >> (len(counts) - 1)
    for count in counts:
        level = lanes(refs[start])[:rows].astype(F32)
        for ref in refs[start + 1 : start + count]:
            level = level + lanes(ref)[:rows].astype(F32)
        start += count
        rows *= 2
        total = level if total is None else level + spread(total, 2, HALF_ROOT)
    put_planes(keep, total[:half])
    put_planes(send, total[half:])


def near_body(meta, keep, recv, dk, dv):
    rows, width = dk.shape[0], keep.shape[2]
    matrix = group_matrix(rows, keep.shape[1] - rows, 2, 1)
    for plane, out in enumerate((dk, dv)):
        own = keep[plane, :rows] + spread(keep[plane, rows:], 2, HALF_ROOT)
        out[:, half_of(meta, width, True)] = own
        other = recv[plane, :rows].astype(F32) + dot(matrix, recv[plane, rows:], NN) * HALF_ROOT
        out[:, half_of(meta, width, False)] = other


def finish_body(meta, base_k, base_v, up_keep, up_recv, dk, dv):
    rows, width = dk.shape[0], up_keep.shape[2]
    times = rows // up_keep.shape[1]
    factor = HALF_ROOT * HALF_ROOT
    matrix = group_matrix(rows, up_recv.shape[1], times, 1)
    mine, theirs = half_of(meta, width, True), half_of(meta, width, False)
    for plane, (base, out) in enumerate(((base_k, dk), (base_v, dv))):
        out[:, mine] = (base[:, mine] + spread(up_keep[plane], times, factor)).astype(BF16)
        received = dot(matrix, up_recv[plane], NN) * factor
        out[:, theirs] = (base[:, theirs] + received).astype(BF16)


def place_body(meta, *refs):
    outs = refs[2 * len(refs) // 3 :]
    for index, out in enumerate(outs):
        width = out.shape[1] // 2
        out[:, half_of(meta, width, True)] = refs[2 * index][...]
        out[:, half_of(meta, width, False)] = refs[2 * index + 1][...]


def body(queries, keys, values, out_weight, out_grad):
    inner = queries.shape[2]
    half = inner // 2
    length = queries.shape[1]
    heads = HEADS // 2
    seq_count = lax.axis_size("seq")
    seq_levels = seq_count.bit_length() - 1
    dp_count = lax.axis_size("dp")
    rank = lax.axis_index("seq")
    bit = rank % 2
    pair = rank // 2
    token_total = length * seq_count * queries.shape[0] * dp_count

    up = [1 << level for level in reversed(range(1, seq_levels))]
    orders = (up[:-2] + [2, 4], [2] + up[:-3] + [4, 8])
    stages = list(zip(*orders, strict=True))
    pieces = seq_count // 2
    masks = [
        [sum(m for s, m in enumerate(order) if index >> s & 1) // 2 for index in range(pieces)]
        for order in orders
    ]
    meta = jnp.stack([bit, pair]).astype(jnp.int32)

    query = queries[0]
    key = keys[0]
    value = values[0]
    grad = out_grad[0]
    if dp_count > 1:
        out_weight = lax.all_gather(out_weight, "dp", axis=1, tiled=True)
    cols = out_weight.shape[1] // 2
    piece = 2 * out_weight.shape[0]

    def part(array, which):
        width = array.shape[1] // 2
        return lax.dynamic_slice_in_dim(array, which * width, width, 1)

    q_half = struct(length, half, BF16)
    g_half = struct(length, cols, BF16)
    kv_other = swap(jnp.stack([part(key, 1 - bit), part(value, 1 - bit)]), 1)
    w_theirs = swap(part(out_weight, 1 - bit), 1)
    kv_own = jnp.stack([part(key, bit), part(value, bit)])
    w_mine = part(out_weight, bit)

    sizes = [length // 2, length // 2] + [2 * length >> level for level in range(2, seq_levels + 1)]
    shapes = [planes(rows, half, BF16) for rows in sizes]
    pooled = call(pool_body, meta, (kv_own, kv_other), shapes)
    next_own, next_other = pooled[:2]
    coarse = dict(zip(range(1, seq_levels), pooled[2:], strict=True))

    w_rows = jnp.where(
        bit == 0,
        jnp.concatenate([w_mine, w_theirs], axis=0),
        jnp.concatenate([w_theirs, w_mine], axis=0),
    )
    w_received = permute(w_rows, stages[0])
    far_masks = [(h, (1 << h) + (low << 3)) for h in range(3, seq_levels) for low in range(1 << (h - 3))]
    high_parts = [swap(coarse[h], mask) for h, mask in far_masks]
    first_panel = swap(coarse[1], 2)
    w_received, first_panel, *high_parts = lax.optimization_barrier(
        (w_received, first_panel, *high_parts)
    )

    high = jnp.concatenate(high_parts, axis=1)
    second = jnp.concatenate([coarse[2], high], axis=1)
    panels = [high, first_panel, swap(high, 2), swap(second, 4), swap(second, 6)]
    for stage in stages[1:-2]:
        w_rows = jnp.concatenate([w_rows, w_received], axis=0)
        w_received = permute(w_rows, stage)
    query, grad = lax.optimization_barrier((query, grad, high))[:2]
    q_other = swap(part(query, 1 - bit), 1)
    g_other = swap(part(grad, 1 - bit), 1)
    q_own = part(query, bit)
    g_own = part(grad, bit)
    n_high, n_second = high.shape[1], coarse[2].shape[1]
    parts = ((1, 0, coarse[1].shape[1]), (3, 0, n_second), (4, 0, n_second))
    parts += ((0, 0, n_high), (2, 0, n_high), (3, n_second, n_high), (4, n_second, n_high))

    w_rows = jnp.concatenate([w_rows, after(w_received, panels[2])], axis=0)
    w_received = permute(w_rows, stages[-2])
    w_last = permute(w_rows, stages[-1])

    key_count = length + length // 2 + sum(rows for _, _, rows in parts)
    att_ops = (q_own, q_other, kv_own, kv_other, next_own, next_other, *panels)
    attn_mine, probs = call(
        lambda *refs: forward_body(parts, *refs),
        after(meta, w_rows),
        att_ops,
        [struct(2 * length, half, BF16), jax.ShapeDtypeStruct((2 * heads, key_count, length), BF16)],
        flops=32 * 2 * length * key_count * half,
    )

    w_received, w_last, _ = lax.optimization_barrier((w_received, w_last, attn_mine))
    quarters = (w_rows, w_received, w_last, permute(w_received, stages[-1]))
    attn_theirs = swap(attn_mine, 1)

    scratch = [pltpu.VMEM((pieces * piece, cols), BF16)]
    wg = call(
        lambda *refs: weight_grad_body(piece, masks, *refs),
        meta,
        (attn_mine, attn_theirs, g_own, g_other),
        [struct(pieces * piece // 4, cols, BF16)] * 4,
        scratch,
    )
    wg_received = [permute(after(part, quarters[3]), stages[-1]) for part in (wg[3], wg[2])]

    d_keep, d_send = call(
        lambda *refs: d_attn_body(piece, masks, *refs),
        after(meta, wg[0]),
        (g_own, g_other, *quarters),
        [struct(2 * length, half, F32), struct(2 * length, half, BF16)],
        scratch,
    )
    d_recv = swap(d_send, 1)

    def add(kept, received):
        return (kept.astype(F32) + received.astype(F32)).astype(BF16)

    back_ops = att_ops + (d_keep, d_recv, probs)

    def backward(which, token, previous):
        width = which[-1] * HS + HS
        near_count = length + length // 2
        shapes = [struct(length, width, BF16)] * 2
        shapes += [planes(near_count, width, F32), planes(near_count, width, BF16)]
        shapes += [planes(p.shape[1], width, BF16) for p in panels]
        return call(
            lambda *refs: backward_body(parts, len(panels), len(shapes), which, *refs),
            token,
            back_ops + tuple(previous),
            shapes,
        )

    grads = backward(range(heads // 2), meta, ())
    wg_send = add(wg[1], after(wg_received[0], grads[0]))
    wg_step = permute(wg_send, stages[-2])
    grads = backward(range(heads // 2, heads), after(meta, wg_send), grads)
    wg_keep = add(wg[0], after(wg_received[1], grads[0]))
    wg_total = add(wg_keep, wg_step)
    wg_rows = wg_total.shape[0] // 2
    wg_keep, wg_send = wg_total[:wg_rows], wg_total[wg_rows:]
    grads = lax.optimization_barrier((*grads, wg_send))[: len(grads)]
    dq_keep, dq_send, near_keep, near_send, high_own, first_grad, *rest = grads

    back = [swap(part, mask) for part, mask in zip(rest, (2, 4, 6), strict=True)]
    first_back = swap(first_grad, 2)
    wg_received = permute(wg_send, stages[-3])
    at_meta = after(meta, high_own)
    near_recv = swap(near_send, 1)
    dq_recv = swap(dq_send, 1)
    base_k, base_v = call(near_body, meta, (near_keep, near_recv), [struct(length, inner, F32)] * 2)

    at_keep, at_send = call(
        lambda *refs: attended_body(piece, masks, *refs),
        at_meta,
        (attn_mine, attn_theirs, *quarters),
        [g_half, g_half],
        scratch,
    )
    grad_queries, attended = call(
        place_body,
        meta,
        (dq_keep, dq_recv, at_keep, swap(at_send, 1)),
        [struct(length, inner, BF16), struct(length, 2 * cols, BF16)],
        last=True,
    )

    wg_received, first_back, *back = lax.optimization_barrier(
        (wg_received, first_back, *back, base_k, base_v, attended, grad_queries)
    )[: 2 + len(back)]
    wg_total = add(wg_keep, wg_received)
    wg_rows = wg_total.shape[0] // 2
    wg_keep, wg_send = wg_total[:wg_rows], wg_total[wg_rows:]
    wg_received = permute(wg_send, stages[-4])
    cuts = [coarse[h].shape[1] for h, _ in far_masks]
    high_shapes = [planes(rows, half, BF16) for rows in cuts]
    high_sums = call(
        lambda *refs: high_body(cuts, (0, n_second, n_second), *refs),
        after(meta, wg_send),
        (high_own, *back),
        high_shapes,
    )
    by_level = {1: [first_back], 2: back[1:]}
    for (h, mask), part in zip(far_masks, high_sums, strict=True):
        by_level.setdefault(h, []).append(swap(part, mask))
    total = wg_keep.astype(F32) + wg_received.astype(F32)
    rows = piece // 2
    wg_mine = lax.dynamic_slice_in_dim(total, bit * rows, rows, 0)
    wg_theirs = swap(lax.dynamic_slice_in_dim(total, (1 - bit) * rows, rows, 0).astype(BF16), 1)
    wg_theirs = wg_theirs.astype(F32)
    weight_grad = jnp.where(
        bit == 0,
        jnp.concatenate([wg_mine, wg_theirs], axis=1),
        jnp.concatenate([wg_theirs, wg_mine], axis=1),
    )
    if dp_count > 1:
        weight_grad = lax.psum_scatter(
            weight_grad.astype(BF16), "dp", scatter_dimension=1, tiled=True
        ).astype(F32)
    weight_grad = weight_grad * (1.0 / math.sqrt(token_total))

    levels = list(reversed(range(1, seq_levels)))
    received = [part for h in levels for part in by_level[h]]
    counts = [len(by_level[h]) for h in levels]
    up_rows = coarse[1].shape[1] // 2
    up_keep, up_send = call(
        lambda *refs: cascade_body(counts, *refs),
        after(meta, weight_grad),
        received,
        [planes(up_rows, half, F32), planes(up_rows, half, BF16)],
    )
    grad_keys, grad_values = call(
        finish_body,
        meta,
        (base_k, base_v, up_keep, swap(up_send, 1)),
        [struct(length, inner, BF16)] * 2,
        last=True,
    )
    return (attended[None], grad_queries[None], grad_keys[None], grad_values[None], weight_grad)


def solution(mesh):
    placed = (
        P("dp", "seq", None),
        P("dp", "seq", None),
        P("dp", "seq", None),
        P("seq", "dp"),
        P("dp", "seq", None),
    )
    return jax.shard_map(
        body,
        mesh=mesh,
        in_specs=placed,
        out_specs=(
            P("dp", "seq", None),
            P("dp", "seq", None),
            P("dp", "seq", None),
            P("dp", "seq", None),
            P("seq", "dp"),
        ),
        check_vma=False,
    )
```

time: 120 us -> 113 us (0.942)
  Pallas kernels: 32.3 us -> 26.2 us
  starting transfers between devices: 33.8 us -> 36 us
  waiting for transfers between devices: 44.9 us -> 43.1 us
  local copies, waits for them, and re-layouts: 5.69 us -> 4.11 us
    pallas_call x11 -> x12, Pallas kernels: 32.3 us -> 26.2 us  [call(): pl.pallas_call(body, grid=(1,) if last else (), in_specs=[pl.BlockSpec(me...]
    unnamed x19 -> x5, local copies, waits for them, and re-layouts: 2.83 us -> 0.03 us
    ppermute x35, starting transfers between devices: 33.8 us -> 36 us  [permute(): lax.ppermute(value, 'seq', [(i, i ^ masks[i & 1]) for i in range(count)])]
    dynamic_slice x4, local copies, waits for them, and re-layouts: 2.13 us -> 4 us  [part(): return lax.dynamic_slice_in_dim(array, which * width, width, 1)]
    ppermute x35, waiting for transfers between devices: 44.9 us -> 43.1 us  [permute(): lax.ppermute(value, 'seq', [(i, i ^ masks[i & 1]) for i in range(count)])]
  transfers between devices with their start and end apart: 35 -> 35, of which waited for: 16 -> 14; matrix products, arithmetic and copies ran while one was open for 2% -> 4% of each run, Pallas kernels for 25% -> 19%
where the time goes in v3:
time: 113 us
  waiting for transfers between devices  43.1 us (38%)
  starting transfers between devices  36 us (32%)
  Pallas kernels  26.2 us (23%)
  local copies, waits for them, and re-layouts  4.11 us (4%)
  other arithmetic  2.45 us (2%)
    ppermute x35, waiting for transfers between devices, permute(): lax.ppermute(value, 'seq', [(i, i ^ masks[i & 1]) for i in range(count)])  43.1 us
    ppermute x35, starting transfers between devices, permute(): lax.ppermute(value, 'seq', [(i, i ^ masks[i & 1]) for i in range(count)])  36 us
    pallas_call x12, Pallas kernels, call(): pl.pallas_call(body, grid=(1,) if last else (), in_specs=[pl.BlockSpec(me...  26.2 us
    dynamic_slice x4, local copies, waits for them, and re-layouts, part(): return lax.dynamic_slice_in_dim(array, which * width, width, 1)  4 us
  transfers between devices with their start and end apart: 35, of which 14 were waited for; matrix products, arithmetic and copies ran while one was open for 4% of the time, Pallas kernels for 19%

profile of v3, /device:TPU:0, one launch (start us, length us, event | category | flops | bytes accessed | tf_op | source)
XLA Modules:
  0.0 112.7 jit_solution(13618073937004330725)
XLA Ops:
  5.7 2.9 %collective-permute-start.3 = (bf16[2,128,512]{2,1,0:T(8,128)(2,1)S(1)}, bf16[2,128,512]{2,1,0:T(8,128)(2,1)S(1)}, u32[]{:S(2)}, u32[]{:S(2)}) collective-permute-start(bf16[2,128,512]{2,1,0:T(8,128)(2,1)S(1)} %get-tuple-element.84), channel_id=1, source_target_pairs={{0,2},{1,3},{2,0},{3,1},{4,6},{5,7},{6,4},{7,5},{8,10},{9,11},{10,... | collective-permute-start | bytes 786440 | tf_op jit(solution)/shard_map/ppermute | solution.py:24
  8.7 2.7 %collective-permute-start.1 = (bf16[64,1024]{1,0:T(8,128)(2,1)S(1)}, bf16[64,1024]{1,0:T(8,128)(2,1)S(1)}, u32[]{:S(2)}, u32[]{:S(2)}) collective-permute-start(bf16[64,1024]{1,0:T(8,128)(2,1)S(1)} %maximum_select_fusion.1), channel_id=1, source_target_pairs={{0,16},{1,3},{2,18},{3,1},{4,20},{5,7},{6,22},{7,5},{8,24},{9,11},... | collective-permute-start | bytes 393224 | tf_op jit(solution)/shard_map/ppermute | solution.py:24
  12.7 1.7 %collective-permute-start.5 = (bf16[2,16,512]{2,1,0:T(8,128)(2,1)S(1)}, bf16[2,16,512]{2,1,0:T(8,128)(2,1)S(1)}, u32[]{:S(2)}, u32[]{:S(2)}) collective-permute-start(bf16[2,16,512]{2,1,0:T(8,128)(2,1)S(1)} %get-tuple-element.86), channel_id=1, source_target_pairs={{0,16},{1,17},{2,18},{3,19},{4,20},{5,21},{6,22},{7,23},{8,24},{9,... | collective-permute-start | bytes 98312 | tf_op jit(solution)/shard_map/ppermute | solution.py:24
  15.8 1.7 %collective-permute-done.1 = bf16[64,1024]{1,0:T(8,128)(2,1)S(1)} collective-permute-done((bf16[64,1024]{1,0:T(8,128)(2,1)S(1)}, bf16[64,1024]{1,0:T(8,128)(2,1)S(1)}, u32[]{:S(2)}, u32[]{:S(2)}) %collective-permute-start.1) | collective-permute-done | bytes 131104 | tf_op jit(solution)/shard_map/ppermute | solution.py:24
  19.1 1.7 %collective-permute-start.11 = (bf16[2,128,512]{2,1,0:T(8,128)(2,1)S(1)}, bf16[2,128,512]{2,1,0:T(8,128)(2,1)S(1)}, u32[]{:S(2)}, u32[]{:S(2)}) collective-permute-start(bf16[2,128,512]{2,1,0:T(8,128)(2,1)S(1)} %get-tuple-element.175), channel_id=1, source_target_pairs={{0,6},{1,7},{2,4},{3,5},{4,2},{5,3},{6,0},{7,1},{8,14},{9,15},{10,... | collective-permute-start | bytes 786440 | tf_op jit(solution)/shard_map/ppermute | solution.py:24
  24.9 4.3 %collective-permute-done.8.refs_9_ = bf16[2,64,512]{2,1,0:T(8,128)(2,1)S(1)} collective-permute-done((bf16[2,64,512]{2,1,0:T(8,128)(2,1)S(1)}, bf16[2,64,512]{2,1,0:T(8,128)(2,1)S(1)}, u32[]{:S(2)}, u32[]{:S(2)}) %collective-permute-start.8) | collective-permute-done | bytes 131104 | tf_op jit(solution)/shard_map/ppermute | solution.py:24
  29.3 1.7 %collective-permute-done.7 = bf16[128,1024]{1,0:T(8,128)(2,1)S(1)} collective-permute-done((bf16[128,1024]{1,0:T(8,128)(2,1)S(1)}, bf16[128,1024]{1,0:T(8,128)(2,1)S(1)}, u32[]{:S(2)}, u32[]{:S(2)}) %collective-permute-start.7) | collective-permute-done | bytes 262176 | tf_op jit(solution)/shard_map/ppermute | solution.py:24
  33.3 4.1 %shard_map.93 = (bf16[512,512]{1,0:T(8,128)(2,1)S(1)}, bf16[8,896,256]{2,1,0:T(8,128)(2,1)S(1)}) custom-call(s32[2]{0:T(128)S(1)} %pad_add_fusion.meta.refs_0_, bf16[256,512]{1,0:T(8,128)(2,1)S(1)} %get-tuple-element.166.refs_1_, bf16[256,512]{1,0:T(8,128)(2,1)S(1)} %collective-permute-done.9.refs_2_, bf16[2,256,512]{2,1,0:T(8,128)(2,1)S(1)} %pad_maximum_fusion.own.refs_3_, ...), custom_call_target="tpu_custom_call" | custom-call | flops 7516192768 | tf_op jit(solution)/shard_map/pallas_call | solution.py:41
  37.5 7.3 %collective-permute-done.15.refs_5_ = bf16[256,1024]{1,0:T(8,128)(2,1)S(1)} collective-permute-done((bf16[256,1024]{1,0:T(8,128)(2,1)S(1)}, bf16[256,1024]{1,0:T(8,128)(2,1)S(1)}, u32[]{:S(2)}, u32[]{:S(2)}) %collective-permute-start.15) | collective-permute-done | bytes 524320 | tf_op jit(solution)/shard_map/ppermute | solution.py:24
  45.3 1.9 %shard_map.94 = (bf16[256,1024]{1,0:T(8,128)(2,1)S(1)}, bf16[256,1024]{1,0:T(8,128)(2,1)S(1)}, bf16[256,1024]{1,0:T(8,128)(2,1)S(1)}, bf16[256,1024]{1,0:T(8,128)(2,1)S(1)}) custom-call(s32[2]{0:T(128)S(1)} %pad_add_fusion.meta.refs_0_, bf16[512,512]{1,0:T(8,128)(2,1)S(1)} %get-tuple-element.98.refs_1_, ...), custom_call_target="tpu_custom_call" | custom-call | tf_op jit(solution)/shard_map/pallas_call | solution.py:41
  47.3 6.7 %collective-permute-done.16.refs_6_ = bf16[256,1024]{1,0:T(8,128)(2,1)S(1)} collective-permute-done((bf16[256,1024]{1,0:T(8,128)(2,1)S(1)}, bf16[256,1024]{1,0:T(8,128)(2,1)S(1)}, u32[]{:S(2)}, u32[]{:S(2)}) %collective-permute-start.16) | collective-permute-done | bytes 524320 | tf_op jit(solution)/shard_map/ppermute | solution.py:24
  54.0 2.0 %shard_map.95 = (f32[512,512]{1,0:T(8,128)S(1)}, bf16[512,512]{1,0:T(8,128)(2,1)S(1)}) custom-call(s32[2]{0:T(128)S(1)} %pad_add_fusion.meta.refs_0_, bf16[256,1024]{1,0:T(8,128)(2,1)S(1)} %get-tuple-element.164.refs_3_.refs_1_, bf16[256,1024]{1,0:T(8,128)(2,1)S(1)} %collective-permute-done.13.refs_4_.refs_2_, ...), custom_call_target="tpu_custom_call" | custom-call | tf_op jit(solution)/shard_map/pallas_call | solution.py:41
  58.1 3.9 %shard_map.96 = (bf16[256,256]{1,0:T(8,128)(2,1)S(1)}, bf16[256,256]{1,0:T(8,128)(2,1)S(1)}, f32[2,384,256]{2,1,0:T(8,128)S(1)}, bf16[2,384,256]{2,1,0:T(8,128)(...) custom-call(s32[2]{0:T(128)S(1)} %pad_add_fusion.meta.refs_0_, ...), custom_call_target="tpu_custom_call" | custom-call | tf_op jit(solution)/shard_map/pallas_call | solution.py:41
  62.1 3.2 %collective-permute-done.17 = bf16[256,1024]{1,0:T(8,128)(2,1)S(1)} collective-permute-done((bf16[256,1024]{1,0:T(8,128)(2,1)S(1)}, bf16[256,1024]{1,0:T(8,128)(2,1)S(1)}, u32[]{:S(2)}, u32[]{:S(2)}) %collective-permute-start.17) | collective-permute-done | bytes 524320 | tf_op jit(solution)/shard_map/ppermute | solution.py:24
  66.8 4.3 %shard_map.97 = (bf16[256,512]{1,0:T(8,128)(2,1)S(1)}, bf16[256,512]{1,0:T(8,128)(2,1)S(1)}, f32[2,384,512]{2,1,0:T(8,128)S(1)}, bf16[2,384,512]{2,1,0:T(8,128)(...) custom-call(s32[2]{0:T(128)S(1)} %pad_add_fusion.meta.refs_0_, ...), custom_call_target="tpu_custom_call" | custom-call | tf_op jit(solution)/shard_map/pallas_call | solution.py:41
  71.1 3.0 %collective-permute-done.19 = bf16[256,1024]{1,0:T(8,128)(2,1)S(1)} collective-permute-done((bf16[256,1024]{1,0:T(8,128)(2,1)S(1)}, bf16[256,1024]{1,0:T(8,128)(2,1)S(1)}, u32[]{:S(2)}, u32[]{:S(2)}) %collective-permute-start.19) | collective-permute-done | bytes 524320 | tf_op jit(solution)/shard_map/ppermute | solution.py:24
  75.0 1.7 %collective-permute-start.23 = (bf16[2,384,512]{2,1,0:T(8,128)(2,1)S(1)}, bf16[2,384,512]{2,1,0:T(8,128)(2,1)S(1)}, u32[]{:S(2)}, u32[]{:S(2)}) collective-permute-start(bf16[2,384,512]{2,1,0:T(8,128)(2,1)S(1)} %get-tuple-element.142), channel_id=1, source_target_pairs={{0,1},{1,0},{2,3},{3,2},{4,5},{5,4},{6,7},{7,6},{8,9},{9,8},{10,11... | collective-permute-start | bytes 2359304 | tf_op jit(solution)/shard_map/ppermute | solution.py:24
  76.7 1.9 %shard_map.98 = (bf16[256,1024]{1,0:T(8,128)(2,1)S(1)}, bf16[256,1024]{1,0:T(8,128)(2,1)S(1)}) custom-call(s32[2]{0:T(128)S(1)} %pad_add_fusion.meta.refs_0_, bf16[512,512]{1,0:T(8,128)(2,1)S(1)} %get-tuple-element.98.refs_1_, bf16[512,512]{1,0:T(8,128)(2,1)S(1)} %collective-permute-done.12.refs_2_, bf16[256,1024]{1,0:T(8,128)(2,1)S(1)} %pad_maximum_fusion.2.refs_3_, ...), custom_call_target="tpu_custom_call" | custom-call | tf_op jit(solution)/shard_map/pallas_call | solution.py:41
  84.9 1.8 %shard_map.99 = (bf16[256,1024]{1,0:T(8,128)(2,1)}, bf16[256,2048]{1,0:T(8,128)(2,1)}) custom-call(s32[2]{0:T(128)S(1)} %pad_add_fusion.meta.refs_0_, bf16[256,512]{1,0:T(8,128)(2,1)S(1)} %get-tuple-element.133.refs_0_, bf16[256,512]{1,0:T(8,128)(2,1)S(1)} %collective-permute-done.21.refs_1_, bf16[256,1024]{1,0:T(8,128)(2,1)S(1)} %get-tuple-element.137.refs_2_, ...), custom_call_target="tpu_custom_call" | custom-call | tf_op jit(solution)/shard_map/pallas_call | solution.py:41
  87.8 8.2 %collective-permute-done.26.refs_2_ = bf16[2,64,512]{2,1,0:T(8,128)(2,1)S(1)} collective-permute-done((bf16[2,64,512]{2,1,0:T(8,128)(2,1)S(1)}, bf16[2,64,512]{2,1,0:T(8,128)(2,1)S(1)}, u32[]{:S(2)}, u32[]{:S(2)}) %collective-permute-start.26) | collective-permute-done | bytes 131104 | tf_op jit(solution)/shard_map/ppermute | solution.py:24
  96.1 2.6 %collective-permute-start.29 = (bf16[64,1024]{1,0:T(8,128)(2,1)S(1)}, bf16[64,1024]{1,0:T(8,128)(2,1)}, u32[]{:S(2)}, u32[]{:S(2)}) collective-permute-start(bf16[64,1024]{1,0:T(8,128)(2,1)S(1)} %slice.19), channel_id=1, source_target_pairs={{0,16},{1,3},{2,18},{3,1},{4,20},{5,7},{6,22},{7,5},{8,24},{9,11},... | collective-permute-start | bytes 393224 | tf_op jit(solution)/shard_map/ppermute | solution.py:24
  99.8 2.5 %collective-permute-start.32 = (bf16[2,16,512]{2,1,0:T(8,128)(2,1)S(1)}, bf16[2,16,512]{2,1,0:T(8,128)(2,1)S(1)}, u32[]{:S(2)}, u32[]{:S(2)}) collective-permute-start(bf16[2,16,512]{2,1,0:T(8,128)(2,1)S(1)} %get-tuple-element.156), channel_id=1, source_target_pairs={{0,24},{1,25},{2,26},{3,27},{4,28},{5,29},{6,30},{7,31},{8,16},{9,... | collective-permute-start | bytes 98312 | tf_op jit(solution)/shard_map/ppermute | solution.py:24
  102.9 2.3 %collective-permute-done.29 = bf16[64,1024]{1,0:T(8,128)(2,1)} collective-permute-done((bf16[64,1024]{1,0:T(8,128)(2,1)S(1)}, bf16[64,1024]{1,0:T(8,128)(2,1)}, u32[]{:S(2)}, u32[]{:S(2)}) %collective-permute-start.29) | collective-permute-done | bytes 131104 | tf_op jit(solution)/shard_map/ppermute | solution.py:24
  110.8 1.9 %shard_map.103 = (bf16[256,1024]{1,0:T(8,128)(2,1)}, bf16[256,1024]{1,0:T(8,128)(2,1)}) custom-call(s32[2]{0:T(128)S(1)} %pad_add_fusion.meta.refs_0_, f32[256,1024]{1,0:T(8,128)S(1)} %get-tuple-element.143.base_k, f32[256,1024]{1,0:T(8,128)S(1)} %get-tuple-element.144.base_v, f32[2,64,512]{2,1,0:T(8,128)S(1)} %get-tuple-element.159.up_keep, ...), custom_call_target="tpu_custom_call" | custom-call | tf_op jit(solution)/shard_map/pallas_call | solution.py:41
  (84 shorter events, 35.8 us)
Async XLA Ops:
  5.7 13.3 %collective-permute-start.3 = (bf16[2,128,512]{2,1,0:T(8,128)(2,1)S(1)}, bf16[2,128,512]{2,1,0:T(8,128)(2,1)S(1)}, u32[]{:S(2)}, u32[]{:S(2)}) collective-permute-start(bf16[2,128,512]{2,1,0:T(8,128)(2,1)S(1)} %get-tuple-element.84), channel_id=1, source_target_pairs={{0,2},{1,3},{2,0},{3,1},{4,6},{5,7},{6,4},{7,5},{8,10},{9,11},{10,... | collective-permute-start | bytes 786440 | tf_op jit(solution)/shard_map/ppermute | solution.py:24
  8.7 8.8 %collective-permute-start.1 = (bf16[64,1024]{1,0:T(8,128)(2,1)S(1)}, bf16[64,1024]{1,0:T(8,128)(2,1)S(1)}, u32[]{:S(2)}, u32[]{:S(2)}) collective-permute-start(bf16[64,1024]{1,0:T(8,128)(2,1)S(1)} %maximum_select_fusion.1), channel_id=1, source_target_pairs={{0,16},{1,3},{2,18},{3,1},{4,20},{5,7},{6,22},{7,5},{8,24},{9,11},... | collective-permute-start | bytes 393224 | tf_op jit(solution)/shard_map/ppermute | solution.py:24
  19.1 13.5 %collective-permute-start.11 = (bf16[2,128,512]{2,1,0:T(8,128)(2,1)S(1)}, bf16[2,128,512]{2,1,0:T(8,128)(2,1)S(1)}, u32[]{:S(2)}, u32[]{:S(2)}) collective-permute-start(bf16[2,128,512]{2,1,0:T(8,128)(2,1)S(1)} %get-tuple-element.175), channel_id=1, source_target_pairs={{0,6},{1,7},{2,4},{3,5},{4,2},{5,3},{6,0},{7,1},{8,14},{9,15},{10,... | collective-permute-start | bytes 786440 | tf_op jit(solution)/shard_map/ppermute | solution.py:24
  20.8 12.5 %collective-permute-start.10 = (bf16[2,128,512]{2,1,0:T(8,128)(2,1)S(1)}, bf16[2,128,512]{2,1,0:T(8,128)(2,1)S(1)}, u32[]{:S(2)}, u32[]{:S(2)}) collective-permute-start(bf16[2,128,512]{2,1,0:T(8,128)(2,1)S(1)} %get-tuple-element.175), channel_id=1, source_target_pairs={{0,4},{1,5},{2,6},{3,7},{4,0},{5,1},{6,2},{7,3},{8,12},{9,13},{10,... | collective-permute-start | bytes 786440 | tf_op jit(solution)/shard_map/ppermute | solution.py:24
  21.1 8.1 %collective-permute-start.8 = (bf16[2,64,512]{2,1,0:T(8,128)(2,1)S(1)}, bf16[2,64,512]{2,1,0:T(8,128)(2,1)S(1)}, u32[]{:S(2)}, u32[]{:S(2)}) collective-permute-start(bf16[2,64,512]{2,1,0:T(8,128)(2,1)S(1)} %get-tuple-element.176.refs_7_), channel_id=1, source_target_pairs={{0,2},{1,3},{2,0},{3,1},{4,6},{5,7},{6,4},{7,5},{8,10},{9,11},{10,... | collective-permute-start | bytes 393224 | tf_op jit(solution)/shard_map/ppermute | solution.py:24
  22.6 8.3 %collective-permute-start.7 = (bf16[128,1024]{1,0:T(8,128)(2,1)S(1)}, bf16[128,1024]{1,0:T(8,128)(2,1)S(1)}, u32[]{:S(2)}, u32[]{:S(2)}) collective-permute-start(bf16[128,1024]{1,0:T(8,128)(2,1)S(1)} %pad_maximum_fusion.3), channel_id=1, source_target_pairs={{0,8},{1,17},{2,10},{3,19},{4,12},{5,21},{6,14},{7,23},{8,0},{9,25... | collective-permute-start | bytes 786440 | tf_op jit(solution)/shard_map/ppermute | solution.py:24
  24.8 8.5 %collective-permute-start.9 = (bf16[256,512]{1,0:T(8,128)(2,1)S(1)}, bf16[256,512]{1,0:T(8,128)(2,1)S(1)}, u32[]{:S(2)}, u32[]{:S(2)}) collective-permute-start(bf16[256,512]{1,0:T(8,128)(2,1)S(1)} %get-tuple-element.165), channel_id=1, source_target_pairs={{0,1},{1,0},{2,3},{3,2},{4,5},{5,4},{6,7},{7,6},{8,9},{9,8},{10,11... | collective-permute-start | bytes 786440 | tf_op jit(solution)/shard_map/ppermute | solution.py:24
  29.3 16.1 %collective-permute-start.13 = (bf16[256,1024]{1,0:T(8,128)(2,1)S(1)}, bf16[256,1024]{1,0:T(8,128)(2,1)S(1)}, u32[]{:S(2)}, u32[]{:S(2)}) collective-permute-start(bf16[256,1024]{1,0:T(8,128)(2,1)S(1)} %get-tuple-element.163), channel_id=1, source_target_pairs={{0,1},{1,0},{2,3},{3,2},{4,5},{5,4},{6,7},{7,6},{8,9},{9,8},{10,11... | collective-permute-start | bytes 1572872 | tf_op jit(solution)/shard_map/ppermute | solution.py:24
  31.0 13.8 %collective-permute-start.15 = (bf16[256,1024]{1,0:T(8,128)(2,1)S(1)}, bf16[256,1024]{1,0:T(8,128)(2,1)S(1)}, u32[]{:S(2)}, u32[]{:S(2)}) collective-permute-start(bf16[256,1024]{1,0:T(8,128)(2,1)S(1)} %pad_maximum_fusion.2.refs_3_), channel_id=1, source_target_pairs={{0,4},{1,9},{2,6},{3,11},{4,0},{5,13},{6,2},{7,15},{8,12},{9,1},{1... | collective-permute-start | bytes 1572872 | tf_op jit(solution)/shard_map/ppermute | solution.py:24
  32.6 12.2 %collective-permute-start.14 = (bf16[256,1024]{1,0:T(8,128)(2,1)S(1)}, bf16[256,1024]{1,0:T(8,128)(2,1)S(1)}, u32[]{:S(2)}, u32[]{:S(2)}) collective-permute-start(bf16[256,1024]{1,0:T(8,128)(2,1)S(1)} %pad_maximum_fusion.2.refs_3_), channel_id=1, source_target_pairs={{0,2},{1,5},{2,0},{3,7},{4,6},{5,1},{6,4},{7,3},{8,10},{9,13},{10,... | collective-permute-start | bytes 1572872 | tf_op jit(solution)/shard_map/ppermute | solution.py:24
  37.4 7.9 %collective-permute-start.12 = (bf16[512,512]{1,0:T(8,128)(2,1)S(1)}, bf16[512,512]{1,0:T(8,128)(2,1)S(1)}, u32[]{:S(2)}, u32[]{:S(2)}) collective-permute-start(bf16[512,512]{1,0:T(8,128)(2,1)S(1)} %get-tuple-element.98.refs_1_), channel_id=1, source_target_pairs={{0,1},{1,0},{2,3},{3,2},{4,5},{5,4},{6,7},{7,6},{8,9},{9,8},{10,11... | collective-permute-start | bytes 1572872 | tf_op jit(solution)/shard_map/ppermute | solution.py:24
  44.8 9.2 %collective-permute-start.16 = (bf16[256,1024]{1,0:T(8,128)(2,1)S(1)}, bf16[256,1024]{1,0:T(8,128)(2,1)S(1)}, u32[]{:S(2)}, u32[]{:S(2)}) collective-permute-start(bf16[256,1024]{1,0:T(8,128)(2,1)S(1)} %collective-permute-done.14.refs_4_), channel_id=1, source_target_pairs={{0,4},{1,9},{2,6},{3,11},{4,0},{5,13},{6,2},{7,15},{8,12},{9,1},{1... | collective-permute-start | bytes 1572872 | tf_op jit(solution)/shard_map/ppermute | solution.py:24
  56.0 9.2 %collective-permute-start.17 = (bf16[256,1024]{1,0:T(8,128)(2,1)S(1)}, bf16[256,1024]{1,0:T(8,128)(2,1)S(1)}, u32[]{:S(2)}, u32[]{:S(2)}) collective-permute-start(bf16[256,1024]{1,0:T(8,128)(2,1)S(1)} %get-tuple-element.103), channel_id=1, source_target_pairs={{0,4},{1,9},{2,6},{3,11},{4,0},{5,13},{6,2},{7,15},{8,12},{9,1},{1... | collective-permute-start | bytes 1572872 | tf_op jit(solution)/shard_map/ppermute | solution.py:24
  56.6 17.4 %collective-permute-start.19 = (bf16[256,1024]{1,0:T(8,128)(2,1)S(1)}, bf16[256,1024]{1,0:T(8,128)(2,1)S(1)}, u32[]{:S(2)}, u32[]{:S(2)}) collective-permute-start(bf16[256,1024]{1,0:T(8,128)(2,1)S(1)} %get-tuple-element.131), channel_id=1, source_target_pairs={{0,4},{1,9},{2,6},{3,11},{4,0},{5,13},{6,2},{7,15},{8,12},{9,1},{1... | collective-permute-start | bytes 1572872 | tf_op jit(solution)/shard_map/ppermute | solution.py:24
  65.5 9.2 %collective-permute-start.20 = (bf16[256,1024]{1,0:T(8,128)(2,1)S(1)}, bf16[256,1024]{1,0:T(8,128)(2,1)S(1)}, u32[]{:S(2)}, u32[]{:S(2)}) collective-permute-start(bf16[256,1024]{1,0:T(8,128)(2,1)S(1)} %add_convert_fusion.2), channel_id=1, source_target_pairs={{0,2},{1,5},{2,0},{3,7},{4,6},{5,1},{6,4},{7,3},{8,10},{9,13},{10,... | collective-permute-start | bytes 1572872 | tf_op jit(solution)/shard_map/ppermute | solution.py:24
  75.0 8.3 %collective-permute-start.23 = (bf16[2,384,512]{2,1,0:T(8,128)(2,1)S(1)}, bf16[2,384,512]{2,1,0:T(8,128)(2,1)S(1)}, u32[]{:S(2)}, u32[]{:S(2)}) collective-permute-start(bf16[2,384,512]{2,1,0:T(8,128)(2,1)S(1)} %get-tuple-element.142), channel_id=1, source_target_pairs={{0,1},{1,0},{2,3},{3,2},{4,5},{5,4},{6,7},{7,6},{8,9},{9,8},{10,11... | collective-permute-start | bytes 2359304 | tf_op jit(solution)/shard_map/ppermute | solution.py:24
  79.2 16.8 %collective-permute-start.25 = (bf16[2,128,512]{2,1,0:T(8,128)(2,1)S(1)}, bf16[2,128,512]{2,1,0:T(8,128)(2,1)S(1)}, u32[]{:S(2)}, u32[]{:S(2)}) collective-permute-start(bf16[2,128,512]{2,1,0:T(8,128)(2,1)S(1)} %get-tuple-element.145), channel_id=1, source_target_pairs={{0,2},{1,3},{2,0},{3,1},{4,6},{5,7},{6,4},{7,5},{8,10},{9,11},{10,... | collective-permute-start | bytes 786440 | tf_op jit(solution)/shard_map/ppermute | solution.py:24
  80.5 15.5 %collective-permute-start.27 = (bf16[2,128,512]{2,1,0:T(8,128)(2,1)S(1)}, bf16[2,128,512]{2,1,0:T(8,128)(2,1)S(1)}, u32[]{:S(2)}, u32[]{:S(2)}) collective-permute-start(bf16[2,128,512]{2,1,0:T(8,128)(2,1)S(1)} %get-tuple-element.147), channel_id=1, source_target_pairs={{0,4},{1,5},{2,6},{3,7},{4,0},{5,1},{6,2},{7,3},{8,12},{9,13},{10,... | collective-permute-start | bytes 786440 | tf_op jit(solution)/shard_map/ppermute | solution.py:24
  81.2 14.8 %collective-permute-start.28 = (bf16[2,128,512]{2,1,0:T(8,128)(2,1)S(1)}, bf16[2,128,512]{2,1,0:T(8,128)(2,1)S(1)}, u32[]{:S(2)}, u32[]{:S(2)}) collective-permute-start(bf16[2,128,512]{2,1,0:T(8,128)(2,1)S(1)} %get-tuple-element.148), channel_id=1, source_target_pairs={{0,6},{1,7},{2,4},{3,5},{4,2},{5,3},{6,0},{7,1},{8,14},{9,15},{10,... | collective-permute-start | bytes 786440 | tf_op jit(solution)/shard_map/ppermute | solution.py:24
  82.7 13.3 %collective-permute-start.24 = (bf16[128,1024]{1,0:T(8,128)(2,1)S(1)}, bf16[128,1024]{1,0:T(8,128)(2,1)S(1)}, u32[]{:S(2)}, u32[]{:S(2)}) collective-permute-start(bf16[128,1024]{1,0:T(8,128)(2,1)S(1)} %slice.16), channel_id=1, source_target_pairs={{0,8},{1,17},{2,10},{3,19},{4,12},{5,21},{6,14},{7,23},{8,0},{9,25... | collective-permute-start | bytes 786440 | tf_op jit(solution)/shard_map/ppermute | solution.py:24
  83.4 12.6 %collective-permute-start.26 = (bf16[2,64,512]{2,1,0:T(8,128)(2,1)S(1)}, bf16[2,64,512]{2,1,0:T(8,128)(2,1)S(1)}, u32[]{:S(2)}, u32[]{:S(2)}) collective-permute-start(bf16[2,64,512]{2,1,0:T(8,128)(2,1)S(1)} %get-tuple-element.146), channel_id=1, source_target_pairs={{0,2},{1,3},{2,0},{3,1},{4,6},{5,7},{6,4},{7,5},{8,10},{9,11},{10,... | collective-permute-start | bytes 393224 | tf_op jit(solution)/shard_map/ppermute | solution.py:24
  96.1 9.1 %collective-permute-start.29 = (bf16[64,1024]{1,0:T(8,128)(2,1)S(1)}, bf16[64,1024]{1,0:T(8,128)(2,1)}, u32[]{:S(2)}, u32[]{:S(2)}) collective-permute-start(bf16[64,1024]{1,0:T(8,128)(2,1)S(1)} %slice.19), channel_id=1, source_target_pairs={{0,16},{1,3},{2,18},{3,1},{4,20},{5,7},{6,22},{7,5},{8,24},{9,11},... | collective-permute-start | bytes 393224 | tf_op jit(solution)/shard_map/ppermute | solution.py:24
  99.3 8.8 %collective-permute-start.31 = (bf16[2,16,512]{2,1,0:T(8,128)(2,1)S(1)}, bf16[2,16,512]{2,1,0:T(8,128)(2,1)S(1)}, u32[]{:S(2)}, u32[]{:S(2)}) collective-permute-start(bf16[2,16,512]{2,1,0:T(8,128)(2,1)S(1)} %get-tuple-element.155), channel_id=1, source_target_pairs={{0,16},{1,17},{2,18},{3,19},{4,20},{5,21},{6,22},{7,23},{8,24},{9,... | collective-permute-start | bytes 98312 | tf_op jit(solution)/shard_map/ppermute | solution.py:24
  99.8 8.4 %collective-permute-start.32 = (bf16[2,16,512]{2,1,0:T(8,128)(2,1)S(1)}, bf16[2,16,512]{2,1,0:T(8,128)(2,1)S(1)}, u32[]{:S(2)}, u32[]{:S(2)}) collective-permute-start(bf16[2,16,512]{2,1,0:T(8,128)(2,1)S(1)} %get-tuple-element.156), channel_id=1, source_target_pairs={{0,24},{1,25},{2,26},{3,27},{4,28},{5,29},{6,30},{7,31},{8,16},{9,... | collective-permute-start | bytes 98312 | tf_op jit(solution)/shard_map/ppermute | solution.py:24
  (12 other events, 64.9 us)

commit v4 on v3

--- a/solution.py
+++ b/solution.py
@@ -149,17 +149,13 @@
 
 
 def backward_body(
-    parts, n_far, n_out, heads, meta, q_own, q_other, kv_own, kv_other, next_own, next_other, *refs
+    parts, n_far, meta, q_own, q_other, kv_own, kv_other, next_own, next_other, *refs
 ):
     far = [(refs[index], start, rows) for index, start, rows in parts]
-    d_keep, d_recv, probs_ref = refs[n_far : n_far + 3]
-    outs = refs[len(refs) - n_out :]
-    for previous, out in zip(refs[n_far + 3 : len(refs) - n_out], outs, strict=False):
-        out[..., : previous.shape[-1]] = previous[...]
-    dq_own, dq_other, near_own, near_other, *far_grads = outs
+    d_keep, d_recv, probs_ref, dq_own, dq_other, near_own, near_other, *far_grads = refs[n_far:]
     near_rows = kv_own.shape[1]
     after_next = near_rows + next_own.shape[1]
-    for head in heads:
+    for head in range(q_own.shape[1] // HS):
         at = slice(head * HS, (head + 1) * HS)
         keys, values = key_sets(kv_own, kv_other, next_own, next_other, far, at)
         grads = ([], [])
@@ -188,18 +184,23 @@
                 done += rows
 
 
-def pieces_of(quarters, piece):
-    return [(quarter, start) for quarter in quarters for start in range(0, quarter.shape[0], piece)]
-
-
-def rows_of_piece(meta, masks, index, piece):
-    owner = meta[1] ^ jnp.where(meta[0] == 0, masks[0][index], masks[1][index])
-    return pl.ds(pl.multiple_of(owner * piece, piece), piece)
-
-
-def ordered_weight(meta, quarters, scratch, piece, masks):
-    for index, (quarter, start) in enumerate(pieces_of(quarters, piece)):
-        scratch[rows_of_piece(meta, masks, index, piece), :] = quarter[start : start + piece, :]
+def pieces_of(parts, piece, masks, meta):
+    for half in range(2):
+        width = parts[0].shape[1]
+        columns = slice(half * width, (half + 1) * width)
+        index = 0
+        for part in parts[2 * half : 2 * half + 2]:
+            for start in range(0, part.shape[0], piece):
+                first, second = masks[half][0][index], masks[half][1][index]
+                owner = meta[1] ^ jnp.where(meta[0] == 0, first, second)
+                rows = pl.ds(pl.multiple_of(owner * piece, piece), piece)
+                yield part, slice(start, start + piece), rows, columns
+                index += 1
+
+
+def ordered_weight(meta, parts, scratch, piece, masks):
+    for part, there, rows, columns in pieces_of(parts, piece, masks, meta):
+        scratch[rows, columns] = part[there, :]
 
 
 def d_attn_body(piece, masks, meta, grad_own, grad_other, *refs):
@@ -238,8 +239,8 @@
         attn_theirs[:length], grad_other[...], TN
     )
     scratch[half_of(meta, width, False), :] = theirs.astype(BF16)
-    for index, (quarter, start) in enumerate(pieces_of(refs[:-1], piece)):
-        quarter[start : start + piece, :] = scratch[rows_of_piece(meta, masks, index, piece), :]
+    for part, there, rows, columns in pieces_of(refs[:-1], piece, masks, meta):
+        part[there, :] = scratch[rows, columns]
 
 
 def high_body(cuts, skips, meta, own, *refs):
@@ -315,13 +316,21 @@
     token_total = length * seq_count * queries.shape[0] * dp_count
 
     up = [1 << level for level in reversed(range(1, seq_levels))]
-    orders = (up[:-2] + [2, 4], [2] + up[:-3] + [4, 8])
-    stages = list(zip(*orders, strict=True))
     pieces = seq_count // 2
-    masks = [
-        [sum(m for s, m in enumerate(order) if index >> s & 1) // 2 for index in range(pieces)]
-        for order in orders
-    ]
+
+    def halves_of(orders):
+        both = [orders, [order[:-2] + order[:-3:-1] for order in orders]]
+        masks = [
+            [
+                [sum(m for s, m in enumerate(order) if index >> s & 1) // 2 for index in range(pieces)]
+                for order in one
+            ]
+            for one in both
+        ]
+        return [list(zip(*one, strict=True)) for one in both], masks
+
+    stages, masks = halves_of([up[:-2] + [2, 4], [2] + up[:-3] + [4, 8]])
+    sum_stages, sum_masks = halves_of([up[:-3] + [4, 8, 2], [2] + up[:-3] + [8, 4]])
     meta = jnp.stack([bit, pair]).astype(jnp.int32)
 
     query = queries[0]
@@ -355,7 +364,7 @@
         jnp.concatenate([w_mine, w_theirs], axis=0),
         jnp.concatenate([w_theirs, w_mine], axis=0),
     )
-    w_received = permute(w_rows, stages[0])
+    w_received = permute(w_rows, stages[0][0])
     far_masks = [(h, (1 << h) + (low << 3)) for h in range(3, seq_levels) for low in range(1 << (h - 3))]
     high_parts = [swap(coarse[h], mask) for h, mask in far_masks]
     first_panel = swap(coarse[1], 2)
@@ -366,7 +375,7 @@
     high = jnp.concatenate(high_parts, axis=1)
     second = jnp.concatenate([coarse[2], high], axis=1)
     panels = [high, first_panel, swap(high, 2), swap(second, 4), swap(second, 6)]
-    for stage in stages[1:-2]:
+    for stage in stages[0][1:-2]:
         w_rows = jnp.concatenate([w_rows, w_received], axis=0)
         w_received = permute(w_rows, stage)
     query, grad = lax.optimization_barrier((query, grad, high))[:2]
@@ -378,33 +387,40 @@
     parts = ((1, 0, coarse[1].shape[1]), (3, 0, n_second), (4, 0, n_second))
     parts += ((0, 0, n_high), (2, 0, n_high), (3, n_second, n_high), (4, n_second, n_high))
 
-    w_rows = jnp.concatenate([w_rows, after(w_received, panels[2])], axis=0)
-    w_received = permute(w_rows, stages[-2])
-    w_last = permute(w_rows, stages[-1])
+    w_received = after(w_received, panels[2])
+    w_width = cols // 2
+    w_rows = [
+        jnp.concatenate([rows[:, start : start + w_width] for rows in (w_rows, w_received)], axis=0)
+        for start in (0, w_width)
+    ]
+    w_received = [permute(rows, order[-2]) for rows, order in zip(w_rows, stages, strict=True)]
 
     key_count = length + length // 2 + sum(rows for _, _, rows in parts)
     att_ops = (q_own, q_other, kv_own, kv_other, next_own, next_other, *panels)
     attn_mine, probs = call(
         lambda *refs: forward_body(parts, *refs),
-        after(meta, w_rows),
+        after(meta, *w_rows),
         att_ops,
         [struct(2 * length, half, BF16), jax.ShapeDtypeStruct((2 * heads, key_count, length), BF16)],
         flops=32 * 2 * length * key_count * half,
     )
 
-    w_received, w_last, _ = lax.optimization_barrier((w_received, w_last, attn_mine))
-    quarters = (w_rows, w_received, w_last, permute(w_received, stages[-1]))
+    w_received = lax.optimization_barrier((*w_received, attn_mine))[:2]
+    w_rows = [jnp.concatenate(rows, axis=0) for rows in zip(w_rows, w_received, strict=True)]
+    w_received = [permute(rows, order[-1]) for rows, order in zip(w_rows, stages, strict=True)]
+    quarters = (w_rows[0], w_received[0], w_rows[1], w_received[1])
     attn_theirs = swap(attn_mine, 1)
 
     scratch = [pltpu.VMEM((pieces * piece, cols), BF16)]
     wg = call(
-        lambda *refs: weight_grad_body(piece, masks, *refs),
+        lambda *refs: weight_grad_body(piece, sum_masks, *refs),
         meta,
         (attn_mine, attn_theirs, g_own, g_other),
-        [struct(pieces * piece // 4, cols, BF16)] * 4,
+        [struct(pieces * piece // 2, w_width, BF16)] * 4,
         scratch,
     )
-    wg_received = [permute(after(part, quarters[3]), stages[-1]) for part in (wg[3], wg[2])]
+    wg_send = lax.optimization_barrier((wg[1], wg[3], *w_received))[:2]
+    wg_received = [permute(part, order[-1]) for part, order in zip(wg_send, sum_stages, strict=True)]
 
     d_keep, d_send = call(
         lambda *refs: d_attn_body(piece, masks, *refs),
@@ -415,39 +431,34 @@
     )
     d_recv = swap(d_send, 1)
 
+    back_ops = att_ops + (d_keep, d_recv, probs)
+
+    near_count = length + length // 2
+    grad_shapes = [q_half, q_half, planes(near_count, half, F32), planes(near_count, half, BF16)]
+    grad_shapes += [planes(p.shape[1], half, BF16) for p in panels]
+    grads = call(
+        lambda *refs: backward_body(parts, len(panels), *refs),
+        meta,
+        att_ops + (d_keep, d_recv, probs),
+        grad_shapes,
+    )
+    dq_keep, dq_send, near_keep, near_send, high_own, first_grad, *rest = grads
+
+    back = [swap(part, mask) for part, mask in zip(rest, (2, 4, 6), strict=True)]
+    first_back = swap(first_grad, 2)
+
     def add(kept, received):
         return (kept.astype(F32) + received.astype(F32)).astype(BF16)
 
-    back_ops = att_ops + (d_keep, d_recv, probs)
-
-    def backward(which, token, previous):
-        width = which[-1] * HS + HS
-        near_count = length + length // 2
-        shapes = [struct(length, width, BF16)] * 2
-        shapes += [planes(near_count, width, F32), planes(near_count, width, BF16)]
-        shapes += [planes(p.shape[1], width, BF16) for p in panels]
-        return call(
-            lambda *refs: backward_body(parts, len(panels), len(shapes), which, *refs),
-            token,
-            back_ops + tuple(previous),
-            shapes,
-        )
-
-    grads = backward(range(heads // 2), meta, ())
-    wg_send = add(wg[1], after(wg_received[0], grads[0]))
-    wg_step = permute(wg_send, stages[-2])
-    grads = backward(range(heads // 2, heads), after(meta, wg_send), grads)
-    wg_keep = add(wg[0], after(wg_received[1], grads[0]))
-    wg_total = add(wg_keep, wg_step)
-    wg_rows = wg_total.shape[0] // 2
-    wg_keep, wg_send = wg_total[:wg_rows], wg_total[wg_rows:]
-    grads = lax.optimization_barrier((*grads, wg_send))[: len(grads)]
-    dq_keep, dq_send, near_keep, near_send, high_own, first_grad, *rest = grads
-
-    back = [swap(part, mask) for part, mask in zip(rest, (2, 4, 6), strict=True)]
-    first_back = swap(first_grad, 2)
-    wg_received = permute(wg_send, stages[-3])
-    at_meta = after(meta, high_own)
+    def add_halves(kept, received):
+        total = add(kept, received)
+        rows = total.shape[0] // 2
+        return total[:rows], total[rows:]
+
+    wg_received = lax.optimization_barrier((*wg_received, back[0]))[:2]
+    wg_keep, wg_send = zip(*map(add_halves, (wg[0], wg[2]), wg_received), strict=True)
+    wg_received = [permute(part, order[-2]) for part, order in zip(wg_send, sum_stages, strict=True)]
+    at_meta = after(meta, *wg_send)
     near_recv = swap(near_send, 1)
     dq_recv = swap(dq_send, 1)
     base_k, base_v = call(near_body, meta, (near_keep, near_recv), [struct(length, inner, F32)] * 2)
@@ -459,32 +470,47 @@
         [g_half, g_half],
         scratch,
     )
+    first_back, *others = lax.optimization_barrier(
+        (first_back, *back, *wg_received, base_k, base_v, at_keep)
+    )
+    back, wg_received = others[: len(back)], others[len(back) : len(back) + 2]
+    wg_total = jnp.concatenate([add(*both) for both in zip(wg_keep, wg_received, strict=True)], axis=1)
+    wg_rows = wg_total.shape[0] // 2
+    wg_keep, wg_send = wg_total[:wg_rows], wg_total[wg_rows:]
+    wg_received = permute(wg_send, sum_stages[0][-3])
     grad_queries, attended = call(
         place_body,
         meta,
-        (dq_keep, dq_recv, at_keep, swap(at_send, 1)),
+        (dq_keep, dq_recv, at_keep, swap(after(at_send, wg_total), 1)),
         [struct(length, inner, BF16), struct(length, 2 * cols, BF16)],
         last=True,
     )
-
-    wg_received, first_back, *back = lax.optimization_barrier(
-        (wg_received, first_back, *back, base_k, base_v, attended, grad_queries)
-    )[: 2 + len(back)]
-    wg_total = add(wg_keep, wg_received)
-    wg_rows = wg_total.shape[0] // 2
-    wg_keep, wg_send = wg_total[:wg_rows], wg_total[wg_rows:]
-    wg_received = permute(wg_send, stages[-4])
     cuts = [coarse[h].shape[1] for h, _ in far_masks]
     high_shapes = [planes(rows, half, BF16) for rows in cuts]
     high_sums = call(
         lambda *refs: high_body(cuts, (0, n_second, n_second), *refs),
-        after(meta, wg_send),
+        meta,
         (high_own, *back),
         high_shapes,
     )
     by_level = {1: [first_back], 2: back[1:]}
-    for (h, mask), part in zip(far_masks, high_sums, strict=True):
-        by_level.setdefault(h, []).append(swap(part, mask))
+    high_back = [swap(part, mask) for (_, mask), part in zip(far_masks, high_sums, strict=True)]
+    *high_back, wg_received = lax.optimization_barrier((*high_back, wg_received))
+    wg_keep, wg_send = add_halves(wg_keep, wg_received)
+    wg_received = permute(wg_send, sum_stages[0][-4])
+    for (h, _), part in zip(far_masks, high_back, strict=True):
+        by_level.setdefault(h, []).append(part)
+    levels = list(reversed(range(1, seq_levels)))
+    received = [part for h in levels for part in by_level[h]]
+    counts = [len(by_level[h]) for h in levels]
+    up_rows = coarse[1].shape[1] // 2
+    up_keep, up_send = call(
+        lambda *refs: cascade_body(counts, *refs),
+        after(meta, wg_send),
+        received,
+        [planes(up_rows, half, F32), planes(up_rows, half, BF16)],
+    )
+    wg_received = after(wg_received, up_keep, attended)
     total = wg_keep.astype(F32) + wg_received.astype(F32)
     rows = piece // 2
     wg_mine = lax.dynamic_slice_in_dim(total, bit * rows, rows, 0)
@@ -500,17 +526,6 @@
             weight_grad.astype(BF16), "dp", scatter_dimension=1, tiled=True
         ).astype(F32)
     weight_grad = weight_grad * (1.0 / math.sqrt(token_total))
-
-    levels = list(reversed(range(1, seq_levels)))
-    received = [part for h in levels for part in by_level[h]]
-    counts = [len(by_level[h]) for h in levels]
-    up_rows = coarse[1].shape[1] // 2
-    up_keep, up_send = call(
-        lambda *refs: cascade_body(counts, *refs),
-        after(meta, weight_grad),
-        received,
-        [planes(up_rows, half, F32), planes(up_rows, half, BF16)],
-    )
     grad_keys, grad_values = call(
         finish_body,
         meta,

time: 113 us -> 108 us (0.956)
  waiting for transfers between devices: 43.1 us -> 32 us
  starting transfers between devices: 36 us -> 39.2 us
  local copies, waits for them, and re-layouts: 4.11 us -> 6.35 us
    ppermute x35 -> x37, waiting for transfers between devices: 43.1 us -> 32 us  [permute(): lax.ppermute(value, 'seq', [(i, i ^ masks[i & 1]) for i in range(count)])]
    ppermute x35 -> x37, starting transfers between devices: 36 us -> 39.2 us  [permute(): lax.ppermute(value, 'seq', [(i, i ^ masks[i & 1]) for i in range(count)])]
    unnamed x5 -> x11, local copies, waits for them, and re-layouts: 0.03 us -> 1.68 us
    pallas_call x12 -> x11, Pallas kernels: 26.2 us -> 26.4 us  [call(): pl.pallas_call(body, grid=(1,) if last else (), in_specs=[pl.BlockSpec(me...]
  transfers between devices with their start and end apart: 35 -> 37, of which waited for: 14 -> 13; matrix products, arithmetic and copies ran while one was open for 4% -> 5% of each run, Pallas kernels for 19% -> 23%
where the time goes in v4:
time: 108 us; the launch traced here: 107 us
  starting transfers between devices  39.2 us (36%)
  waiting for transfers between devices  32 us (30%)
  Pallas kernels  26.4 us (24%)
  local copies, waits for them, and re-layouts  6.35 us (6%)
  other arithmetic  2.59 us (2%)
    ppermute x37, starting transfers between devices, permute(): lax.ppermute(value, 'seq', [(i, i ^ masks[i & 1]) for i in range(count)])  39.2 us
    ppermute x37, waiting for transfers between devices, permute(): lax.ppermute(value, 'seq', [(i, i ^ masks[i & 1]) for i in range(count)])  32 us
    pallas_call x11, Pallas kernels, call(): pl.pallas_call(body, grid=(1,) if last else (), in_specs=[pl.BlockSpec(me...  26.4 us
    dynamic_slice x4, local copies, waits for them, and re-layouts, part(): return lax.dynamic_slice_in_dim(array, which * width, width, 1)  3.92 us
  transfers between devices with their start and end apart: 37, of which 13 were waited for; matrix products, arithmetic and copies ran while one was open for 5% of the time, Pallas kernels for 23%

profile of v4, /device:TPU:0, one launch (start us, length us, event | category | flops | bytes accessed | tf_op | source)
XLA Modules:
  0.0 107.5 jit_solution(2665337784502107141)
XLA Ops:
  5.7 2.9 %collective-permute-start.3 = (bf16[2,128,512]{2,1,0:T(8,128)(2,1)S(1)}, bf16[2,128,512]{2,1,0:T(8,128)(2,1)S(1)}, u32[]{:S(2)}, u32[]{:S(2)}) collective-permute-start(bf16[2,128,512]{2,1,0:T(8,128)(2,1)S(1)} %get-tuple-element.71), channel_id=1, source_target_pairs={{0,2},{1,3},{2,0},{3,1},{4,6},{5,7},{6,4},{7,5},{8,10},{9,11},{10,... | collective-permute-start | bytes 786440 | tf_op jit(solution)/shard_map/ppermute | solution.py:24
  8.6 2.6 %collective-permute-start.1 = (bf16[64,1024]{1,0:T(8,128)(2,1)S(1)}, bf16[64,1024]{1,0:T(8,128)(2,1)S(1)}, u32[]{:S(2)}, u32[]{:S(2)}) collective-permute-start(bf16[64,1024]{1,0:T(8,128)(2,1)S(1)} %maximum_select_fusion.1), channel_id=1, source_target_pairs={{0,16},{1,3},{2,18},{3,1},{4,20},{5,7},{6,22},{7,5},{8,24},{9,11},... | collective-permute-start | bytes 393224 | tf_op jit(solution)/shard_map/ppermute | solution.py:24
  12.6 1.7 %collective-permute-start.5 = (bf16[2,16,512]{2,1,0:T(8,128)(2,1)S(1)}, bf16[2,16,512]{2,1,0:T(8,128)(2,1)S(1)}, u32[]{:S(2)}, u32[]{:S(2)}) collective-permute-start(bf16[2,16,512]{2,1,0:T(8,128)(2,1)S(1)} %get-tuple-element.73), channel_id=1, source_target_pairs={{0,16},{1,17},{2,18},{3,19},{4,20},{5,21},{6,22},{7,23},{8,24},{9,... | collective-permute-start | bytes 98312 | tf_op jit(solution)/shard_map/ppermute | solution.py:24
  15.6 1.9 %collective-permute-done.1 = bf16[64,1024]{1,0:T(8,128)(2,1)S(1)} collective-permute-done((bf16[64,1024]{1,0:T(8,128)(2,1)S(1)}, bf16[64,1024]{1,0:T(8,128)(2,1)S(1)}, u32[]{:S(2)}, u32[]{:S(2)}) %collective-permute-start.1) | collective-permute-done | bytes 131104 | tf_op jit(solution)/shard_map/ppermute | solution.py:24
  18.9 1.7 %collective-permute-start.10 = (bf16[2,128,512]{2,1,0:T(8,128)(2,1)S(1)}, bf16[2,128,512]{2,1,0:T(8,128)(2,1)S(1)}, u32[]{:S(2)}, u32[]{:S(2)}) collective-permute-start(bf16[2,128,512]{2,1,0:T(8,128)(2,1)S(1)} %get-tuple-element.153), channel_id=1, source_target_pairs={{0,6},{1,7},{2,4},{3,5},{4,2},{5,3},{6,0},{7,1},{8,14},{9,15},{10,... | collective-permute-start | bytes 786440 | tf_op jit(solution)/shard_map/ppermute | solution.py:24
  24.9 4.4 %collective-permute-done.8.refs_9_ = bf16[2,64,512]{2,1,0:T(8,128)(2,1)S(1)} collective-permute-done((bf16[2,64,512]{2,1,0:T(8,128)(2,1)S(1)}, bf16[2,64,512]{2,1,0:T(8,128)(2,1)S(1)}, u32[]{:S(2)}, u32[]{:S(2)}) %collective-permute-start.8) | collective-permute-done | bytes 131104 | tf_op jit(solution)/shard_map/ppermute | solution.py:24
  31.4 1.9 %collective-permute-start.15 = (bf16[256,512]{1,0:T(8,128)(2,1)S(1)}, bf16[256,512]{1,0:T(8,128)(2,1)S(1)}, u32[]{:S(2)}, u32[]{:S(2)}) collective-permute-start(bf16[256,512]{1,0:T(8,128)(2,1)S(1)} %pad_maximum_fusion.7), channel_id=1, source_target_pairs={{0,4},{1,9},{2,6},{3,11},{4,0},{5,13},{6,2},{7,15},{8,12},{9,1},{1... | collective-permute-start | bytes 786440 | tf_op jit(solution)/shard_map/ppermute | solution.py:24
  33.3 4.2 %shard_map.93 = (bf16[512,512]{1,0:T(8,128)(2,1)S(1)}, bf16[8,896,256]{2,1,0:T(8,128)(2,1)S(1)}) custom-call(s32[2]{0:T(128)S(1)} %pad_add_fusion.meta.refs_0_, bf16[256,512]{1,0:T(8,128)(2,1)S(1)} %get-tuple-element.140.refs_1_, bf16[256,512]{1,0:T(8,128)(2,1)S(1)} %collective-permute-done.7.refs_2_, ...), custom_call_target="tpu_custom_call" | custom-call | flops 7516192768 | tf_op jit(solution)/shard_map/pallas_call | solution.py:41
  41.2 2.0 %shard_map.94 = (bf16[512,512]{1,0:T(8,128)(2,1)S(1)}, bf16[512,512]{1,0:T(8,128)(2,1)S(1)}, bf16[512,512]{1,0:T(8,128)(2,1)S(1)}, bf16[512,512]{1,0:T(8,128)(2,1)S(1)}) custom-call(s32[2]{0:T(128)S(1)} %pad_add_fusion.meta.refs_0_, bf16[512,512]{1,0:T(8,128)(2,1)S(1)} %get-tuple-element.85.refs_1_, bf16[512,512]{1,0:T(8,128)(2,1)S(1)} %collective-permute-done.12.refs_2_, ...), custom_call_target="tpu_custom_call" | custom-call | tf_op jit(solution)/shard_map/pallas_call | solution.py:41
  43.1 4.3 %collective-permute-done.17.refs_6_ = bf16[512,512]{1,0:T(8,128)(2,1)S(1)} collective-permute-done((bf16[512,512]{1,0:T(8,128)(2,1)S(1)}, bf16[512,512]{1,0:T(8,128)(2,1)S(1)}, u32[]{:S(2)}, u32[]{:S(2)}) %collective-permute-start.17) | collective-permute-done | bytes 524320 | tf_op jit(solution)/shard_map/ppermute | solution.py:24
  47.5 4.7 %collective-permute-done.16.refs_4_ = bf16[512,512]{1,0:T(8,128)(2,1)S(1)} collective-permute-done((bf16[512,512]{1,0:T(8,128)(2,1)S(1)}, bf16[512,512]{1,0:T(8,128)(2,1)S(1)}, u32[]{:S(2)}, u32[]{:S(2)}) %collective-permute-start.16) | collective-permute-done | bytes 524320 | tf_op jit(solution)/shard_map/ppermute | solution.py:24
  52.1 2.0 %shard_map.95 = (f32[512,512]{1,0:T(8,128)S(1)}, bf16[512,512]{1,0:T(8,128)(2,1)S(1)}) custom-call(s32[2]{0:T(128)S(1)} %pad_add_fusion.meta.refs_0_, bf16[256,1024]{1,0:T(8,128)(2,1)S(1)} %get-tuple-element.138.refs_3_.refs_1_, bf16[256,1024]{1,0:T(8,128)(2,1)S(1)} %collective-permute-done.13.refs_4_.refs_2_, ...), custom_call_target="tpu_custom_call" | custom-call | tf_op jit(solution)/shard_map/pallas_call | solution.py:41
  56.1 7.4 %shard_map.96 = (bf16[256,512]{1,0:T(8,128)(2,1)S(1)}, bf16[256,512]{1,0:T(8,128)(2,1)}, f32[2,384,512]{2,1,0:T(8,128)S(1)}, bf16[2,384,512]{2,1,0:T(8,128)(2,1)...) custom-call(s32[2]{0:T(128)S(1)} %pad_add_fusion.meta.refs_0_, ...), custom_call_target="tpu_custom_call" | custom-call | tf_op jit(solution)/shard_map/pallas_call | solution.py:41
  66.1 2.4 %collective-permute-done.21 = bf16[512,512]{1,0:T(8,128)(2,1)S(1)} collective-permute-done((bf16[512,512]{1,0:T(8,128)(2,1)S(1)}, bf16[512,512]{1,0:T(8,128)(2,1)S(1)}, u32[]{:S(2)}, u32[]{:S(2)}) %collective-permute-start.21) | collective-permute-done | bytes 524320 | tf_op jit(solution)/shard_map/ppermute | solution.py:24
  68.6 2.1 %collective-permute-start.25 = (bf16[2,128,512]{2,1,0:T(8,128)(2,1)S(1)}, bf16[2,128,512]{2,1,0:T(8,128)(2,1)S(1)}, u32[]{:S(2)}, u32[]{:S(2)}) collective-permute-start(bf16[2,128,512]{2,1,0:T(8,128)(2,1)S(1)} %get-tuple-element.109), channel_id=1, source_target_pairs={{0,6},{1,7},{2,4},{3,5},{4,2},{5,3},{6,0},{7,1},{8,14},{9,15},{10,... | collective-permute-start | bytes 786440 | tf_op jit(solution)/shard_map/ppermute | solution.py:24
  72.7 2.3 %shard_map.97 = (bf16[256,1024]{1,0:T(8,128)(2,1)S(1)}, bf16[256,1024]{1,0:T(8,128)(2,1)}) custom-call(s32[2]{0:T(128)S(1)} %pad_add_fusion.meta.refs_0_, bf16[512,512]{1,0:T(8,128)(2,1)S(1)} %get-tuple-element.85.refs_1_, bf16[512,512]{1,0:T(8,128)(2,1)S(1)} %collective-permute-done.12.refs_2_, bf16[512,512]{1,0:T(8,128)(2,1)S(1)} %pad_maximum_fusion.3.refs_3_, ...), custom_call_target="tpu_custom_call" | custom-call | tf_op jit(solution)/shard_map/pallas_call | solution.py:41
  76.1 4.7 %collective-permute-done.25.refs_4_.refs_5_ = bf16[2,128,512]{2,1,0:T(8,128)(2,1)S(1)} collective-permute-done((bf16[2,128,512]{2,1,0:T(8,128)(2,1)S(1)}, bf16[2,128,512]{2,1,0:T(8,128)(2,1)S(1)}, u32[]{:S(2)}, u32[]{:S(2)}) %collective-permute-start.25) | collective-permute-done | bytes 262176 | tf_op jit(solution)/shard_map/ppermute | solution.py:24
  80.8 2.8 %collective-permute-done.27 = bf16[256,512]{1,0:T(8,128)(2,1)S(1)} collective-permute-done((bf16[256,512]{1,0:T(8,128)(2,1)S(1)}, bf16[256,512]{1,0:T(8,128)(2,1)S(1)}, u32[]{:S(2)}, u32[]{:S(2)}) %collective-permute-start.27) | collective-permute-done | bytes 262176 | tf_op jit(solution)/shard_map/ppermute | solution.py:24
  87.2 2.1 %collective-permute-start.31 = (bf16[2,16,512]{2,1,0:T(8,128)(2,1)S(1)}, bf16[2,16,512]{2,1,0:T(8,128)(2,1)S(1)}, u32[]{:S(2)}, u32[]{:S(2)}) collective-permute-start(bf16[2,16,512]{2,1,0:T(8,128)(2,1)S(1)} %get-tuple-element.124), channel_id=1, source_target_pairs={{0,16},{1,17},{2,18},{3,19},{4,20},{5,21},{6,22},{7,23},{8,24},{9,... | collective-permute-start | bytes 98312 | tf_op jit(solution)/shard_map/ppermute | solution.py:24
  89.2 1.6 %collective-permute-start.32 = (bf16[2,16,512]{2,1,0:T(8,128)(2,1)S(1)}, bf16[2,16,512]{2,1,0:T(8,128)(2,1)S(1)}, u32[]{:S(2)}, u32[]{:S(2)}) collective-permute-start(bf16[2,16,512]{2,1,0:T(8,128)(2,1)S(1)} %get-tuple-element.125), channel_id=1, source_target_pairs={{0,24},{1,25},{2,26},{3,27},{4,28},{5,29},{6,30},{7,31},{8,16},{9,... | collective-permute-start | bytes 98312 | tf_op jit(solution)/shard_map/ppermute | solution.py:24
  90.9 1.9 %collective-permute-done.31.refs_1_ = bf16[2,16,512]{2,1,0:T(8,128)(2,1)S(1)} collective-permute-done((bf16[2,16,512]{2,1,0:T(8,128)(2,1)S(1)}, bf16[2,16,512]{2,1,0:T(8,128)(2,1)S(1)}, u32[]{:S(2)}, u32[]{:S(2)}) %collective-permute-start.31) | collective-permute-done | bytes 32800 | tf_op jit(solution)/shard_map/ppermute | solution.py:24
  92.7 2.3 %collective-permute-start.19 = (bf16[256,512]{1,0:T(8,128)(2,1)}, bf16[256,512]{1,0:T(8,128)(2,1)}, u32[]{:S(2)}, u32[]{:S(2)}) collective-permute-start(bf16[256,512]{1,0:T(8,128)(2,1)} %get-tuple-element.95), channel_id=1, source_target_pairs={{0,1},{1,0},{2,3},{3,2},{4,5},{5,4},{6,7},{7,6},{8,9},{9,8},{10,11... | collective-permute-start | bytes 786440 | tf_op jit(solution)/shard_map/ppermute | solution.py:24
  98.8 2.4 %shard_map.99 = (bf16[256,1024]{1,0:T(8,128)(2,1)}, bf16[256,2048]{1,0:T(8,128)(2,1)}) custom-call(s32[2]{0:T(128)S(1)} %pad_add_fusion.meta.refs_0_, bf16[256,512]{1,0:T(8,128)(2,1)S(1)} %copy-done.1, bf16[256,512]{1,0:T(8,128)(2,1)} %collective-permute-done.19.refs_1_, bf16[256,1024]{1,0:T(8,128)(2,1)S(1)} %get-tuple-element.105.refs_2_, ...), custom_call_target="tpu_custom_call" | custom-call | tf_op jit(solution)/shard_map/pallas_call | solution.py:41
  104.8 1.9 %shard_map.102 = (bf16[256,1024]{1,0:T(8,128)(2,1)}, bf16[256,1024]{1,0:T(8,128)(2,1)}) custom-call(s32[2]{0:T(128)S(1)} %pad_add_fusion.meta.refs_0_, f32[256,1024]{1,0:T(8,128)S(1)} %get-tuple-element.112.base_k, f32[256,1024]{1,0:T(8,128)S(1)} %get-tuple-element.113.base_v, f32[2,64,512]{2,1,0:T(8,128)S(1)} %get-tuple-element.132.up_keep, ...), custom_call_target="tpu_custom_call" | custom-call | tf_op jit(solution)/shard_map/pallas_call | solution.py:41
  (102 shorter events, 38.3 us)
Async XLA Ops:
  5.7 13.2 %collective-permute-start.3 = (bf16[2,128,512]{2,1,0:T(8,128)(2,1)S(1)}, bf16[2,128,512]{2,1,0:T(8,128)(2,1)S(1)}, u32[]{:S(2)}, u32[]{:S(2)}) collective-permute-start(bf16[2,128,512]{2,1,0:T(8,128)(2,1)S(1)} %get-tuple-element.71), channel_id=1, source_target_pairs={{0,2},{1,3},{2,0},{3,1},{4,6},{5,7},{6,4},{7,5},{8,10},{9,11},{10,... | collective-permute-start | bytes 786440 | tf_op jit(solution)/shard_map/ppermute | solution.py:24
  8.6 8.9 %collective-permute-start.1 = (bf16[64,1024]{1,0:T(8,128)(2,1)S(1)}, bf16[64,1024]{1,0:T(8,128)(2,1)S(1)}, u32[]{:S(2)}, u32[]{:S(2)}) collective-permute-start(bf16[64,1024]{1,0:T(8,128)(2,1)S(1)} %maximum_select_fusion.1), channel_id=1, source_target_pairs={{0,16},{1,3},{2,18},{3,1},{4,20},{5,7},{6,22},{7,5},{8,24},{9,11},... | collective-permute-start | bytes 393224 | tf_op jit(solution)/shard_map/ppermute | solution.py:24
  18.9 12.4 %collective-permute-start.10 = (bf16[2,128,512]{2,1,0:T(8,128)(2,1)S(1)}, bf16[2,128,512]{2,1,0:T(8,128)(2,1)S(1)}, u32[]{:S(2)}, u32[]{:S(2)}) collective-permute-start(bf16[2,128,512]{2,1,0:T(8,128)(2,1)S(1)} %get-tuple-element.153), channel_id=1, source_target_pairs={{0,6},{1,7},{2,4},{3,5},{4,2},{5,3},{6,0},{7,1},{8,14},{9,15},{10,... | collective-permute-start | bytes 786440 | tf_op jit(solution)/shard_map/ppermute | solution.py:24
  20.7 12.6 %collective-permute-start.9 = (bf16[2,128,512]{2,1,0:T(8,128)(2,1)S(1)}, bf16[2,128,512]{2,1,0:T(8,128)(2,1)S(1)}, u32[]{:S(2)}, u32[]{:S(2)}) collective-permute-start(bf16[2,128,512]{2,1,0:T(8,128)(2,1)S(1)} %get-tuple-element.153), channel_id=1, source_target_pairs={{0,4},{1,5},{2,6},{3,7},{4,0},{5,1},{6,2},{7,3},{8,12},{9,13},{10,... | collective-permute-start | bytes 786440 | tf_op jit(solution)/shard_map/ppermute | solution.py:24
  21.1 8.2 %collective-permute-start.8 = (bf16[2,64,512]{2,1,0:T(8,128)(2,1)S(1)}, bf16[2,64,512]{2,1,0:T(8,128)(2,1)S(1)}, u32[]{:S(2)}, u32[]{:S(2)}) collective-permute-start(bf16[2,64,512]{2,1,0:T(8,128)(2,1)S(1)} %get-tuple-element.154.refs_7_), channel_id=1, source_target_pairs={{0,2},{1,3},{2,0},{3,1},{4,6},{5,7},{6,4},{7,5},{8,10},{9,11},{10,... | collective-permute-start | bytes 393224 | tf_op jit(solution)/shard_map/ppermute | solution.py:24
  22.5 8.3 %collective-permute-start.11 = (bf16[128,1024]{1,0:T(8,128)(2,1)S(1)}, bf16[128,1024]{1,0:T(8,128)(2,1)S(1)}, u32[]{:S(2)}, u32[]{:S(2)}) collective-permute-start(bf16[128,1024]{1,0:T(8,128)(2,1)S(1)} %pad_maximum_fusion.5), channel_id=1, source_target_pairs={{0,8},{1,17},{2,10},{3,19},{4,12},{5,21},{6,14},{7,23},{8,0},{9,25... | collective-permute-start | bytes 786440 | tf_op jit(solution)/shard_map/ppermute | solution.py:24
  24.7 8.7 %collective-permute-start.7 = (bf16[256,512]{1,0:T(8,128)(2,1)S(1)}, bf16[256,512]{1,0:T(8,128)(2,1)S(1)}, u32[]{:S(2)}, u32[]{:S(2)}) collective-permute-start(bf16[256,512]{1,0:T(8,128)(2,1)S(1)} %get-tuple-element.139), channel_id=1, source_target_pairs={{0,1},{1,0},{2,3},{3,2},{4,5},{5,4},{6,7},{7,6},{8,9},{9,8},{10,11... | collective-permute-start | bytes 786440 | tf_op jit(solution)/shard_map/ppermute | solution.py:24
  29.3 11.9 %collective-permute-start.13 = (bf16[256,1024]{1,0:T(8,128)(2,1)S(1)}, bf16[256,1024]{1,0:T(8,128)(2,1)S(1)}, u32[]{:S(2)}, u32[]{:S(2)}) collective-permute-start(bf16[256,1024]{1,0:T(8,128)(2,1)S(1)} %get-tuple-element.137), channel_id=1, source_target_pairs={{0,1},{1,0},{2,3},{3,2},{4,5},{5,4},{6,7},{7,6},{8,9},{9,8},{10,11... | collective-permute-start | bytes 1572872 | tf_op jit(solution)/shard_map/ppermute | solution.py:24
  30.9 6.7 %collective-permute-start.14 = (bf16[256,512]{1,0:T(8,128)(2,1)S(1)}, bf16[256,512]{1,0:T(8,128)(2,1)S(1)}, u32[]{:S(2)}, u32[]{:S(2)}) collective-permute-start(bf16[256,512]{1,0:T(8,128)(2,1)S(1)} %pad_maximum_fusion.6), channel_id=1, source_target_pairs={{0,2},{1,5},{2,0},{3,7},{4,6},{5,1},{6,4},{7,3},{8,10},{9,13},{10,... | collective-permute-start | bytes 786440 | tf_op jit(solution)/shard_map/ppermute | solution.py:24
  38.2 9.2 %collective-permute-start.17 = (bf16[512,512]{1,0:T(8,128)(2,1)S(1)}, bf16[512,512]{1,0:T(8,128)(2,1)S(1)}, u32[]{:S(2)}, u32[]{:S(2)}) collective-permute-start(bf16[512,512]{1,0:T(8,128)(2,1)S(1)} %pad_maximum_fusion.4.refs_5_), channel_id=1, source_target_pairs={{0,2},{1,5},{2,0},{3,7},{4,6},{5,1},{6,4},{7,3},{8,10},{9,13},{10,... | collective-permute-start | bytes 1572872 | tf_op jit(solution)/shard_map/ppermute | solution.py:24
  39.8 12.4 %collective-permute-start.16 = (bf16[512,512]{1,0:T(8,128)(2,1)S(1)}, bf16[512,512]{1,0:T(8,128)(2,1)S(1)}, u32[]{:S(2)}, u32[]{:S(2)}) collective-permute-start(bf16[512,512]{1,0:T(8,128)(2,1)S(1)} %pad_maximum_fusion.3.refs_3_), channel_id=1, source_target_pairs={{0,4},{1,9},{2,6},{3,11},{4,0},{5,13},{6,2},{7,15},{8,12},{9,1},{1... | collective-permute-start | bytes 1572872 | tf_op jit(solution)/shard_map/ppermute | solution.py:24
  54.2 11.5 %collective-permute-start.20 = (bf16[512,512]{1,0:T(8,128)(2,1)S(1)}, bf16[512,512]{1,0:T(8,128)(2,1)S(1)}, u32[]{:S(2)}, u32[]{:S(2)}) collective-permute-start(bf16[512,512]{1,0:T(8,128)(2,1)S(1)} %get-tuple-element.98), channel_id=1, source_target_pairs={{0,2},{1,5},{2,0},{3,7},{4,6},{5,1},{6,4},{7,3},{8,10},{9,13},{10,... | collective-permute-start | bytes 1572872 | tf_op jit(solution)/shard_map/ppermute | solution.py:24
  55.6 13.0 %collective-permute-start.21 = (bf16[512,512]{1,0:T(8,128)(2,1)S(1)}, bf16[512,512]{1,0:T(8,128)(2,1)S(1)}, u32[]{:S(2)}, u32[]{:S(2)}) collective-permute-start(bf16[512,512]{1,0:T(8,128)(2,1)S(1)} %get-tuple-element.99), channel_id=1, source_target_pairs={{0,8},{1,9},{2,10},{3,11},{4,12},{5,13},{6,14},{7,15},{8,0},{9,1},... | collective-permute-start | bytes 1572872 | tf_op jit(solution)/shard_map/ppermute | solution.py:24
  63.6 8.4 %collective-permute-start.28 = (bf16[2,384,512]{2,1,0:T(8,128)(2,1)S(1)}, bf16[2,384,512]{2,1,0:T(8,128)(2,1)S(1)}, u32[]{:S(2)}, u32[]{:S(2)}) collective-permute-start(bf16[2,384,512]{2,1,0:T(8,128)(2,1)S(1)} %get-tuple-element.111), channel_id=1, source_target_pairs={{0,1},{1,0},{2,3},{3,2},{4,5},{5,4},{6,7},{7,6},{8,9},{9,8},{10,11... | collective-permute-start | bytes 2359304 | tf_op jit(solution)/shard_map/ppermute | solution.py:24
  63.7 6.9 %collective-permute-start.22 = (bf16[2,64,512]{2,1,0:T(8,128)(2,1)S(1)}, bf16[2,64,512]{2,1,0:T(8,128)(2,1)S(1)}, u32[]{:S(2)}, u32[]{:S(2)}) collective-permute-start(bf16[2,64,512]{2,1,0:T(8,128)(2,1)S(1)} %get-tuple-element.100), channel_id=1, source_target_pairs={{0,2},{1,3},{2,0},{3,1},{4,6},{5,7},{6,4},{7,5},{8,10},{9,11},{10,... | collective-permute-start | bytes 393224 | tf_op jit(solution)/shard_map/ppermute | solution.py:24
  65.0 11.0 %collective-permute-start.23 = (bf16[2,128,512]{2,1,0:T(8,128)(2,1)S(1)}, bf16[2,128,512]{2,1,0:T(8,128)(2,1)S(1)}, u32[]{:S(2)}, u32[]{:S(2)}) collective-permute-start(bf16[2,128,512]{2,1,0:T(8,128)(2,1)S(1)} %get-tuple-element.107), channel_id=1, source_target_pairs={{0,2},{1,3},{2,0},{3,1},{4,6},{5,7},{6,4},{7,5},{8,10},{9,11},{10,... | collective-permute-start | bytes 786440 | tf_op jit(solution)/shard_map/ppermute | solution.py:24
  65.7 10.3 %collective-permute-start.24 = (bf16[2,128,512]{2,1,0:T(8,128)(2,1)S(1)}, bf16[2,128,512]{2,1,0:T(8,128)(2,1)S(1)}, u32[]{:S(2)}, u32[]{:S(2)}) collective-permute-start(bf16[2,128,512]{2,1,0:T(8,128)(2,1)S(1)} %get-tuple-element.108), channel_id=1, source_target_pairs={{0,4},{1,5},{2,6},{3,7},{4,0},{5,1},{6,2},{7,3},{8,12},{9,13},{10,... | collective-permute-start | bytes 786440 | tf_op jit(solution)/shard_map/ppermute | solution.py:24
  68.6 12.2 %collective-permute-start.25 = (bf16[2,128,512]{2,1,0:T(8,128)(2,1)S(1)}, bf16[2,128,512]{2,1,0:T(8,128)(2,1)S(1)}, u32[]{:S(2)}, u32[]{:S(2)}) collective-permute-start(bf16[2,128,512]{2,1,0:T(8,128)(2,1)S(1)} %get-tuple-element.109), channel_id=1, source_target_pairs={{0,6},{1,7},{2,4},{3,5},{4,2},{5,3},{6,0},{7,1},{8,14},{9,15},{10,... | collective-permute-start | bytes 786440 | tf_op jit(solution)/shard_map/ppermute | solution.py:24
  71.0 9.8 %collective-permute-start.26 = (bf16[256,512]{1,0:T(8,128)(2,1)S(1)}, bf16[256,512]{1,0:T(8,128)(2,1)S(1)}, u32[]{:S(2)}, u32[]{:S(2)}) collective-permute-start(bf16[256,512]{1,0:T(8,128)(2,1)S(1)} %slice.52), channel_id=1, source_target_pairs={{0,8},{1,9},{2,10},{3,11},{4,12},{5,13},{6,14},{7,15},{8,0},{9,1},... | collective-permute-start | bytes 786440 | tf_op jit(solution)/shard_map/ppermute | solution.py:24
  72.0 11.6 %collective-permute-start.27 = (bf16[256,512]{1,0:T(8,128)(2,1)S(1)}, bf16[256,512]{1,0:T(8,128)(2,1)S(1)}, u32[]{:S(2)}, u32[]{:S(2)}) collective-permute-start(bf16[256,512]{1,0:T(8,128)(2,1)S(1)} %slice.53), channel_id=1, source_target_pairs={{0,2},{1,5},{2,0},{3,7},{4,6},{5,1},{6,4},{7,3},{8,10},{9,13},{10,... | collective-permute-start | bytes 786440 | tf_op jit(solution)/shard_map/ppermute | solution.py:24
  83.8 11.3 %collective-permute-start.33 = (bf16[128,1024]{1,0:T(8,128)(2,1)S(1)}, bf16[128,1024]{1,0:T(8,128)(2,1)S(1)}, u32[]{:S(2)}, u32[]{:S(2)}) collective-permute-start(bf16[128,1024]{1,0:T(8,128)(2,1)S(1)} %fusion.1), channel_id=1, source_target_pairs={{0,4},{1,17},{2,6},{3,19},{4,0},{5,21},{6,2},{7,23},{8,12},{9,25},... | collective-permute-start | bytes 786440 | tf_op jit(solution)/shard_map/ppermute | solution.py:24
  84.3 13.5 %collective-permute-start.29 = (bf16[256,1024]{1,0:T(8,128)(2,1)}, bf16[256,1024]{1,0:T(8,128)(2,1)}, u32[]{:S(2)}, u32[]{:S(2)}) collective-permute-start(bf16[256,1024]{1,0:T(8,128)(2,1)} %get-tuple-element.116), channel_id=1, source_target_pairs={{0,1},{1,0},{2,3},{3,2},{4,5},{5,4},{6,7},{7,6},{8,9},{9,8},{10,11... | collective-permute-start | bytes 1572872 | tf_op jit(solution)/shard_map/ppermute | solution.py:24
  86.4 8.7 %collective-permute-start.30 = (bf16[2,32,512]{2,1,0:T(8,128)(2,1)S(1)}, bf16[2,32,512]{2,1,0:T(8,128)(2,1)S(1)}, u32[]{:S(2)}, u32[]{:S(2)}) collective-permute-start(bf16[2,32,512]{2,1,0:T(8,128)(2,1)S(1)} %get-tuple-element.123), channel_id=1, source_target_pairs={{0,8},{1,9},{2,10},{3,11},{4,12},{5,13},{6,14},{7,15},{8,0},{9,1},... | collective-permute-start | bytes 196616 | tf_op jit(solution)/shard_map/ppermute | solution.py:24
  96.5 7.2 %collective-permute-start.35 = (bf16[64,1024]{1,0:T(8,128)(2,1)}, bf16[64,1024]{1,0:T(8,128)(2,1)}, u32[]{:S(2)}, u32[]{:S(2)}) collective-permute-start(bf16[64,1024]{1,0:T(8,128)(2,1)} %slice.60), channel_id=1, source_target_pairs={{0,16},{1,3},{2,18},{3,1},{4,20},{5,7},{6,22},{7,5},{8,24},{9,11},... | collective-permute-start | bytes 393224 | tf_op jit(solution)/shard_map/ppermute | solution.py:24
  (17 other events, 92.8 us)

commit v5 on v4

--- a/solution.py
+++ b/solution.py
@@ -255,6 +255,25 @@
             start += rows
 
 
+def add_body(meta, kept, received, keep, send):
+    rows = keep.shape[0]
+    total = kept[...].astype(F32) + received[...].astype(F32)
+    keep[...] = total[:rows].astype(keep.dtype)
+    send[...] = total[rows:].astype(send.dtype)
+
+
+def last_add_body(meta, kept, received, keep, send):
+    for out, mine in ((keep, True), (send, False)):
+        rows = half_of(meta, keep.shape[0], mine)
+        out[...] = (kept[rows, :].astype(F32) + received[rows, :].astype(F32)).astype(out.dtype)
+
+
+def scale_body(factor, meta, keep, received, out):
+    width = keep.shape[1]
+    out[:, half_of(meta, width, True)] = keep[...] * factor
+    out[:, half_of(meta, width, False)] = received[...].astype(F32) * factor
+
+
 def cascade_body(counts, meta, *refs):
     keep, send = refs[-2:]
     half = keep.shape[1]
@@ -471,20 +490,14 @@
         scratch,
     )
     first_back, *others = lax.optimization_barrier(
-        (first_back, *back, *wg_received, base_k, base_v, at_keep)
+        (first_back, *back, *wg_received, base_k, base_v, at_keep, dq_recv)
     )
     back, wg_received = others[: len(back)], others[len(back) : len(back) + 2]
     wg_total = jnp.concatenate([add(*both) for both in zip(wg_keep, wg_received, strict=True)], axis=1)
     wg_rows = wg_total.shape[0] // 2
     wg_keep, wg_send = wg_total[:wg_rows], wg_total[wg_rows:]
     wg_received = permute(wg_send, sum_stages[0][-3])
-    grad_queries, attended = call(
-        place_body,
-        meta,
-        (dq_keep, dq_recv, at_keep, swap(after(at_send, wg_total), 1)),
-        [struct(length, inner, BF16), struct(length, 2 * cols, BF16)],
-        last=True,
-    )
+    at_recv = swap(after(at_send, wg_total), 1)
     cuts = [coarse[h].shape[1] for h, _ in far_masks]
     high_shapes = [planes(rows, half, BF16) for rows in cuts]
     high_sums = call(
@@ -496,7 +509,8 @@
     by_level = {1: [first_back], 2: back[1:]}
     high_back = [swap(part, mask) for (_, mask), part in zip(far_masks, high_sums, strict=True)]
     *high_back, wg_received = lax.optimization_barrier((*high_back, wg_received))
-    wg_keep, wg_send = add_halves(wg_keep, wg_received)
+    half_rows = struct(piece, cols, BF16)
+    wg_keep, wg_send = call(add_body, meta, (wg_keep, wg_received), [half_rows, half_rows])
     wg_received = permute(wg_send, sum_stages[0][-4])
     for (h, _), part in zip(far_masks, high_back, strict=True):
         by_level.setdefault(h, []).append(part)
@@ -510,22 +524,27 @@
         received,
         [planes(up_rows, half, F32), planes(up_rows, half, BF16)],
     )
+    grad_queries, attended = call(
+        place_body,
+        after(meta, up_keep),
+        (dq_keep, dq_recv, at_keep, at_recv),
+        [struct(length, inner, BF16), struct(length, 2 * cols, BF16)],
+        last=True,
+    )
     wg_received = after(wg_received, up_keep, attended)
-    total = wg_keep.astype(F32) + wg_received.astype(F32)
-    rows = piece // 2
-    wg_mine = lax.dynamic_slice_in_dim(total, bit * rows, rows, 0)
-    wg_theirs = swap(lax.dynamic_slice_in_dim(total, (1 - bit) * rows, rows, 0).astype(BF16), 1)
-    wg_theirs = wg_theirs.astype(F32)
-    weight_grad = jnp.where(
-        bit == 0,
-        jnp.concatenate([wg_mine, wg_theirs], axis=1),
-        jnp.concatenate([wg_theirs, wg_mine], axis=1),
+    last = (struct(piece // 2, cols, F32), struct(piece // 2, cols, BF16))
+    wg_keep, wg_send = call(last_add_body, meta, (wg_keep, wg_received), last)
+    (weight_grad,) = call(
+        lambda *refs: scale_body(1.0 / math.sqrt(token_total), *refs),
+        meta,
+        (wg_keep, swap(wg_send, 1)),
+        [struct(piece // 2, 2 * cols, F32)],
+        last=True,
     )
     if dp_count > 1:
         weight_grad = lax.psum_scatter(
             weight_grad.astype(BF16), "dp", scatter_dimension=1, tiled=True
         ).astype(F32)
-    weight_grad = weight_grad * (1.0 / math.sqrt(token_total))
     grad_keys, grad_values = call(
         finish_body,
         meta,

time: 108 us -> 106 us (0.981)
  waiting for transfers between devices: 32 us -> 35.1 us
  local copies, waits for them, and re-layouts: 6.35 us -> 4.02 us
  other arithmetic: 2.59 us -> 0.83 us
  starting transfers between devices: 39.2 us -> 37.5 us
    ppermute x37, waiting for transfers between devices: 32 us -> 35.1 us  [permute(): lax.ppermute(value, 'seq', [(i, i ^ masks[i & 1]) for i in range(count)])]
    ppermute x37, starting transfers between devices: 39.2 us -> 37.5 us  [permute(): lax.ppermute(value, 'seq', [(i, i ^ masks[i & 1]) for i in range(count)])]
    unnamed x11 -> x5, local copies, waits for them, and re-layouts: 1.68 us -> 0.03 us
    pallas_call x11 -> x14, Pallas kernels: 26.4 us -> 27.4 us  [call(): pl.pallas_call(body, grid=(1,) if last else (), in_specs=[pl.BlockSpec(me...]
  transfers between devices with their start and end apart: 37 -> 37, of which waited for: 13 -> 15; matrix products, arithmetic and copies ran while one was open for 5% -> 3% of each run, Pallas kernels for 23% -> 23%
where the time goes in v5:
time: 106 us
  starting transfers between devices  37.5 us (35%)
  waiting for transfers between devices  35.1 us (33%)
  Pallas kernels  27.4 us (26%)
  local copies, waits for them, and re-layouts  4.02 us (4%)
    ppermute x37, starting transfers between devices, permute(): lax.ppermute(value, 'seq', [(i, i ^ masks[i & 1]) for i in range(count)])  37.5 us
    ppermute x37, waiting for transfers between devices, permute(): lax.ppermute(value, 'seq', [(i, i ^ masks[i & 1]) for i in range(count)])  35.1 us
    pallas_call x14, Pallas kernels, call(): pl.pallas_call(body, grid=(1,) if last else (), in_specs=[pl.BlockSpec(me...  27.4 us
    dynamic_slice x4, local copies, waits for them, and re-layouts, part(): return lax.dynamic_slice_in_dim(array, which * width, width, 1)  3.92 us
  transfers between devices with their start and end apart: 37, of which 15 were waited for; matrix products, arithmetic and copies ran while one was open for 3% of the time, Pallas kernels for 23%

profile of v5, /device:TPU:0, one launch (start us, length us, event | category | flops | bytes accessed | tf_op | source)
XLA Modules:
  0.0 105.8 jit_solution(15173593075389254281)
XLA Ops:
  5.7 2.8 %collective-permute-start.3 = (bf16[2,128,512]{2,1,0:T(8,128)(2,1)S(1)}, bf16[2,128,512]{2,1,0:T(8,128)(2,1)S(1)}, u32[]{:S(2)}, u32[]{:S(2)}) collective-permute-start(bf16[2,128,512]{2,1,0:T(8,128)(2,1)S(1)} %get-tuple-element.76), channel_id=1, source_target_pairs={{0,2},{1,3},{2,0},{3,1},{4,6},{5,7},{6,4},{7,5},{8,10},{9,11},{10,... | collective-permute-start | bytes 786440 | tf_op jit(solution)/shard_map/ppermute | solution.py:24
  8.6 2.7 %collective-permute-start.1 = (bf16[64,1024]{1,0:T(8,128)(2,1)S(1)}, bf16[64,1024]{1,0:T(8,128)(2,1)S(1)}, u32[]{:S(2)}, u32[]{:S(2)}) collective-permute-start(bf16[64,1024]{1,0:T(8,128)(2,1)S(1)} %maximum_select_fusion), channel_id=1, source_target_pairs={{0,16},{1,3},{2,18},{3,1},{4,20},{5,7},{6,22},{7,5},{8,24},{9,11},... | collective-permute-start | bytes 393224 | tf_op jit(solution)/shard_map/ppermute | solution.py:24
  12.6 1.7 %collective-permute-start.5 = (bf16[2,16,512]{2,1,0:T(8,128)(2,1)S(1)}, bf16[2,16,512]{2,1,0:T(8,128)(2,1)S(1)}, u32[]{:S(2)}, u32[]{:S(2)}) collective-permute-start(bf16[2,16,512]{2,1,0:T(8,128)(2,1)S(1)} %get-tuple-element.78), channel_id=1, source_target_pairs={{0,16},{1,17},{2,18},{3,19},{4,20},{5,21},{6,22},{7,23},{8,24},{9,... | collective-permute-start | bytes 98312 | tf_op jit(solution)/shard_map/ppermute | solution.py:24
  15.6 1.8 %collective-permute-done.1 = bf16[64,1024]{1,0:T(8,128)(2,1)S(1)} collective-permute-done((bf16[64,1024]{1,0:T(8,128)(2,1)S(1)}, bf16[64,1024]{1,0:T(8,128)(2,1)S(1)}, u32[]{:S(2)}, u32[]{:S(2)}) %collective-permute-start.1) | collective-permute-done | bytes 131104 | tf_op jit(solution)/shard_map/ppermute | solution.py:24
  18.9 1.7 %collective-permute-start.11 = (bf16[2,128,512]{2,1,0:T(8,128)(2,1)S(1)}, bf16[2,128,512]{2,1,0:T(8,128)(2,1)S(1)}, u32[]{:S(2)}, u32[]{:S(2)}) collective-permute-start(bf16[2,128,512]{2,1,0:T(8,128)(2,1)S(1)} %get-tuple-element.165), channel_id=1, source_target_pairs={{0,6},{1,7},{2,4},{3,5},{4,2},{5,3},{6,0},{7,1},{8,14},{9,15},{10,... | collective-permute-start | bytes 786440 | tf_op jit(solution)/shard_map/ppermute | solution.py:24
  24.9 4.4 %collective-permute-done.8.refs_9_ = bf16[2,64,512]{2,1,0:T(8,128)(2,1)S(1)} collective-permute-done((bf16[2,64,512]{2,1,0:T(8,128)(2,1)S(1)}, bf16[2,64,512]{2,1,0:T(8,128)(2,1)S(1)}, u32[]{:S(2)}, u32[]{:S(2)}) %collective-permute-start.8) | collective-permute-done | bytes 131104 | tf_op jit(solution)/shard_map/ppermute | solution.py:24
  31.4 1.9 %collective-permute-start.15 = (bf16[256,512]{1,0:T(8,128)(2,1)S(1)}, bf16[256,512]{1,0:T(8,128)(2,1)S(1)}, u32[]{:S(2)}, u32[]{:S(2)}) collective-permute-start(bf16[256,512]{1,0:T(8,128)(2,1)S(1)} %pad_maximum_fusion.7), channel_id=1, source_target_pairs={{0,4},{1,9},{2,6},{3,11},{4,0},{5,13},{6,2},{7,15},{8,12},{9,1},{1... | collective-permute-start | bytes 786440 | tf_op jit(solution)/shard_map/ppermute | solution.py:24
  33.3 4.2 %shard_map.93 = (bf16[512,512]{1,0:T(8,128)(2,1)S(1)}, bf16[8,896,256]{2,1,0:T(8,128)(2,1)S(1)}) custom-call(s32[2]{0:T(128)S(1)} %pad_add_fusion.meta.refs_0_, bf16[256,512]{1,0:T(8,128)(2,1)S(1)} %get-tuple-element.152.refs_1_, bf16[256,512]{1,0:T(8,128)(2,1)S(1)} %collective-permute-done.9.refs_2_, ...), custom_call_target="tpu_custom_call" | custom-call | flops 7516192768 | tf_op jit(solution)/shard_map/pallas_call | solution.py:41
  41.1 2.0 %shard_map.94 = (bf16[512,512]{1,0:T(8,128)(2,1)S(1)}, bf16[512,512]{1,0:T(8,128)(2,1)S(1)}, bf16[512,512]{1,0:T(8,128)(2,1)S(1)}, bf16[512,512]{1,0:T(8,128)(2,1)S(1)}) custom-call(s32[2]{0:T(128)S(1)} %pad_add_fusion.meta.refs_0_, bf16[512,512]{1,0:T(8,128)(2,1)S(1)} %get-tuple-element.90.refs_1_, bf16[512,512]{1,0:T(8,128)(2,1)S(1)} %collective-permute-done.12.refs_2_, ...), custom_call_target="tpu_custom_call" | custom-call | tf_op jit(solution)/shard_map/pallas_call | solution.py:41
  43.1 4.3 %collective-permute-done.17.refs_6_ = bf16[512,512]{1,0:T(8,128)(2,1)S(1)} collective-permute-done((bf16[512,512]{1,0:T(8,128)(2,1)S(1)}, bf16[512,512]{1,0:T(8,128)(2,1)S(1)}, u32[]{:S(2)}, u32[]{:S(2)}) %collective-permute-start.17) | collective-permute-done | bytes 524320 | tf_op jit(solution)/shard_map/ppermute | solution.py:24
  47.4 4.7 %collective-permute-done.16.refs_4_ = bf16[512,512]{1,0:T(8,128)(2,1)S(1)} collective-permute-done((bf16[512,512]{1,0:T(8,128)(2,1)S(1)}, bf16[512,512]{1,0:T(8,128)(2,1)S(1)}, u32[]{:S(2)}, u32[]{:S(2)}) %collective-permute-start.16) | collective-permute-done | bytes 524320 | tf_op jit(solution)/shard_map/ppermute | solution.py:24
  52.1 2.0 %shard_map.95 = (f32[512,512]{1,0:T(8,128)S(1)}, bf16[512,512]{1,0:T(8,128)(2,1)S(1)}) custom-call(s32[2]{0:T(128)S(1)} %pad_add_fusion.meta.refs_0_, bf16[256,1024]{1,0:T(8,128)(2,1)S(1)} %get-tuple-element.148.refs_3_.refs_1_, bf16[256,1024]{1,0:T(8,128)(2,1)S(1)} %collective-permute-done.13.refs_4_.refs_2_, ...), custom_call_target="tpu_custom_call" | custom-call | tf_op jit(solution)/shard_map/pallas_call | solution.py:41
  56.1 6.9 %shard_map.96 = (bf16[256,512]{1,0:T(8,128)(2,1)S(1)}, bf16[256,512]{1,0:T(8,128)(2,1)S(1)}, f32[2,384,512]{2,1,0:T(8,128)S(1)}, bf16[2,384,512]{2,1,0:T(8,128)(...) custom-call(s32[2]{0:T(128)S(1)} %pad_add_fusion.meta.refs_0_, ...), custom_call_target="tpu_custom_call" | custom-call | tf_op jit(solution)/shard_map/pallas_call | solution.py:41
  65.7 2.9 %collective-permute-done.19 = bf16[512,512]{1,0:T(8,128)(2,1)S(1)} collective-permute-done((bf16[512,512]{1,0:T(8,128)(2,1)S(1)}, bf16[512,512]{1,0:T(8,128)(2,1)S(1)}, u32[]{:S(2)}, u32[]{:S(2)}) %collective-permute-start.19) | collective-permute-done | bytes 524320 | tf_op jit(solution)/shard_map/ppermute | solution.py:24
  68.5 2.1 %collective-permute-start.24 = (bf16[2,128,512]{2,1,0:T(8,128)(2,1)S(1)}, bf16[2,128,512]{2,1,0:T(8,128)(2,1)S(1)}, u32[]{:S(2)}, u32[]{:S(2)}) collective-permute-start(bf16[2,128,512]{2,1,0:T(8,128)(2,1)S(1)} %get-tuple-element.107), channel_id=1, source_target_pairs={{0,6},{1,7},{2,4},{3,5},{4,2},{5,3},{6,0},{7,1},{8,14},{9,15},{10,... | collective-permute-start | bytes 786440 | tf_op jit(solution)/shard_map/ppermute | solution.py:24
  71.0 4.1 %collective-permute-done.22.refs_6_ = bf16[2,128,512]{2,1,0:T(8,128)(2,1)S(1)} collective-permute-done((bf16[2,128,512]{2,1,0:T(8,128)(2,1)S(1)}, bf16[2,128,512]{2,1,0:T(8,128)(2,1)S(1)}, u32[]{:S(2)}, u32[]{:S(2)}) %collective-permute-start.22) | collective-permute-done | bytes 262176 | tf_op jit(solution)/shard_map/ppermute | solution.py:24
  77.3 2.0 %shard_map.98 = (bf16[256,1024]{1,0:T(8,128)(2,1)S(1)}, bf16[256,1024]{1,0:T(8,128)(2,1)S(1)}) custom-call(s32[2]{0:T(128)S(1)} %pad_add_fusion.meta.refs_0_, bf16[512,512]{1,0:T(8,128)(2,1)S(1)} %get-tuple-element.90.refs_1_, bf16[512,512]{1,0:T(8,128)(2,1)S(1)} %collective-permute-done.12.refs_2_, bf16[512,512]{1,0:T(8,128)(2,1)S(1)} %pad_maximum_fusion.3.refs_3_, ...), custom_call_target="tpu_custom_call" | custom-call | tf_op jit(solution)/shard_map/pallas_call | solution.py:41
  80.5 2.0 %collective-permute-done.25 = bf16[256,512]{1,0:T(8,128)(2,1)S(1)} collective-permute-done((bf16[256,512]{1,0:T(8,128)(2,1)S(1)}, bf16[256,512]{1,0:T(8,128)(2,1)S(1)}, u32[]{:S(2)}, u32[]{:S(2)}) %collective-permute-start.25) | collective-permute-done | bytes 262176 | tf_op jit(solution)/shard_map/ppermute | solution.py:24
  86.0 2.7 %collective-permute-start.30 = (bf16[2,16,512]{2,1,0:T(8,128)(2,1)S(1)}, bf16[2,16,512]{2,1,0:T(8,128)(2,1)S(1)}, u32[]{:S(2)}, u32[]{:S(2)}) collective-permute-start(bf16[2,16,512]{2,1,0:T(8,128)(2,1)S(1)} %get-tuple-element.124), channel_id=1, source_target_pairs={{0,16},{1,17},{2,18},{3,19},{4,20},{5,21},{6,22},{7,23},{8,24},{9,... | collective-permute-start | bytes 98312 | tf_op jit(solution)/shard_map/ppermute | solution.py:24
  89.4 2.0 %collective-permute-done.30.refs_1_ = bf16[2,16,512]{2,1,0:T(8,128)(2,1)S(1)} collective-permute-done((bf16[2,16,512]{2,1,0:T(8,128)(2,1)S(1)}, bf16[2,16,512]{2,1,0:T(8,128)(2,1)S(1)}, u32[]{:S(2)}, u32[]{:S(2)}) %collective-permute-start.30) | collective-permute-done | bytes 32800 | tf_op jit(solution)/shard_map/ppermute | solution.py:24
  91.5 3.1 %collective-permute-done.31.refs_2_ = bf16[2,16,512]{2,1,0:T(8,128)(2,1)S(1)} collective-permute-done((bf16[2,16,512]{2,1,0:T(8,128)(2,1)S(1)}, bf16[2,16,512]{2,1,0:T(8,128)(2,1)S(1)}, u32[]{:S(2)}, u32[]{:S(2)}) %collective-permute-start.31) | collective-permute-done | bytes 32800 | tf_op jit(solution)/shard_map/ppermute | solution.py:24
  95.2 2.2 %collective-permute-start.35 = (bf16[64,1024]{1,0:T(8,128)(2,1)S(1)}, bf16[64,1024]{1,0:T(8,128)(2,1)S(1)}, u32[]{:S(2)}, u32[]{:S(2)}) collective-permute-start(bf16[64,1024]{1,0:T(8,128)(2,1)S(1)} %get-tuple-element.127), channel_id=1, source_target_pairs={{0,16},{1,3},{2,18},{3,1},{4,20},{5,7},{6,22},{7,5},{8,24},{9,11},... | collective-permute-start | bytes 393224 | tf_op jit(solution)/shard_map/ppermute | solution.py:24
  98.6 1.8 %shard_map.102 = (bf16[256,1024]{1,0:T(8,128)(2,1)}, bf16[256,2048]{1,0:T(8,128)(2,1)}) custom-call(s32[2]{0:T(128)S(1)} %pad_add_fusion.meta.refs_0_, bf16[256,512]{1,0:T(8,128)(2,1)S(1)} %get-tuple-element.135.refs_0_, bf16[256,512]{1,0:T(8,128)(2,1)S(1)} %collective-permute-done.28.refs_1_, bf16[256,1024]{1,0:T(8,128)(2,1)S(1)} %get-tuple-element.115.refs_2_, ...), custom_call_target="tpu_custom_call" | custom-call | tf_op jit(solution)/shard_map/pallas_call | solution.py:41
  102.7 1.9 %shard_map.103 = (bf16[256,1024]{1,0:T(8,128)(2,1)}, bf16[256,1024]{1,0:T(8,128)(2,1)}) custom-call(s32[2]{0:T(128)S(1)} %pad_add_fusion.meta.refs_0_, f32[256,1024]{1,0:T(8,128)S(1)} %get-tuple-element.112.base_k, f32[256,1024]{1,0:T(8,128)S(1)} %get-tuple-element.113.base_v, f32[2,64,512]{2,1,0:T(8,128)S(1)} %get-tuple-element.133.up_keep, ...), custom_call_target="tpu_custom_call" | custom-call | tf_op jit(solution)/shard_map/pallas_call | solution.py:41
  (92 shorter events, 36.9 us)
Async XLA Ops:
  5.7 13.2 %collective-permute-start.3 = (bf16[2,128,512]{2,1,0:T(8,128)(2,1)S(1)}, bf16[2,128,512]{2,1,0:T(8,128)(2,1)S(1)}, u32[]{:S(2)}, u32[]{:S(2)}) collective-permute-start(bf16[2,128,512]{2,1,0:T(8,128)(2,1)S(1)} %get-tuple-element.76), channel_id=1, source_target_pairs={{0,2},{1,3},{2,0},{3,1},{4,6},{5,7},{6,4},{7,5},{8,10},{9,11},{10,... | collective-permute-start | bytes 786440 | tf_op jit(solution)/shard_map/ppermute | solution.py:24
  8.6 8.9 %collective-permute-start.1 = (bf16[64,1024]{1,0:T(8,128)(2,1)S(1)}, bf16[64,1024]{1,0:T(8,128)(2,1)S(1)}, u32[]{:S(2)}, u32[]{:S(2)}) collective-permute-start(bf16[64,1024]{1,0:T(8,128)(2,1)S(1)} %maximum_select_fusion), channel_id=1, source_target_pairs={{0,16},{1,3},{2,18},{3,1},{4,20},{5,7},{6,22},{7,5},{8,24},{9,11},... | collective-permute-start | bytes 393224 | tf_op jit(solution)/shard_map/ppermute | solution.py:24
  18.9 12.5 %collective-permute-start.11 = (bf16[2,128,512]{2,1,0:T(8,128)(2,1)S(1)}, bf16[2,128,512]{2,1,0:T(8,128)(2,1)S(1)}, u32[]{:S(2)}, u32[]{:S(2)}) collective-permute-start(bf16[2,128,512]{2,1,0:T(8,128)(2,1)S(1)} %get-tuple-element.165), channel_id=1, source_target_pairs={{0,6},{1,7},{2,4},{3,5},{4,2},{5,3},{6,0},{7,1},{8,14},{9,15},{10,... | collective-permute-start | bytes 786440 | tf_op jit(solution)/shard_map/ppermute | solution.py:24
  20.7 12.6 %collective-permute-start.10 = (bf16[2,128,512]{2,1,0:T(8,128)(2,1)S(1)}, bf16[2,128,512]{2,1,0:T(8,128)(2,1)S(1)}, u32[]{:S(2)}, u32[]{:S(2)}) collective-permute-start(bf16[2,128,512]{2,1,0:T(8,128)(2,1)S(1)} %get-tuple-element.165), channel_id=1, source_target_pairs={{0,4},{1,5},{2,6},{3,7},{4,0},{5,1},{6,2},{7,3},{8,12},{9,13},{10,... | collective-permute-start | bytes 786440 | tf_op jit(solution)/shard_map/ppermute | solution.py:24
  21.1 8.2 %collective-permute-start.8 = (bf16[2,64,512]{2,1,0:T(8,128)(2,1)S(1)}, bf16[2,64,512]{2,1,0:T(8,128)(2,1)S(1)}, u32[]{:S(2)}, u32[]{:S(2)}) collective-permute-start(bf16[2,64,512]{2,1,0:T(8,128)(2,1)S(1)} %get-tuple-element.166.refs_7_), channel_id=1, source_target_pairs={{0,2},{1,3},{2,0},{3,1},{4,6},{5,7},{6,4},{7,5},{8,10},{9,11},{10,... | collective-permute-start | bytes 393224 | tf_op jit(solution)/shard_map/ppermute | solution.py:24
  22.5 8.3 %collective-permute-start.7 = (bf16[128,1024]{1,0:T(8,128)(2,1)S(1)}, bf16[128,1024]{1,0:T(8,128)(2,1)S(1)}, u32[]{:S(2)}, u32[]{:S(2)}) collective-permute-start(bf16[128,1024]{1,0:T(8,128)(2,1)S(1)} %pad_maximum_fusion.5), channel_id=1, source_target_pairs={{0,8},{1,17},{2,10},{3,19},{4,12},{5,21},{6,14},{7,23},{8,0},{9,25... | collective-permute-start | bytes 786440 | tf_op jit(solution)/shard_map/ppermute | solution.py:24
  24.7 8.7 %collective-permute-start.9 = (bf16[256,512]{1,0:T(8,128)(2,1)S(1)}, bf16[256,512]{1,0:T(8,128)(2,1)S(1)}, u32[]{:S(2)}, u32[]{:S(2)}) collective-permute-start(bf16[256,512]{1,0:T(8,128)(2,1)S(1)} %get-tuple-element.151), channel_id=1, source_target_pairs={{0,1},{1,0},{2,3},{3,2},{4,5},{5,4},{6,7},{7,6},{8,9},{9,8},{10,11... | collective-permute-start | bytes 786440 | tf_op jit(solution)/shard_map/ppermute | solution.py:24
  29.3 11.9 %collective-permute-start.13 = (bf16[256,1024]{1,0:T(8,128)(2,1)S(1)}, bf16[256,1024]{1,0:T(8,128)(2,1)S(1)}, u32[]{:S(2)}, u32[]{:S(2)}) collective-permute-start(bf16[256,1024]{1,0:T(8,128)(2,1)S(1)} %get-tuple-element.147), channel_id=1, source_target_pairs={{0,1},{1,0},{2,3},{3,2},{4,5},{5,4},{6,7},{7,6},{8,9},{9,8},{10,11... | collective-permute-start | bytes 1572872 | tf_op jit(solution)/shard_map/ppermute | solution.py:24
  30.9 6.8 %collective-permute-start.14 = (bf16[256,512]{1,0:T(8,128)(2,1)S(1)}, bf16[256,512]{1,0:T(8,128)(2,1)S(1)}, u32[]{:S(2)}, u32[]{:S(2)}) collective-permute-start(bf16[256,512]{1,0:T(8,128)(2,1)S(1)} %pad_maximum_fusion.6), channel_id=1, source_target_pairs={{0,2},{1,5},{2,0},{3,7},{4,6},{5,1},{6,4},{7,3},{8,10},{9,13},{10,... | collective-permute-start | bytes 786440 | tf_op jit(solution)/shard_map/ppermute | solution.py:24
  38.2 9.2 %collective-permute-start.17 = (bf16[512,512]{1,0:T(8,128)(2,1)S(1)}, bf16[512,512]{1,0:T(8,128)(2,1)S(1)}, u32[]{:S(2)}, u32[]{:S(2)}) collective-permute-start(bf16[512,512]{1,0:T(8,128)(2,1)S(1)} %pad_maximum_fusion.4.refs_5_), channel_id=1, source_target_pairs={{0,2},{1,5},{2,0},{3,7},{4,6},{5,1},{6,4},{7,3},{8,10},{9,13},{10,... | collective-permute-start | bytes 1572872 | tf_op jit(solution)/shard_map/ppermute | solution.py:24
  39.8 12.4 %collective-permute-start.16 = (bf16[512,512]{1,0:T(8,128)(2,1)S(1)}, bf16[512,512]{1,0:T(8,128)(2,1)S(1)}, u32[]{:S(2)}, u32[]{:S(2)}) collective-permute-start(bf16[512,512]{1,0:T(8,128)(2,1)S(1)} %pad_maximum_fusion.3.refs_3_), channel_id=1, source_target_pairs={{0,4},{1,9},{2,6},{3,11},{4,0},{5,13},{6,2},{7,15},{8,12},{9,1},{1... | collective-permute-start | bytes 1572872 | tf_op jit(solution)/shard_map/ppermute | solution.py:24
  54.2 11.0 %collective-permute-start.18 = (bf16[512,512]{1,0:T(8,128)(2,1)S(1)}, bf16[512,512]{1,0:T(8,128)(2,1)S(1)}, u32[]{:S(2)}, u32[]{:S(2)}) collective-permute-start(bf16[512,512]{1,0:T(8,128)(2,1)S(1)} %get-tuple-element.97), channel_id=1, source_target_pairs={{0,2},{1,5},{2,0},{3,7},{4,6},{5,1},{6,4},{7,3},{8,10},{9,13},{10,... | collective-permute-start | bytes 1572872 | tf_op jit(solution)/shard_map/ppermute | solution.py:24
  55.6 13.0 %collective-permute-start.19 = (bf16[512,512]{1,0:T(8,128)(2,1)S(1)}, bf16[512,512]{1,0:T(8,128)(2,1)S(1)}, u32[]{:S(2)}, u32[]{:S(2)}) collective-permute-start(bf16[512,512]{1,0:T(8,128)(2,1)S(1)} %get-tuple-element.98), channel_id=1, source_target_pairs={{0,8},{1,9},{2,10},{3,11},{4,12},{5,13},{6,14},{7,15},{8,0},{9,1},... | collective-permute-start | bytes 1572872 | tf_op jit(solution)/shard_map/ppermute | solution.py:24
  63.0 13.5 %collective-permute-start.27 = (bf16[2,384,512]{2,1,0:T(8,128)(2,1)S(1)}, bf16[2,384,512]{2,1,0:T(8,128)(2,1)S(1)}, u32[]{:S(2)}, u32[]{:S(2)}) collective-permute-start(bf16[2,384,512]{2,1,0:T(8,128)(2,1)S(1)} %get-tuple-element.111), channel_id=1, source_target_pairs={{0,1},{1,0},{2,3},{3,2},{4,5},{5,4},{6,7},{7,6},{8,9},{9,8},{10,11... | collective-permute-start | bytes 2359304 | tf_op jit(solution)/shard_map/ppermute | solution.py:24
  63.2 7.5 %collective-permute-start.21 = (bf16[2,64,512]{2,1,0:T(8,128)(2,1)S(1)}, bf16[2,64,512]{2,1,0:T(8,128)(2,1)S(1)}, u32[]{:S(2)}, u32[]{:S(2)}) collective-permute-start(bf16[2,64,512]{2,1,0:T(8,128)(2,1)S(1)} %get-tuple-element.103), channel_id=1, source_target_pairs={{0,2},{1,3},{2,0},{3,1},{4,6},{5,7},{6,4},{7,5},{8,10},{9,11},{10,... | collective-permute-start | bytes 393224 | tf_op jit(solution)/shard_map/ppermute | solution.py:24
  64.5 10.6 %collective-permute-start.22 = (bf16[2,128,512]{2,1,0:T(8,128)(2,1)S(1)}, bf16[2,128,512]{2,1,0:T(8,128)(2,1)S(1)}, u32[]{:S(2)}, u32[]{:S(2)}) collective-permute-start(bf16[2,128,512]{2,1,0:T(8,128)(2,1)S(1)} %get-tuple-element.105), channel_id=1, source_target_pairs={{0,2},{1,3},{2,0},{3,1},{4,6},{5,7},{6,4},{7,5},{8,10},{9,11},{10,... | collective-permute-start | bytes 786440 | tf_op jit(solution)/shard_map/ppermute | solution.py:24
  65.2 15.1 %collective-permute-start.23 = (bf16[2,128,512]{2,1,0:T(8,128)(2,1)S(1)}, bf16[2,128,512]{2,1,0:T(8,128)(2,1)S(1)}, u32[]{:S(2)}, u32[]{:S(2)}) collective-permute-start(bf16[2,128,512]{2,1,0:T(8,128)(2,1)S(1)} %get-tuple-element.106), channel_id=1, source_target_pairs={{0,4},{1,5},{2,6},{3,7},{4,0},{5,1},{6,2},{7,3},{8,12},{9,13},{10,... | collective-permute-start | bytes 786440 | tf_op jit(solution)/shard_map/ppermute | solution.py:24
  68.5 11.9 %collective-permute-start.24 = (bf16[2,128,512]{2,1,0:T(8,128)(2,1)S(1)}, bf16[2,128,512]{2,1,0:T(8,128)(2,1)S(1)}, u32[]{:S(2)}, u32[]{:S(2)}) collective-permute-start(bf16[2,128,512]{2,1,0:T(8,128)(2,1)S(1)} %get-tuple-element.107), channel_id=1, source_target_pairs={{0,6},{1,7},{2,4},{3,5},{4,2},{5,3},{6,0},{7,1},{8,14},{9,15},{10,... | collective-permute-start | bytes 786440 | tf_op jit(solution)/shard_map/ppermute | solution.py:24
  70.6 9.8 %collective-permute-start.28 = (bf16[256,512]{1,0:T(8,128)(2,1)S(1)}, bf16[256,512]{1,0:T(8,128)(2,1)S(1)}, u32[]{:S(2)}, u32[]{:S(2)}) collective-permute-start(bf16[256,512]{1,0:T(8,128)(2,1)S(1)} %get-tuple-element.116), channel_id=1, source_target_pairs={{0,1},{1,0},{2,3},{3,2},{4,5},{5,4},{6,7},{7,6},{8,9},{9,8},{10,11... | collective-permute-start | bytes 786440 | tf_op jit(solution)/shard_map/ppermute | solution.py:24
  75.1 7.4 %collective-permute-start.25 = (bf16[256,512]{1,0:T(8,128)(2,1)S(1)}, bf16[256,512]{1,0:T(8,128)(2,1)S(1)}, u32[]{:S(2)}, u32[]{:S(2)}) collective-permute-start(bf16[256,512]{1,0:T(8,128)(2,1)S(1)} %slice.45), channel_id=1, source_target_pairs={{0,8},{1,9},{2,10},{3,11},{4,12},{5,13},{6,14},{7,15},{8,0},{9,1},... | collective-permute-start | bytes 786440 | tf_op jit(solution)/shard_map/ppermute | solution.py:24
  80.4 18.3 %collective-permute-start.33 = (bf16[256,1024]{1,0:T(8,128)(2,1)S(1)}, bf16[256,1024]{1,0:T(8,128)(2,1)S(1)}, u32[]{:S(2)}, u32[]{:S(2)}) collective-permute-start(bf16[256,1024]{1,0:T(8,128)(2,1)S(1)} %get-tuple-element.137), channel_id=1, source_target_pairs={{0,1},{1,0},{2,3},{3,2},{4,5},{5,4},{6,7},{7,6},{8,9},{9,8},{10,11... | collective-permute-start | bytes 1572872 | tf_op jit(solution)/shard_map/ppermute | solution.py:24
  83.3 11.3 %collective-permute-start.32 = (bf16[128,1024]{1,0:T(8,128)(2,1)S(1)}, bf16[128,1024]{1,0:T(8,128)(2,1)S(1)}, u32[]{:S(2)}, u32[]{:S(2)}) collective-permute-start(bf16[128,1024]{1,0:T(8,128)(2,1)S(1)} %get-tuple-element.149), channel_id=1, source_target_pairs={{0,4},{1,17},{2,6},{3,19},{4,0},{5,21},{6,2},{7,23},{8,12},{9,25},... | collective-permute-start | bytes 786440 | tf_op jit(solution)/shard_map/ppermute | solution.py:24
  84.5 10.1 %collective-permute-start.29 = (bf16[2,32,512]{2,1,0:T(8,128)(2,1)S(1)}, bf16[2,32,512]{2,1,0:T(8,128)(2,1)S(1)}, u32[]{:S(2)}, u32[]{:S(2)}) collective-permute-start(bf16[2,32,512]{2,1,0:T(8,128)(2,1)S(1)} %get-tuple-element.123), channel_id=1, source_target_pairs={{0,8},{1,9},{2,10},{3,11},{4,12},{5,13},{6,14},{7,15},{8,0},{9,1},... | collective-permute-start | bytes 196616 | tf_op jit(solution)/shard_map/ppermute | solution.py:24
  95.2 6.8 %collective-permute-start.35 = (bf16[64,1024]{1,0:T(8,128)(2,1)S(1)}, bf16[64,1024]{1,0:T(8,128)(2,1)S(1)}, u32[]{:S(2)}, u32[]{:S(2)}) collective-permute-start(bf16[64,1024]{1,0:T(8,128)(2,1)S(1)} %get-tuple-element.127), channel_id=1, source_target_pairs={{0,16},{1,3},{2,18},{3,1},{4,20},{5,7},{6,22},{7,5},{8,24},{9,11},... | collective-permute-start | bytes 393224 | tf_op jit(solution)/shard_map/ppermute | solution.py:24
  (14 other events, 82.7 us)
